TPU v7x, 32 devices: a whole 2x2x4 slice. The times are simulated.
32 devices in a mesh: det: 8 (over z, x), row: 4 (over y, core).
Axes of the slice: x: 2, y: 2, z: 4, core: 2. Of those that a mesh axis runs over, the one named last changes fastest.
Arguments:
- images: bfloat16 [48, 3, 384, 384], P('det', None, 'row'), may hold values from -6 to 6
- warp_rows: bfloat16 [48, 3, 384, 384], P('det', None, 'row'), may hold values from -0.3125 to 0.3125
- warp_cols: bfloat16 [48, 3, 384, 384], P('det'), may hold values from -0.3125 to 0.3125
- psf_coef: float32 [48, 3, 21], P('det'), may hold values from -1.25 to 1.25
- taps: float32 [21, 21], replicated, may hold values from -1.25 to 1.25
- dest_patch: int32 [432, 1], replicated, may hold values from 0 to 7; in each aligned block of 54 rows (0 to 53, 54 to 107, ...) at most 14 rows name the same one
- dest_block: int32 [432], replicated, may hold values from 0 to 2
- weight_index: int32 [48, 3], replicated, may hold values from 0 to 7
- weight_table: float32 [8], replicated, may hold values from 0.25 to 4
- patch_home: int32 [8], replicated, may hold values from 0 to 7, each once
Outputs:
- difference: bfloat16 [48, 3, 384, 384], P('det', None, 'row')
- coadd: bfloat16 [8, 384, 384], P('det', 'row')
Inputs may be any that keep to these rules, and one draw needn't show every extreme that they name: `dest_patch`: within the 54 rows of one device (an aligned block of rows), no patch is named more than 14 times. `patch_home`: each position once.
All inputs are finite; a program needn't handle non-finite values.
Results may differ from a plain program's by a relative error of at most 0.0082.
Values may be sent and summed in bfloat16 or wider, within the bound.
No kernel may reach another device: no remote copies, remote signals or barrier semaphores. Data moves between devices by JAX's collectives and lax.ppermute only.
A program may use at most 128 MiB of HBM per device.

v0:
```python
import jax
import jax.numpy as jnp
from jax import lax
from jax.sharding import PartitionSpec as P

TILE = 128


def extended(value, sides, width):
    for axis, dim in sides:
        size, length = (lax.axis_size(axis), value.shape[dim])
        up = [(i, (i + 1) % size) for i in range(size - 1)]
        down = [(j, i) for i, j in up]
        last = lax.slice_in_dim(value, length - width, length, axis=dim)
        first = lax.slice_in_dim(value, 0, width, axis=dim)
        before = lax.ppermute(last, axis, up)
        after = lax.ppermute(first, axis, down)
        value = jnp.concatenate([before, value, after], axis=dim)
    return value


def toeplitz_table(values, out_len, in_len):
    span_len = values.shape[1]
    offsets = jnp.arange(in_len)[None, :] - jnp.arange(out_len)[:, None]
    picks = (offsets[:, :, None] == jnp.arange(span_len)[None, None, :]).astype(jnp.float32)
    return jnp.einsum("oij,kj->koi", picks, values.astype(jnp.float32)).astype(jnp.bfloat16)


def per_device(
    images,
    warp_rows,
    warp_cols,
    psf_coef,
    taps,
    dest_patch,
    dest_block,
    weight_index,
    weight_table,
    patch_home,
):
    det_count, visit_count, band_rows, side_cols = images.shape
    kernel_count, tap_count = taps.shape
    reach = (tap_count - 1) // 2
    tile_cols = TILE
    tile_count = side_cols // tile_cols
    det_devices = lax.axis_size("det")
    my_index = lax.axis_index("det")
    image_count = det_count * visit_count
    piece_count = image_count * tile_count
    capacity = max(2, 2 * ((piece_count + det_devices - 1) // det_devices))
    slot_count = det_devices * capacity
    padded_rows = band_rows + 2 * reach
    col_warped = jnp.einsum(
        "dvbs,dvst->dvbt", images, warp_cols, preferred_element_type=jnp.float32
    ).astype(jnp.bfloat16)
    warped = jnp.einsum(
        "dvbr,dvrs->dvbs",
        warp_rows,
        lax.all_gather(col_warped, "row", axis=2, tiled=True),
        preferred_element_type=jnp.float32,
    ).astype(jnp.bfloat16)
    padded = extended(warped, (("row", 2),), reach)
    taps_half = taps.astype(jnp.bfloat16)
    col_table = toeplitz_table(taps_half, tile_cols, tile_cols + 2 * reach)
    tiles_in = padded.reshape(image_count, padded_rows, side_cols)
    coef_rows = psf_coef.reshape(image_count, kernel_count)

    def match_image(inputs):
        tile_image, coef_row = inputs
        widened = jnp.pad(tile_image, ((0, 0), (reach, reach)))
        windows = jnp.stack(
            [
                widened[
                    :, column_tile * tile_cols : column_tile * tile_cols + tile_cols + 2 * reach
                ]
                for column_tile in range(tile_count)
            ],
            axis=1,
        )
        conv_cols = jnp.einsum(
            "rtw,kcw->krtc", windows, col_table, preferred_element_type=jnp.float32
        ).astype(jnp.bfloat16)
        conv_cols = conv_cols.reshape(kernel_count, padded_rows, side_cols)
        scaled = (coef_row[:, None] * taps).astype(jnp.bfloat16)
        row_table = toeplitz_table(scaled, band_rows, padded_rows)
        return jnp.einsum("kbr,krs->bs", row_table, conv_cols, preferred_element_type=jnp.float32)

    matched = lax.map(match_image, (tiles_in, coef_rows))
    level_count = weight_table.shape[0]
    level_onehot = (weight_index[:, :, None] == jnp.arange(level_count)[None, None, :]).astype(
        jnp.float32
    )
    weight_all = jnp.sum(level_onehot * weight_table[None, None, :], axis=2)
    weight_mine = lax.dynamic_slice_in_dim(weight_all, my_index * det_count, det_count, 0).reshape(
        image_count
    )
    weighted = (
        (weight_mine[:, None, None] * matched)
        .astype(jnp.bfloat16)
        .reshape(image_count, band_rows, tile_count, tile_cols)
    )
    patch_count = patch_home.shape[0]
    patch_ids = dest_patch[:, 0]
    owner_all = jnp.sum(
        jnp.where(patch_ids[:, None] == jnp.arange(patch_count)[None, :], patch_home[None, :], 0),
        axis=1,
    )
    owner_grid = owner_all.reshape(det_devices, piece_count)
    earlier = jnp.arange(piece_count)[None, :] < jnp.arange(piece_count)[:, None]
    rank_grid = jnp.sum(
        ((owner_grid[:, :, None] == owner_grid[:, None, :]) & earlier[None]).astype(jnp.int32),
        axis=2,
    )
    slot_grid = owner_grid * capacity + rank_grid
    slot_mine = lax.dynamic_slice_in_dim(slot_grid, my_index, 1, 0)[0]
    send_pick = (
        (jnp.arange(slot_count)[:, None] == slot_mine[None, :])
        .astype(jnp.bfloat16)
        .reshape(slot_count, image_count, tile_count)
    )
    weight_pieces = jnp.repeat(weight_all.reshape(-1), tile_count)
    to_mine = owner_all == my_index
    block_onehot = (dest_block[:, None] == jnp.arange(tile_count)[None, :]).astype(jnp.float32)
    denominator = jnp.sum(
        jnp.where(to_mine[:, None], block_onehot * weight_pieces[:, None], 0.0), axis=0
    )
    source_slot = jnp.arange(
        det_devices * piece_count
    ) // piece_count * capacity + rank_grid.reshape(-1)
    slot_onehot = (
        (source_slot[:, None] == jnp.arange(slot_count)[None, :]) & to_mine[:, None]
    ).astype(jnp.float32)
    gather_matrix = jnp.einsum("iq,is->qs", block_onehot, slot_onehot).astype(jnp.bfloat16)
    outgoing = jnp.einsum(
        "spq,pbqc->sbc", send_pick, weighted, preferred_element_type=jnp.float32
    ).astype(jnp.bfloat16)
    received = lax.all_to_all(outgoing, "det", split_axis=0, concat_axis=0, tiled=True)
    numerator = jnp.einsum(
        "qs,sbc->bqc", gather_matrix, received, preferred_element_type=jnp.float32
    )
    template = (numerator / jnp.maximum(denominator, 1.0)[None, :, None]).astype(jnp.bfloat16)
    coadd_band = template.reshape(1, band_rows, side_cols)
    returned = jnp.einsum(
        "qs,bqc->sbc", gather_matrix, template, preferred_element_type=jnp.float32
    ).astype(jnp.bfloat16)
    arrived = lax.all_to_all(returned, "det", split_axis=0, concat_axis=0, tiled=True)
    local_template = jnp.einsum(
        "spq,sbc->pbqc", send_pick, arrived, preferred_element_type=jnp.float32
    )
    difference = (
        matched.reshape(image_count, band_rows, tile_count, tile_cols) - local_template
    ).astype(jnp.bfloat16)
    difference = difference.reshape(det_count, visit_count, band_rows, side_cols)
    return (difference, coadd_band)


def solution(mesh):
    placed = (
        P("det", None, "row", None),
        P("det", None, "row", None),
        P("det", None, None, None),
        P("det", None, None),
        P(),
        P(),
        P(),
        P(),
        P(),
        P(),
    )
    return jax.shard_map(
        per_device,
        mesh=mesh,
        in_specs=placed,
        out_specs=(P("det", None, "row", None), P("det", "row", None)),
        check_vma=False,
    )
```

profile of v0, /device:TPU:0, one launch (start us, length us, event | category | flops | bytes accessed | tf_op | source)
XLA Modules:
  0.0 401.3 jit_solution(2774191905715374119)
XLA Ops:
  8.5 4.7 %convolution_convert_fusion.3 = bf16[6,3,96,384]{3,2,1,0:T(8,128)(2,1)} fusion(bf16[6,3,96,384]{3,2,1,0:T(8,128)(2,1)S(1)} %copy-done, bf16[6,3,384,384]{3,2,1,0:T(8,128)(2,1)} %param.14), kind=kOutput, calls=%fused_computation.40 | convolution fusion | flops 510271488 | bytes 7962624 | tf_op jit(solution)/shard_map/dvbs,dvst->dvbt/dot_general | solution.py:53
  16.6 40.3 %all-gather.2.cloned.1.call-done = bf16[6,3,384,384]{3,2,1,0:T(8,128)(2,1)} async-done(((bf16[6,3,96,384]{3,2,1,0:T(8,128)(2,1)}), bf16[6,3,384,384]{3,2,1,0:T(8,128)(2,1)}) %all-gather.2.cloned.1.call-update) | async-done | bytes 5308432 | tf_op jit(solution)/shard_map/all_gather | solution.py:59
  56.9 4.1 %fusion.23 = bf16[6,3,96,384]{3,2,1,0:T(8,128)(2,1)S(1)} fusion(bf16[6,3,96,384]{3,2,1,0:T(8,128)(2,1)} %param.13, bf16[6,3,384,384]{3,2,1,0:T(8,128)(2,1)} %all-gather.2.cloned.1.call-done), kind=kOutput, calls=%fused_computation.42 | convolution fusion | flops 510271488 | bytes 7962624 | tf_op jit(solution)/shard_map/dvbr,dvrs->dvbs/dot_general | solution.py:56
  69.5 164.3 %while.12 = (s32[]{:T(128)}, f32[18,96,384]{2,1,0:T(8,128)}, f32[18,21]{1,0:T(8,128)S(1)}, f32[21,21]{1,0:T(8,128)S(1)}, bf16[18,116,384]{2,1,0:T(8,128)(2,1)}, /*index=5*/bf16[21,128,148]{1,2,0:T(8,128)(2,1)}, s32[]{:T(128)}) while((s32[]{:T(128)}, f32[18,96,384]{2,1,0:T(8,128)}, f32[18,21]{1,0:T(8,128)S(1)}, f32[21,21]{1,0:T(8,128)S(1)}, ...), condition=%wide.region_1.2_spmd, body=%wide.region_0.1_spmd.sunk | while | flops 468033056 | bytes 10153205 | solution.py:88
  70.6 3.2 convert_bitcast_fusion.2
  79.7 3.2 convert_bitcast_fusion.2
  97.9 3.2 convert_bitcast_fusion.2
  116.2 3.2 convert_bitcast_fusion.2
  125.3 3.2 convert_bitcast_fusion.2
  143.6 3.2 convert_bitcast_fusion.2
  152.7 3.2 convert_bitcast_fusion.2
  161.8 3.2 convert_bitcast_fusion.2
  171.0 3.2 convert_bitcast_fusion.2
  180.1 3.2 convert_bitcast_fusion.2
  189.2 3.2 convert_bitcast_fusion.2
  198.4 3.2 convert_bitcast_fusion.2
  207.5 3.2 convert_bitcast_fusion.2
  216.6 3.2 convert_bitcast_fusion.2
  225.7 3.2 convert_bitcast_fusion.2
  236.9 3.6 reshape.134
  244.4 5.6 %all-to-all-start = ((bf16[112,96,128]{2,1,0:T(8,128)(2,1)}), bf16[112,96,128]{2,1,0:T(8,128)(2,1)}, u32[]{:S(2)}, u32[]{:S(2)}) async-start(bf16[112,96,128]{2,1,0:T(8,128)(2,1)} %copy.86), calls=%async_computation | async-start | bytes 5505024 | tf_op jit(solution)/shard_map/all_to_all | solution.py:137
  251.1 60.1 %all-to-all-done = bf16[112,96,128]{2,1,0:T(8,128)(2,1)} async-done(((bf16[112,96,128]{2,1,0:T(8,128)(2,1)}), bf16[112,96,128]{2,1,0:T(8,128)(2,1)}, u32[]{:S(2)}, u32[]{:S(2)}) %all-to-all-start) | async-done | bytes 2752544 | tf_op jit(solution)/shard_map/all_to_all | solution.py:137
  317.0 6.2 %all-to-all-start.1 = ((bf16[112,96,128]{2,1,0:T(8,128)(2,1)}), bf16[112,96,128]{2,1,0:T(8,128)(2,1)}, u32[]{:S(2)}, u32[]{:S(2)}) async-start(bf16[112,96,128]{2,1,0:T(8,128)(2,1)} %copy.89), calls=%async_computation.1 | async-start | bytes 5505024 | tf_op jit(solution)/shard_map/all_to_all | solution.py:146
  323.9 63.6 %all-to-all-done.1 = bf16[112,96,128]{2,1,0:T(8,128)(2,1)} async-done(((bf16[112,96,128]{2,1,0:T(8,128)(2,1)}), bf16[112,96,128]{2,1,0:T(8,128)(2,1)}, u32[]{:S(2)}, u32[]{:S(2)}) %all-to-all-start.1) | async-done | bytes 2752544 | tf_op jit(solution)/shard_map/all_to_all | solution.py:146
  (213 shorter events, 150.1 us)
Async XLA Ops:
  7.2 1.3 copy-start
  7.2 6.1 %copy-start.4 = (s32[48,3]{0,1:T(4,128)S(1)}, s32[48,3]{0,1:T(4,128)}, u32[]{:S(2)}) copy-start(s32[48,3]{0,1:T(4,128)} %param.19) | copy-start | bytes 1732
  7.2 6.1 %copy-start.7 = (f32[8]{0:T(128)S(1)}, f32[8]{0:T(128)}, u32[]{:S(2)}) copy-start(f32[8]{0:T(128)} %param.20) | copy-start | bytes 100
  7.2 6.4 %copy-start.2 = (f32[21,21]{1,0:T(8,128)S(1)}, f32[21,21]{1,0:T(8,128)}, u32[]{:S(2)}) copy-start(f32[21,21]{1,0:T(8,128)} %param.16) | copy-start | bytes 5296
  7.2 49.7 %all-gather.2.cloned.1.call-start = ((), (), s32[]{:S(2)}) async-start(), calls=%async_computation.2 | async-start | bytes 6635520 | tf_op jit(solution)/shard_map/all_gather | solution.py:59
  13.2 2.0 copy-start.3
  13.2 2.0 copy-start.5
  13.2 2.0 copy-start.8
  61.0 3.7 collective-permute-start
  63.2 3.5 collective-permute-start.1
  244.4 6.3 %copy-start.6 = (s32[432]{0:T(512)S(1)}, s32[432]{0:T(512)}, u32[]{:S(2)}) copy-start(s32[432]{0:T(512)} %param.18) | copy-start | bytes 5188
  244.4 66.8 %all-to-all-start = ((bf16[112,96,128]{2,1,0:T(8,128)(2,1)}), bf16[112,96,128]{2,1,0:T(8,128)(2,1)}, u32[]{:S(2)}, u32[]{:S(2)}) async-start(bf16[112,96,128]{2,1,0:T(8,128)(2,1)} %copy.86), calls=%async_computation | async-start | bytes 5505024 | tf_op jit(solution)/shard_map/all_to_all | solution.py:137
  317.0 70.4 %all-to-all-start.1 = ((bf16[112,96,128]{2,1,0:T(8,128)(2,1)}), bf16[112,96,128]{2,1,0:T(8,128)(2,1)}, u32[]{:S(2)}, u32[]{:S(2)}) async-start(bf16[112,96,128]{2,1,0:T(8,128)(2,1)} %copy.89), calls=%async_computation.1 | async-start | bytes 5505024 | tf_op jit(solution)/shard_map/all_to_all | solution.py:146
  387.5 3.1 copy-start.1
Sparse Core Ops, SparseCore 0:
  13.4 43.4 all-gather.1
where the time goes:
time: 404 us; the launch traced here: 401 us
  waiting for transfers between devices  166 us (41%)
  matrix products  107 us (26%)
  local copies, waits for them, and re-layouts  89.5 us (22%)
  starting transfers between devices  15.3 us (4%)
  between operations  14.3 us (4%)
  other arithmetic  8.03 us (2%)
    all_to_all x1, waiting for transfers between devices, per_device(): lax.all_to_all(returned, 'det', split_axis=0, concat_axis=0, tiled=True)  63.6 us
    all_to_all x1, waiting for transfers between devices, per_device(): lax.all_to_all(outgoing, 'det', split_axis=0, concat_axis=0, tiled=True)  60.1 us
    dot_general x18, matrix products, match_image(): jnp.einsum('rtw,kcw->krtc', windows, col_table, preferred_element_type=jn...  57.5 us
    convert_element_type x18, local copies, waits for them, and re-layouts, match_image(): conv_cols = jnp.einsum('rtw,kcw->krtc', windows, col_table, preferred_ele...  54.3 us
    all_gather x1, waiting for transfers between devices, per_device(): lax.all_gather(col_warped, 'row', axis=2, tiled=True)  40.3 us
    dot_general x18, matrix products, match_image(): jnp.einsum('kbr,krs->bs', row_table, conv_cols, preferred_element_type=jn...  25.3 us
    dynamic_slice x36, local copies, waits for them, and re-layouts, per_device(): matched = lax.map(match_image, (tiles_in, coef_rows))  18.5 us
  transfers between devices with their start and end apart: 5, of which 4 were waited for; matrix products, arithmetic and copies ran while one was open for 1% of the time, Pallas kernels for 0%

commit v1 on v0

v1 whole, which is shorter than its diff:
```python
import functools

import jax
import jax.numpy as jnp
from jax import lax
from jax.experimental import pallas as pl
from jax.experimental.pallas import tpu as pltpu
from jax.sharding import PartitionSpec as P

TILE = 128
ALIGN = 16
CHUNKS = (6, 6, 3, 3)
VMEM = 56 * 1024 * 1024
F32 = jnp.float32
BF16 = jnp.bfloat16


def match_kernel(
    slot_ref,
    weight_ref,
    row_ref,
    *refs,
    start,
    taps,
    shards,
    first,
    last,
    parts,
):
    shard_refs = refs[:shards]
    rows_ref, above_ref, below_ref, cols_ref, profile_ref = refs[shards : shards + 5]
    refs = refs[shards + 5 :]
    if not first:
        numer_in = refs[1]
        refs = refs[2:]
    matched_ref = refs[0]
    if last:
        part_refs = refs[1 : 1 + parts]
        numer = refs[1 + parts]
        refs = refs[2 + parts :]
    else:
        numer = refs[1]
        refs = refs[2:]
    image, extended, wide, stack, table = refs
    step = pl.program_id(0)
    band, side = rows_ref.shape[1:]
    pad = above_ref.shape[1]
    span = band + 2 * pad
    reach = (taps - 1) // 2
    tiles = side // TILE

    @pl.when(step == 0)
    def _():
        wide[...] = jnp.zeros_like(wide)
        if first:
            numer[...] = jnp.zeros_like(numer)
        else:
            numer[...] = numer_in[...]

    row = row_ref[0]
    for mask, shard in enumerate(shard_refs):
        at = pl.multiple_of((row ^ mask) * band, band)
        image[pl.ds(at, band), :] = shard[0]
    extended[0:pad, :] = above_ref[0]
    extended[pad : pad + band, :] = rows_ref[0]
    extended[pad + band : span, :] = below_ref[0]
    by_rows = jnp.dot(extended[...], image[...], preferred_element_type=F32).astype(BF16)
    warped = jnp.dot(by_rows, cols_ref[0], preferred_element_type=F32).astype(BF16)
    wide[:, TILE : TILE + side] = warped
    for t in range(taps):
        left = TILE - reach + t
        stack[span * t : span * (t + 1), :] = wide[:, left : left + side]
        profile = jnp.broadcast_to(profile_ref[0, t : t + 1, :], (band, span))
        shifted = pltpu.roll(profile, 0, 1, stride=1, stride_axis=0)
        table[:, span * t : span * (t + 1)] = shifted.astype(BF16)
    matched = jnp.dot(table[...], stack[...], preferred_element_type=F32)
    matched_ref[0] = matched
    index = start + step
    weight = weight_ref[index]
    for q in range(tiles):
        slot = slot_ref[index * tiles + q]
        piece = (weight * matched[:, TILE * q : TILE * (q + 1)]).astype(BF16)
        numer[slot] += piece.astype(F32)

    if last:

        @pl.when(step == pl.num_programs(0) - 1)
        def _():
            each = numer.shape[0] // parts
            for m in range(parts):
                part_refs[m][...] = numer[each * m : each * (m + 1)].astype(BF16)


def match_chunk(slots, weights, row, shards, operands, carry, start, count, taps, parts, last):
    rows, above, below, cols, profiles = operands
    images, band, side = rows.shape
    pad = above.shape[1]
    span = band + 2 * pad
    slot_count = parts * (side // TILE)
    first = carry is None

    def per_image(array):
        offset = start if array.shape[0] == images else 0
        return pl.BlockSpec((1,) + array.shape[1:], lambda i, *_: (i + offset, 0, 0))

    def whole(shape):
        return pl.BlockSpec(shape, lambda i, *_: (0,) * len(shape))

    arrays = list(shards) + [rows, above, below, cols, profiles]
    in_specs = [per_image(a) for a in arrays]
    aliases = {}
    numer_shape = (slot_count, band, TILE)
    if not first:
        aliases = {3 + len(arrays): 0}
        arrays += list(carry)
        in_specs += [pl.BlockSpec(memory_space=pl.ANY), whole(numer_shape)]
    out_shape = [jax.ShapeDtypeStruct((images, band, side), F32)]
    out_specs = [pl.BlockSpec((1, band, side), lambda i, *_: (i + start, 0, 0))]
    scratch = []
    if last:
        part = (slot_count // parts, band, TILE)
        out_shape += [jax.ShapeDtypeStruct(part, BF16)] * parts
        out_specs += [whole(part)] * parts
        scratch = [pltpu.VMEM(numer_shape, F32)]
    else:
        out_shape.append(jax.ShapeDtypeStruct(numer_shape, F32))
        out_specs.append(whole(numer_shape))
    scratch += [
        pltpu.VMEM((side, side), BF16),
        pltpu.VMEM((span, side), BF16),
        pltpu.VMEM((span, side + 2 * TILE), BF16),
        pltpu.VMEM((taps * span, side), BF16),
        pltpu.VMEM((band, taps * span), BF16),
    ]
    flops = 2 * count * (2 * span * side * side + band * taps * span * side)
    return pl.pallas_call(
        functools.partial(
            match_kernel,
            start=start,
            taps=taps,
            shards=len(shards),
            first=first,
            last=last,
            parts=parts,
        ),
        grid_spec=pltpu.PrefetchScalarGridSpec(
            num_scalar_prefetch=3,
            grid=(count,),
            in_specs=in_specs,
            out_specs=out_specs,
            scratch_shapes=scratch,
        ),
        out_shape=out_shape,
        input_output_aliases=aliases,
        compiler_params=pltpu.CompilerParams(vmem_limit_bytes=VMEM),
        cost_estimate=pl.CostEstimate(
            flops=flops, bytes_accessed=count * 900000, transcendentals=0
        ),
    )(slots, weights, row, *arrays)


def template_kernel(denom_ref, *refs):
    part_refs, template_ref, coadd_ref = refs[:-2], refs[-2], refs[-1]
    for q in range(template_ref.shape[0]):
        total = part_refs[0][q].astype(F32)
        for part in part_refs[1:]:
            total = total + part[q].astype(F32)
        box = (total / jnp.maximum(denom_ref[q], 1.0)).astype(BF16)
        template_ref[q] = box
        coadd_ref[:, TILE * q : TILE * (q + 1)] = box


def difference_kernel(slot_ref, matched_ref, *refs):
    template_refs, out_ref, held = refs[:-2], refs[-2], refs[-1]
    step = pl.program_id(0)
    each = template_refs[0].shape[0]
    count, _, side = matched_ref.shape
    tiles = side // TILE

    @pl.when(step == 0)
    def _():
        for m, template in enumerate(template_refs):
            held[each * m : each * (m + 1)] = template[...]

    for i in range(count):
        for q in range(tiles):
            slot = slot_ref[(step * count + i) * tiles + q]
            columns = slice(TILE * q, TILE * (q + 1))
            box = held[slot].astype(F32)
            out_ref[i, :, columns] = (matched_ref[i, :, columns] - box).astype(BF16)


def exchange(value, axis, mask):
    size = lax.axis_size(axis)
    return lax.ppermute(value, axis, [(i, i ^ mask) for i in range(size)])


def per_device(
    images,
    warp_rows,
    warp_cols,
    psf_coef,
    taps,
    dest_patch,
    dest_block,
    weight_index,
    weight_table,
    patch_home,
):
    det_count, visit_count, band, side = images.shape
    kernel_count, tap_count = taps.shape
    reach = (tap_count - 1) // 2
    pad = -(-reach // ALIGN) * ALIGN
    span = band + 2 * pad
    tiles = side // TILE
    det_devices = lax.axis_size("det")
    row_devices = lax.axis_size("row")
    mine = lax.axis_index("det")
    row = lax.axis_index("row").astype(jnp.int32).reshape(1)
    image_count = det_count * visit_count
    pixels = images.reshape(image_count, band, side)
    rows = warp_rows.reshape(image_count, band, side)
    cols = warp_cols.reshape(image_count, side, side)

    chunks = CHUNKS if sum(CHUNKS) == image_count else (image_count,)
    starts = [sum(chunks[:c]) for c in range(len(chunks))]
    far = [exchange(pixels[s : s + n], "row", 2) for s, n in zip(starts, chunks)]
    sibling = exchange(pixels, "row", 1)
    upward = [(i, i + 1) for i in range(row_devices - 1)]
    downward = [(j, i) for i, j in upward]
    above = lax.ppermute(rows[:, band - pad :], "row", upward)
    below = lax.ppermute(rows[:, :pad], "row", downward)

    with jax.named_scope("profiles"):
        scaled = (psf_coef.reshape(image_count, kernel_count)[:, :, None] * taps).astype(BF16)
        profiles = jnp.einsum(
            "nkt,ku->nut", scaled, taps.astype(BF16), preferred_element_type=F32
        )
        profiles = jnp.pad(
            profiles,
            ((0, 0), (0, -tap_count % 8), (pad - reach, span - tap_count - pad + reach)),
        )
    with jax.named_scope("targets"):
        level_count = weight_table.shape[0]
        levels = jnp.arange(level_count)
        weight_all = jnp.sum(
            jnp.where(weight_index[:, :, None] == levels, weight_table, 0.0), axis=2
        ).reshape(-1)
        weights = lax.dynamic_slice_in_dim(weight_all, mine * image_count, image_count, 0)
        patches = jnp.arange(patch_home.shape[0])
        owner = jnp.sum(jnp.where(dest_patch == patches, patch_home, 0), axis=1)
        slot_all = (owner ^ mine) * tiles + dest_block
        slots = lax.dynamic_slice_in_dim(
            slot_all, mine * image_count * tiles, image_count * tiles, 0
        )
        piece_weight = jnp.repeat(weight_all, tiles)
        own = slot_all[:, None] == jnp.arange(tiles)
        denom = jnp.sum(jnp.where(own, piece_weight[:, None], 0.0), axis=0)

    carry = None
    for c, (s, n) in enumerate(zip(starts, chunks)):
        diagonal = exchange(far[c], "row", 1)
        shards = (pixels, sibling, far[c], diagonal)
        carry = match_chunk(
            slots,
            weights,
            row,
            shards,
            (rows, above, below, cols, profiles),
            carry,
            s,
            n,
            tap_count,
            det_devices,
            c == len(chunks) - 1,
        )
    matched, parts = carry[0], carry[1:]
    received = [parts[0]] + [exchange(parts[m], "det", m) for m in range(1, det_devices)]
    box_shape = (tiles, band, TILE)
    template, coadd = pl.pallas_call(
        template_kernel,
        in_specs=[pl.BlockSpec(memory_space=pltpu.SMEM)]
        + [pl.BlockSpec(memory_space=pltpu.VMEM)] * det_devices,
        out_specs=[pl.BlockSpec(memory_space=pltpu.VMEM)] * 2,
        out_shape=[
            jax.ShapeDtypeStruct(box_shape, BF16),
            jax.ShapeDtypeStruct((band, side), BF16),
        ],
        compiler_params=pltpu.CompilerParams(vmem_limit_bytes=VMEM),
    )(denom, *received)
    templates = [template] + [exchange(template, "det", m) for m in range(1, det_devices)]
    group = 3 if image_count % 3 == 0 else 1
    block = pl.BlockSpec((group, band, side), lambda i, *_: (i, 0, 0))
    difference = pl.pallas_call(
        difference_kernel,
        grid_spec=pltpu.PrefetchScalarGridSpec(
            num_scalar_prefetch=1,
            grid=(image_count // group,),
            in_specs=[block] + [pl.BlockSpec(box_shape, lambda i, *_: (0, 0, 0))] * det_devices,
            out_specs=block,
            scratch_shapes=[pltpu.VMEM((det_devices * tiles, band, TILE), BF16)],
        ),
        out_shape=jax.ShapeDtypeStruct((image_count, band, side), BF16),
        compiler_params=pltpu.CompilerParams(vmem_limit_bytes=VMEM),
    )(slots, matched, *templates)
    return difference.reshape(images.shape), coadd.reshape(1, band, side)


def solution(mesh):
    placed = (
        P("det", None, "row", None),
        P("det", None, "row", None),
        P("det", None, None, None),
        P("det", None, None),
        P(),
        P(),
        P(),
        P(),
        P(),
        P(),
    )
    return jax.shard_map(
        per_device,
        mesh=mesh,
        in_specs=placed,
        out_specs=(P("det", None, "row", None), P("det", "row", None)),
        check_vma=False,
    )
```

time: 404 us -> 139 us (0.34)
  waiting for transfers between devices: 166 us -> 35 us
  matrix products: 107 us -> 1.05 us
  local copies, waits for them, and re-layouts: 89.5 us -> 15.4 us
  Pallas kernels: 0 us -> 49.1 us
  starting transfers between devices: 15.3 us -> 35.1 us
  between operations: 14.3 us -> 0.94 us
  other arithmetic: 8.03 us -> 1.61 us
    all_to_all x2 -> x0, waiting for transfers between devices: 124 us -> none  [the longest x1 63.6 us: per_device(): lax.all_to_all(returned, 'det', split_axis=0, concat_axis=0, tiled=True)]
    dot_general x62 -> x1, matrix products: 107 us -> 1.05 us  [per_device(): jnp.einsum('nkt,ku->nut', scaled, taps.astype(BF16), preferred_element_ty...]
    convert_element_type x21 -> x0, local copies, waits for them, and re-layouts: 59.6 us -> none  [the longest x18 54.3 us: match_image(): conv_cols = jnp.einsum('rtw,kcw->krtc', windows, col_table, preferred_ele...]
    pallas_call x0 -> x6, Pallas kernels: none -> 49.1 us  [the longest x4 41.5 us: match_chunk(): pl.pallas_call(functools.partial(match_kernel, start=start, taps=taps, sh...]
    all_gather x1 -> x0, waiting for transfers between devices: 40.3 us -> none  [per_device(): lax.all_gather(col_warped, 'row', axis=2, tiled=True)]
    ppermute x2 -> x25, waiting for transfers between devices: 1.99 us -> 35 us  [the longest x23 35 us: exchange(): return lax.ppermute(value, axis, [(i, i ^ mask) for i in range(size)])]
    ppermute x2 -> x25, starting transfers between devices: 3.46 us -> 35.1 us  [the longest x23 31.7 us: exchange(): return lax.ppermute(value, axis, [(i, i ^ mask) for i in range(size)])]
    dynamic_slice x39 -> x2, local copies, waits for them, and re-layouts: 18.7 us -> 1.91 us  [the longest x1 1.31 us: per_device(): lax.dynamic_slice_in_dim(weight_all, mine * image_count, image_count, 0)]
  transfers between devices with their start and end apart: 5 -> 25, of which waited for: 4 -> 8; matrix products, arithmetic and copies ran while one was open for 1% -> 10% of each run, Pallas kernels for 0% -> 24%
where the time goes in v1:
time: 139 us; the launch traced here: 138 us
  Pallas kernels  49.1 us (35%)
  starting transfers between devices  35.1 us (25%)
  waiting for transfers between devices  35 us (25%)
  local copies, waits for them, and re-layouts  15.4 us (11%)
  other arithmetic  1.61 us (1%)
    pallas_call x4, Pallas kernels, match_chunk(): pl.pallas_call(functools.partial(match_kernel, start=start, taps=taps, sh...  41.5 us
    ppermute x23, waiting for transfers between devices, exchange(): return lax.ppermute(value, axis, [(i, i ^ mask) for i in range(size)])  35 us
    ppermute x23, starting transfers between devices, exchange(): return lax.ppermute(value, axis, [(i, i ^ mask) for i in range(size)])  31.7 us
    pallas_call x1, Pallas kernels, per_device(): pl.pallas_call(difference_kernel, grid_spec=pltpu.PrefetchScalarGridSpec(...  5.7 us
    unnamed x58, local copies, waits for them, and re-layouts  4.59 us
    slice x2, local copies, waits for them, and re-layouts, per_device(): far = [exchange(pixels[s:s + n], 'row', 2) for s, n in zip(starts, chunks)]  3.08 us
  transfers between devices with their start and end apart: 25, of which 8 were waited for; matrix products, arithmetic and copies ran while one was open for 10% of the time, Pallas kernels for 24%

profile of v1, /device:TPU:0, one launch (start us, length us, event | category | flops | bytes accessed | tf_op | source)
XLA Modules:
  0.0 138.2 jit_solution(7471959380989308998)
XLA Ops:
  2.4 2.6 %collective-permute-start.9 = (bf16[6,96,384]{2,1,0:T(8,128)(2,1)S(1)}, bf16[6,96,384]{2,1,0:T(8,128)(2,1)S(1)}, u32[]{:S(2)}, u32[]{:S(2)}) collective-permute-start(bf16[6,96,384]{2,1,0:T(8,128)(2,1)S(1)} %bitcast.34), channel_id=1, source_target_pairs={{0,2},{1,3},{2,0},{3,1},{4,6},{5,7},{6,4},{7,5},{8,10},{9,11},{10,... | collective-permute-start | bytes 1327112 | tf_op jit(solution)/shard_map/ppermute | solution.py:195
  5.0 1.9 %fusion.5 = (bf16[18,16,384]{2,1,0:T(8,128)(2,1)}, bf16[18,16,384]{2,1,0:T(8,128)(2,1)}) fusion(bf16[18,96,384]{2,1,0:T(8,128)(2,1)} %bitcast.27), kind=kLoop, calls=%fused_computation.16 | loop fusion | bytes 884736 | tf_op jit(solution)/shard_map/slice | solution.py:232
  6.9 2.1 %collective-permute-start.3 = (bf16[18,16,384]{2,1,0:T(8,128)(2,1)}, bf16[18,16,384]{2,1,0:T(8,128)(2,1)S(1)}, u32[]{:S(2)}, u32[]{:S(2)}) collective-permute-start(bf16[18,16,384]{2,1,0:T(8,128)(2,1)} %get-tuple-element.41), channel_id=1, source_target_pairs={{0,1},{1,2},{2,3},{4,5},{5,6},{6,7},{8,9},{9,10},{10,11},{12,13},{... | collective-permute-start | bytes 663560 | tf_op jit(solution)/shard_map/ppermute | solution.py:231
  10.3 2.3 %collective-permute-start.7 = (bf16[6,96,384]{2,1,0:T(8,128)(2,1)S(1)}, bf16[6,96,384]{2,1,0:T(8,128)(2,1)S(1)}, u32[]{:S(2)}, u32[]{:S(2)}) collective-permute-start(bf16[6,96,384]{2,1,0:T(8,128)(2,1)S(1)} %bitcast.33), channel_id=1, source_target_pairs={{0,2},{1,3},{2,0},{3,1},{4,6},{5,7},{6,4},{7,5},{8,10},{9,11},{10,... | collective-permute-start | bytes 1327112 | tf_op jit(solution)/shard_map/ppermute | solution.py:195
  12.7 1.8 %slice_bitcast_fusion = (bf16[3,96,384]{2,1,0:T(8,128)(2,1)}, bf16[3,96,384]{2,1,0:T(8,128)(2,1)}) fusion(bf16[6,3,96,384]{3,2,1,0:T(8,128)(2,1)} %param.10), kind=kLoop, calls=%fused_computation.1 | loop fusion | bytes 884736 | tf_op jit(solution)/shard_map/slice | solution.py:227
  16.1 11.6 %collective-permute-done.7.refs_2_ = bf16[6,96,384]{2,1,0:T(8,128)(2,1)S(1)} collective-permute-done((bf16[6,96,384]{2,1,0:T(8,128)(2,1)S(1)}, bf16[6,96,384]{2,1,0:T(8,128)(2,1)S(1)}, u32[]{:S(2)}, u32[]{:S(2)}) %collective-permute-start.7) | collective-permute-done | bytes 442400 | tf_op jit(solution)/shard_map/ppermute | solution.py:195
  37.2 4.5 %collective-permute-done.5.refs_2_ = bf16[3,96,384]{2,1,0:T(8,128)(2,1)S(1)} collective-permute-done((bf16[3,96,384]{2,1,0:T(8,128)(2,1)}, bf16[3,96,384]{2,1,0:T(8,128)(2,1)S(1)}, u32[]{:S(2)}, u32[]{:S(2)}) %collective-permute-start.5) | collective-permute-done | bytes 221216 | tf_op jit(solution)/shard_map/ppermute | solution.py:195
  41.7 4.3 %collective-permute-done.1.refs_2_ = bf16[3,96,384]{2,1,0:T(8,128)(2,1)S(1)} collective-permute-done((bf16[3,96,384]{2,1,0:T(8,128)(2,1)}, bf16[3,96,384]{2,1,0:T(8,128)(2,1)S(1)}, u32[]{:S(2)}, u32[]{:S(2)}) %collective-permute-start.1) | collective-permute-done | bytes 221216 | tf_op jit(solution)/shard_map/ppermute | solution.py:195
  47.3 12.3 %shard_map.113 = (f32[18,96,384]{2,1,0:T(8,128)}, f32[24,96,128]{2,1,0:T(8,128)}) custom-call(s32[54]{0:T(128)} %dynamic_slice.6.slot_ref, f32[18]{0:T(128)} %dynamic_slice.7.weight_ref, s32[1]{0:T(128)} %bitcast.1.row_ref, bf16[18,96,384]{2,1,0:T(8,128)(2,1)} %bitcast.23, bf16[18,96,384]{2,1,0:T(8,128)(2,1)} %copy-done, bf16[6,96,384]{2,1,0:T(8,128)(2,1)} %copy-done.5, ...), custom_call_target="tpu_custom_call" | custom-call | flops 1642070016 | bytes 5400000 | tf_op jit(solution)/shard_map/pallas_call | solution.py:136
  60.4 12.9 %shard_map.114 = (f32[18,96,384]{2,1,0:T(8,128)}, f32[24,96,128]{2,1,0:T(8,128)}) custom-call(s32[54]{0:T(128)} %dynamic_slice.6.slot_ref, f32[18]{0:T(128)} %dynamic_slice.7.weight_ref, s32[1]{0:T(128)} %bitcast.1.row_ref, bf16[18,96,384]{2,1,0:T(8,128)(2,1)} %bitcast.24, bf16[18,96,384]{2,1,0:T(8,128)(2,1)} %copy-done, ...), custom_call_target="tpu_custom_call", output_to_operand_aliasing={{0}: (12, {})} | custom-call | flops 1642070016 | bytes 5400000 | tf_op jit(solution)/shard_map/pallas_call | solution.py:136
  74.0 8.1 %shard_map.115 = (f32[18,96,384]{2,1,0:T(8,128)}, f32[24,96,128]{2,1,0:T(8,128)}) custom-call(s32[54]{0:T(128)} %dynamic_slice.6.slot_ref, f32[18]{0:T(128)} %dynamic_slice.7.weight_ref, s32[1]{0:T(128)} %bitcast.1.row_ref, bf16[18,96,384]{2,1,0:T(8,128)(2,1)} %bitcast.25, bf16[18,96,384]{2,1,0:T(8,128)(2,1)} %copy-done, ...), custom_call_target="tpu_custom_call", output_to_operand_aliasing={{0}: (12, {})} | custom-call | flops 821035008 | bytes 2700000 | tf_op jit(solution)/shard_map/pallas_call | solution.py:136
  82.8 8.2 %shard_map.116 = (f32[18,96,384]{2,1,0:T(8,128)}, bf16[3,96,128]{2,1,0:T(8,128)(2,1)}, bf16[3,96,128]{2,1,0:T(8,128)(2,1)}, bf16[3,96,128]{2,1,0:T(8,128)(2,1)},...) custom-call(s32[54]{0:T(128)} %dynamic_slice.6.slot_ref, ...), custom_call_target="tpu_custom_call", output_to_operand_aliasing={{0}: (12, {})} | custom-call | flops 821035008 | bytes 2700000 | tf_op jit(solution)/shard_map/pallas_call | solution.py:136
  91.0 1.7 %collective-permute-start.11 = (bf16[3,96,128]{2,1,0:T(8,128)(2,1)}, bf16[3,96,128]{2,1,0:T(8,128)(2,1)S(1)}, u32[]{:S(2)}, u32[]{:S(2)}) collective-permute-start(bf16[3,96,128]{2,1,0:T(8,128)(2,1)} %get-tuple-element.27), channel_id=1, source_target_pairs={{0,4},{4,0},{8,12},{12,8},{16,20},{20,16},{24,28},{28,24},{1,5},{5... | collective-permute-start | bytes 221192 | tf_op jit(solution)/shard_map/ppermute | solution.py:195
  94.9 2.8 %collective-permute-start.14 = (bf16[3,96,128]{2,1,0:T(8,128)(2,1)}, bf16[3,96,128]{2,1,0:T(8,128)(2,1)S(1)}, u32[]{:S(2)}, u32[]{:S(2)}) collective-permute-start(bf16[3,96,128]{2,1,0:T(8,128)(2,1)} %get-tuple-element.30), channel_id=1, source_target_pairs={{0,16},{4,20},{8,24},{12,28},{16,0},{20,4},{24,8},{28,12},{1,17},{... | collective-permute-start | bytes 221192 | tf_op jit(solution)/shard_map/ppermute | solution.py:195
  98.9 3.6 %collective-permute-start.16 = (bf16[3,96,128]{2,1,0:T(8,128)(2,1)}, bf16[3,96,128]{2,1,0:T(8,128)(2,1)S(1)}, u32[]{:S(2)}, u32[]{:S(2)}) collective-permute-start(bf16[3,96,128]{2,1,0:T(8,128)(2,1)} %get-tuple-element.32), channel_id=1, source_target_pairs={{0,24},{4,28},{8,16},{12,20},{16,8},{20,12},{24,0},{28,4},{1,25},{... | collective-permute-start | bytes 221192 | tf_op jit(solution)/shard_map/ppermute | solution.py:195
  103.4 5.8 %collective-permute-done.15.refs_5_ = bf16[3,96,128]{2,1,0:T(8,128)(2,1)S(1)} collective-permute-done((bf16[3,96,128]{2,1,0:T(8,128)(2,1)}, bf16[3,96,128]{2,1,0:T(8,128)(2,1)S(1)}, u32[]{:S(2)}, u32[]{:S(2)}) %collective-permute-start.15) | collective-permute-done | bytes 73760 | tf_op jit(solution)/shard_map/ppermute | solution.py:195
  110.6 1.9 %shard_map.117 = (bf16[3,96,128]{2,1,0:T(8,128)(2,1)}, bf16[96,384]{1,0:T(8,128)(2,1)}) custom-call(f32[3]{0:T(128)} %select_reduce_fusion.2.denom_ref, bf16[3,96,128]{2,1,0:T(8,128)(2,1)} %get-tuple-element.26.refs_0_, bf16[3,96,128]{2,1,0:T(8,128)(2,1)} %copy-done.11, bf16[3,96,128]{2,1,0:T(8,128)(2,1)} %copy-done.12, bf16[3,96,128]{2,1,0:T(8,128)(2,1)} %copy-done.13, ...), custom_call_target="tpu_custom_call" | custom-call | tf_op jit(solution)/shard_map/pallas_call | solution.py:280
  113.1 3.5 %collective-permute-start.19 = (bf16[3,96,128]{2,1,0:T(8,128)(2,1)}, bf16[3,96,128]{2,1,0:T(8,128)(2,1)S(1)}, u32[]{:S(2)}, u32[]{:S(2)}) collective-permute-start(bf16[3,96,128]{2,1,0:T(8,128)(2,1)} %get-tuple-element.34.refs_0_), channel_id=1, source_target_pairs={{0,8},{4,12},{8,0},{12,4},{16,24},{20,28},{24,16},{28,20},{1,9},{5... | collective-permute-start | bytes 221192 | tf_op jit(solution)/shard_map/ppermute | solution.py:195
  117.1 3.6 %collective-permute-start.21 = (bf16[3,96,128]{2,1,0:T(8,128)(2,1)}, bf16[3,96,128]{2,1,0:T(8,128)(2,1)S(1)}, u32[]{:S(2)}, u32[]{:S(2)}) collective-permute-start(bf16[3,96,128]{2,1,0:T(8,128)(2,1)} %get-tuple-element.34.refs_0_), channel_id=1, source_target_pairs={{0,16},{4,20},{8,24},{12,28},{16,0},{20,4},{24,8},{28,12},{1,17},{... | collective-permute-start | bytes 221192 | tf_op jit(solution)/shard_map/ppermute | solution.py:195
  120.7 2.4 %collective-permute-start.23 = (bf16[3,96,128]{2,1,0:T(8,128)(2,1)}, bf16[3,96,128]{2,1,0:T(8,128)(2,1)S(1)}, u32[]{:S(2)}, u32[]{:S(2)}) collective-permute-start(bf16[3,96,128]{2,1,0:T(8,128)(2,1)} %get-tuple-element.34.refs_0_), channel_id=1, source_target_pairs={{0,24},{4,28},{8,16},{12,20},{16,8},{20,12},{24,0},{28,4},{1,25},{... | collective-permute-start | bytes 221192 | tf_op jit(solution)/shard_map/ppermute | solution.py:195
  123.1 2.3 %collective-permute-start.24 = (bf16[3,96,128]{2,1,0:T(8,128)(2,1)}, bf16[3,96,128]{2,1,0:T(8,128)(2,1)S(1)}, u32[]{:S(2)}, u32[]{:S(2)}) collective-permute-start(bf16[3,96,128]{2,1,0:T(8,128)(2,1)} %get-tuple-element.34.refs_0_), channel_id=1, source_target_pairs={{0,28},{4,24},{8,20},{12,16},{16,12},{20,8},{24,4},{28,0},{1,29},{... | collective-permute-start | bytes 221192 | tf_op jit(solution)/shard_map/ppermute | solution.py:195
  125.4 3.5 %collective-permute-done.21.refs_4_ = bf16[3,96,128]{2,1,0:T(8,128)(2,1)S(1)} collective-permute-done((bf16[3,96,128]{2,1,0:T(8,128)(2,1)}, bf16[3,96,128]{2,1,0:T(8,128)(2,1)S(1)}, u32[]{:S(2)}, u32[]{:S(2)}) %collective-permute-start.21) | collective-permute-done | bytes 73760 | tf_op jit(solution)/shard_map/ppermute | solution.py:195
  128.9 2.9 %collective-permute-done.22.refs_5_ = bf16[3,96,128]{2,1,0:T(8,128)(2,1)S(1)} collective-permute-done((bf16[3,96,128]{2,1,0:T(8,128)(2,1)}, bf16[3,96,128]{2,1,0:T(8,128)(2,1)S(1)}, u32[]{:S(2)}, u32[]{:S(2)}) %collective-permute-start.22) | collective-permute-done | bytes 73760 | tf_op jit(solution)/shard_map/ppermute | solution.py:195
  132.5 5.7 %shard_map.118 = bf16[18,96,384]{2,1,0:T(8,128)(2,1)} custom-call(s32[54]{0:T(128)} %dynamic_slice.6.slot_ref, f32[18,96,384]{2,1,0:T(8,128)} %get-tuple-element.25.matched_ref, bf16[3,96,128]{2,1,0:T(8,128)(2,1)} %get-tuple-element.34.refs_0_, bf16[3,96,128]{2,1,0:T(8,128)(2,1)} %copy-done.18, bf16[3,96,128]{2,1,0:T(8,128)(2,1)} %copy-done.19, ...), custom_call_target="tpu_custom_call" | custom-call | tf_op jit(solution)/shard_map/pallas_call | solution.py:294
  (106 shorter events, 25.0 us)
Async XLA Ops:
  0.6 45.4 %collective-permute-start = (bf16[18,96,384]{2,1,0:T(8,128)(2,1)}, bf16[18,96,384]{2,1,0:T(8,128)(2,1)S(1)}, u32[]{:S(2)}, u32[]{:S(2)}) collective-permute-start(bf16[18,96,384]{2,1,0:T(8,128)(2,1)} %bitcast.22), channel_id=1, source_target_pairs={{0,1},{1,0},{2,3},{3,2},{4,5},{5,4},{6,7},{7,6},{8,9},{9,8},{10,11... | collective-permute-start | bytes 3981320 | tf_op jit(solution)/shard_map/ppermute | solution.py:195
  2.4 13.6 %collective-permute-start.9 = (bf16[6,96,384]{2,1,0:T(8,128)(2,1)S(1)}, bf16[6,96,384]{2,1,0:T(8,128)(2,1)S(1)}, u32[]{:S(2)}, u32[]{:S(2)}) collective-permute-start(bf16[6,96,384]{2,1,0:T(8,128)(2,1)S(1)} %bitcast.34), channel_id=1, source_target_pairs={{0,2},{1,3},{2,0},{3,1},{4,6},{5,7},{6,4},{7,5},{8,10},{9,11},{10,... | collective-permute-start | bytes 1327112 | tf_op jit(solution)/shard_map/ppermute | solution.py:195
  6.9 26.4 %collective-permute-start.3 = (bf16[18,16,384]{2,1,0:T(8,128)(2,1)}, bf16[18,16,384]{2,1,0:T(8,128)(2,1)S(1)}, u32[]{:S(2)}, u32[]{:S(2)}) collective-permute-start(bf16[18,16,384]{2,1,0:T(8,128)(2,1)} %get-tuple-element.41), channel_id=1, source_target_pairs={{0,1},{1,2},{2,3},{4,5},{5,6},{6,7},{8,9},{9,10},{10,11},{12,13},{... | collective-permute-start | bytes 663560 | tf_op jit(solution)/shard_map/ppermute | solution.py:231
  9.0 25.8 %collective-permute-start.4 = (bf16[18,16,384]{2,1,0:T(8,128)(2,1)}, bf16[18,16,384]{2,1,0:T(8,128)(2,1)S(1)}, u32[]{:S(2)}, u32[]{:S(2)}) collective-permute-start(bf16[18,16,384]{2,1,0:T(8,128)(2,1)} %get-tuple-element.40), channel_id=1, source_target_pairs={{1,0},{2,1},{3,2},{5,4},{6,5},{7,6},{9,8},{10,9},{11,10},{13,12},{... | collective-permute-start | bytes 663560 | tf_op jit(solution)/shard_map/ppermute | solution.py:232
  10.3 17.4 %collective-permute-start.7 = (bf16[6,96,384]{2,1,0:T(8,128)(2,1)S(1)}, bf16[6,96,384]{2,1,0:T(8,128)(2,1)S(1)}, u32[]{:S(2)}, u32[]{:S(2)}) collective-permute-start(bf16[6,96,384]{2,1,0:T(8,128)(2,1)S(1)} %bitcast.33), channel_id=1, source_target_pairs={{0,2},{1,3},{2,0},{3,1},{4,6},{5,7},{6,4},{7,5},{8,10},{9,11},{10,... | collective-permute-start | bytes 1327112 | tf_op jit(solution)/shard_map/ppermute | solution.py:195
  16.0 30.0 %collective-permute-start.10 = (bf16[6,96,384]{2,1,0:T(8,128)(2,1)S(1)}, bf16[6,96,384]{2,1,0:T(8,128)(2,1)S(1)}, u32[]{:S(2)}, u32[]{:S(2)}) collective-permute-start(bf16[6,96,384]{2,1,0:T(8,128)(2,1)S(1)} %collective-permute-done.9.refs_2_), channel_id=1, source_target_pairs={{0,1},{1,0},{2,3},{3,2},{4,5},{5,4},{6,7},{7,6},{8,9},{9,8},{10,11... | collective-permute-start | bytes 1327112 | tf_op jit(solution)/shard_map/ppermute | solution.py:195
  27.7 31.9 %collective-permute-start.8 = (bf16[6,96,384]{2,1,0:T(8,128)(2,1)S(1)}, bf16[6,96,384]{2,1,0:T(8,128)(2,1)S(1)}, u32[]{:S(2)}, u32[]{:S(2)}) collective-permute-start(bf16[6,96,384]{2,1,0:T(8,128)(2,1)S(1)} %collective-permute-done.7.refs_2_), channel_id=1, source_target_pairs={{0,1},{1,0},{2,3},{3,2},{4,5},{5,4},{6,7},{7,6},{8,9},{9,8},{10,11... | collective-permute-start | bytes 1327112 | tf_op jit(solution)/shard_map/ppermute | solution.py:195
  33.3 8.4 %collective-permute-start.5 = (bf16[3,96,384]{2,1,0:T(8,128)(2,1)}, bf16[3,96,384]{2,1,0:T(8,128)(2,1)S(1)}, u32[]{:S(2)}, u32[]{:S(2)}) collective-permute-start(bf16[3,96,384]{2,1,0:T(8,128)(2,1)} %get-tuple-element.38), channel_id=1, source_target_pairs={{0,2},{1,3},{2,0},{3,1},{4,6},{5,7},{6,4},{7,5},{8,10},{9,11},{10,... | collective-permute-start | bytes 663560 | tf_op jit(solution)/shard_map/ppermute | solution.py:195
  34.8 11.2 %collective-permute-start.1 = (bf16[3,96,384]{2,1,0:T(8,128)(2,1)}, bf16[3,96,384]{2,1,0:T(8,128)(2,1)S(1)}, u32[]{:S(2)}, u32[]{:S(2)}) collective-permute-start(bf16[3,96,384]{2,1,0:T(8,128)(2,1)} %get-tuple-element.39), channel_id=1, source_target_pairs={{0,2},{1,3},{2,0},{3,1},{4,6},{5,7},{6,4},{7,5},{8,10},{9,11},{10,... | collective-permute-start | bytes 663560 | tf_op jit(solution)/shard_map/ppermute | solution.py:195
  41.7 31.5 %collective-permute-start.6 = (bf16[3,96,384]{2,1,0:T(8,128)(2,1)S(1)}, bf16[3,96,384]{2,1,0:T(8,128)(2,1)S(1)}, u32[]{:S(2)}, u32[]{:S(2)}) collective-permute-start(bf16[3,96,384]{2,1,0:T(8,128)(2,1)S(1)} %collective-permute-done.5.refs_2_), channel_id=1, source_target_pairs={{0,1},{1,0},{2,3},{3,2},{4,5},{5,4},{6,7},{7,6},{8,9},{9,8},{10,11... | collective-permute-start | bytes 663560 | tf_op jit(solution)/shard_map/ppermute | solution.py:195
  46.0 36.1 %collective-permute-start.2 = (bf16[3,96,384]{2,1,0:T(8,128)(2,1)S(1)}, bf16[3,96,384]{2,1,0:T(8,128)(2,1)S(1)}, u32[]{:S(2)}, u32[]{:S(2)}) collective-permute-start(bf16[3,96,384]{2,1,0:T(8,128)(2,1)S(1)} %collective-permute-done.1.refs_2_), channel_id=1, source_target_pairs={{0,1},{1,0},{2,3},{3,2},{4,5},{5,4},{6,7},{7,6},{8,9},{9,8},{10,11... | collective-permute-start | bytes 663560 | tf_op jit(solution)/shard_map/ppermute | solution.py:195
  91.0 7.9 %collective-permute-start.11 = (bf16[3,96,128]{2,1,0:T(8,128)(2,1)}, bf16[3,96,128]{2,1,0:T(8,128)(2,1)S(1)}, u32[]{:S(2)}, u32[]{:S(2)}) collective-permute-start(bf16[3,96,128]{2,1,0:T(8,128)(2,1)} %get-tuple-element.27), channel_id=1, source_target_pairs={{0,4},{4,0},{8,12},{12,8},{16,20},{20,16},{24,28},{28,24},{1,5},{5... | collective-permute-start | bytes 221192 | tf_op jit(solution)/shard_map/ppermute | solution.py:195
  92.7 9.9 %collective-permute-start.12 = (bf16[3,96,128]{2,1,0:T(8,128)(2,1)}, bf16[3,96,128]{2,1,0:T(8,128)(2,1)S(1)}, u32[]{:S(2)}, u32[]{:S(2)}) collective-permute-start(bf16[3,96,128]{2,1,0:T(8,128)(2,1)} %get-tuple-element.28), channel_id=1, source_target_pairs={{0,8},{4,12},{8,0},{12,4},{16,24},{20,28},{24,16},{28,20},{1,9},{5... | collective-permute-start | bytes 221192 | tf_op jit(solution)/shard_map/ppermute | solution.py:195
  94.6 8.7 %collective-permute-start.13 = (bf16[3,96,128]{2,1,0:T(8,128)(2,1)}, bf16[3,96,128]{2,1,0:T(8,128)(2,1)S(1)}, u32[]{:S(2)}, u32[]{:S(2)}) collective-permute-start(bf16[3,96,128]{2,1,0:T(8,128)(2,1)} %get-tuple-element.29), channel_id=1, source_target_pairs={{0,12},{4,8},{8,4},{12,0},{16,28},{20,24},{24,20},{28,16},{1,13},{... | collective-permute-start | bytes 221192 | tf_op jit(solution)/shard_map/ppermute | solution.py:195
  94.9 8.4 %collective-permute-start.14 = (bf16[3,96,128]{2,1,0:T(8,128)(2,1)}, bf16[3,96,128]{2,1,0:T(8,128)(2,1)S(1)}, u32[]{:S(2)}, u32[]{:S(2)}) collective-permute-start(bf16[3,96,128]{2,1,0:T(8,128)(2,1)} %get-tuple-element.30), channel_id=1, source_target_pairs={{0,16},{4,20},{8,24},{12,28},{16,0},{20,4},{24,8},{28,12},{1,17},{... | collective-permute-start | bytes 221192 | tf_op jit(solution)/shard_map/ppermute | solution.py:195
  97.7 11.4 %collective-permute-start.15 = (bf16[3,96,128]{2,1,0:T(8,128)(2,1)}, bf16[3,96,128]{2,1,0:T(8,128)(2,1)S(1)}, u32[]{:S(2)}, u32[]{:S(2)}) collective-permute-start(bf16[3,96,128]{2,1,0:T(8,128)(2,1)} %get-tuple-element.31), channel_id=1, source_target_pairs={{0,20},{4,16},{8,28},{12,24},{16,4},{20,0},{24,12},{28,8},{1,21},{... | collective-permute-start | bytes 221192 | tf_op jit(solution)/shard_map/ppermute | solution.py:195
  98.9 10.2 %collective-permute-start.16 = (bf16[3,96,128]{2,1,0:T(8,128)(2,1)}, bf16[3,96,128]{2,1,0:T(8,128)(2,1)S(1)}, u32[]{:S(2)}, u32[]{:S(2)}) collective-permute-start(bf16[3,96,128]{2,1,0:T(8,128)(2,1)} %get-tuple-element.32), channel_id=1, source_target_pairs={{0,24},{4,28},{8,16},{12,20},{16,8},{20,12},{24,0},{28,4},{1,25},{... | collective-permute-start | bytes 221192 | tf_op jit(solution)/shard_map/ppermute | solution.py:195
  112.5 8.2 %collective-permute-start.18 = (bf16[3,96,128]{2,1,0:T(8,128)(2,1)}, bf16[3,96,128]{2,1,0:T(8,128)(2,1)S(1)}, u32[]{:S(2)}, u32[]{:S(2)}) collective-permute-start(bf16[3,96,128]{2,1,0:T(8,128)(2,1)} %get-tuple-element.34.refs_0_), channel_id=1, source_target_pairs={{0,4},{4,0},{8,12},{12,8},{16,20},{20,16},{24,28},{28,24},{1,5},{5... | collective-permute-start | bytes 221192 | tf_op jit(solution)/shard_map/ppermute | solution.py:195
  113.1 10.0 %collective-permute-start.19 = (bf16[3,96,128]{2,1,0:T(8,128)(2,1)}, bf16[3,96,128]{2,1,0:T(8,128)(2,1)S(1)}, u32[]{:S(2)}, u32[]{:S(2)}) collective-permute-start(bf16[3,96,128]{2,1,0:T(8,128)(2,1)} %get-tuple-element.34.refs_0_), channel_id=1, source_target_pairs={{0,8},{4,12},{8,0},{12,4},{16,24},{20,28},{24,16},{28,20},{1,9},{5... | collective-permute-start | bytes 221192 | tf_op jit(solution)/shard_map/ppermute | solution.py:195
  116.5 8.9 %collective-permute-start.20 = (bf16[3,96,128]{2,1,0:T(8,128)(2,1)}, bf16[3,96,128]{2,1,0:T(8,128)(2,1)S(1)}, u32[]{:S(2)}, u32[]{:S(2)}) collective-permute-start(bf16[3,96,128]{2,1,0:T(8,128)(2,1)} %get-tuple-element.34.refs_0_), channel_id=1, source_target_pairs={{0,12},{4,8},{8,4},{12,0},{16,28},{20,24},{24,20},{28,16},{1,13},{... | collective-permute-start | bytes 221192 | tf_op jit(solution)/shard_map/ppermute | solution.py:195
  117.1 11.8 %collective-permute-start.21 = (bf16[3,96,128]{2,1,0:T(8,128)(2,1)}, bf16[3,96,128]{2,1,0:T(8,128)(2,1)S(1)}, u32[]{:S(2)}, u32[]{:S(2)}) collective-permute-start(bf16[3,96,128]{2,1,0:T(8,128)(2,1)} %get-tuple-element.34.refs_0_), channel_id=1, source_target_pairs={{0,16},{4,20},{8,24},{12,28},{16,0},{20,4},{24,8},{28,12},{1,17},{... | collective-permute-start | bytes 221192 | tf_op jit(solution)/shard_map/ppermute | solution.py:195
  120.6 11.2 %collective-permute-start.22 = (bf16[3,96,128]{2,1,0:T(8,128)(2,1)}, bf16[3,96,128]{2,1,0:T(8,128)(2,1)S(1)}, u32[]{:S(2)}, u32[]{:S(2)}) collective-permute-start(bf16[3,96,128]{2,1,0:T(8,128)(2,1)} %get-tuple-element.34.refs_0_), channel_id=1, source_target_pairs={{0,20},{4,16},{8,28},{12,24},{16,4},{20,0},{24,12},{28,8},{1,21},{... | collective-permute-start | bytes 221192 | tf_op jit(solution)/shard_map/ppermute | solution.py:195
  120.7 11.1 %collective-permute-start.23 = (bf16[3,96,128]{2,1,0:T(8,128)(2,1)}, bf16[3,96,128]{2,1,0:T(8,128)(2,1)S(1)}, u32[]{:S(2)}, u32[]{:S(2)}) collective-permute-start(bf16[3,96,128]{2,1,0:T(8,128)(2,1)} %get-tuple-element.34.refs_0_), channel_id=1, source_target_pairs={{0,24},{4,28},{8,16},{12,20},{16,8},{20,12},{24,0},{28,4},{1,25},{... | collective-permute-start | bytes 221192 | tf_op jit(solution)/shard_map/ppermute | solution.py:195
  123.1 8.7 %collective-permute-start.24 = (bf16[3,96,128]{2,1,0:T(8,128)(2,1)}, bf16[3,96,128]{2,1,0:T(8,128)(2,1)S(1)}, u32[]{:S(2)}, u32[]{:S(2)}) collective-permute-start(bf16[3,96,128]{2,1,0:T(8,128)(2,1)} %get-tuple-element.34.refs_0_), channel_id=1, source_target_pairs={{0,28},{4,24},{8,20},{12,16},{16,12},{20,8},{24,4},{28,0},{1,29},{... | collective-permute-start | bytes 221192 | tf_op jit(solution)/shard_map/ppermute | solution.py:195
  (30 other events, 243.2 us)

commit v2 on v1

v2 whole, which is shorter than its diff:
```python
import functools

import jax
import jax.numpy as jnp
from jax import lax
from jax.experimental import pallas as pl
from jax.experimental.pallas import tpu as pltpu
from jax.sharding import PartitionSpec as P

TILE = 128
ALIGN = 16
CHUNKS = (4, 3, 2)
INNER = 7
MIB = 1024 * 1024
F32 = jnp.float32
BF16 = jnp.bfloat16


def match_kernel(
    slot_ref, weight_ref, row_ref, *refs, start, taps, first, last
):
    shard_refs = refs[:4]
    rows_refs = refs[4:6]
    edge_refs = refs[6:8]
    cols_ref, profile_ref = refs[8:10]
    refs = refs[10:]
    if not first:
        carried = refs[2:4]
        refs = refs[4:]
    matched_refs, sums_refs = refs[:2], refs[2:4]
    refs = refs[4:]
    image, extended, wide, stack, table = refs[:5]
    numers = (sums_refs[0], refs[5]) if last else sums_refs
    step = pl.program_id(0)
    images = pl.num_programs(0)
    band, side = rows_refs[0].shape[1:]
    pad = edge_refs[0].shape[1]
    span = band + 2 * pad
    reach = (taps - 1) // 2
    outer = -(-taps // INNER)
    tiles = side // TILE
    width = stack.shape[2]
    row = row_ref[0]
    core = row & 1

    @pl.when(step == 0)
    def _():
        wide[...] = jnp.zeros_like(wide)
        table[...] = jnp.zeros_like(table)
        for m in range(2):
            numers[m][...] = jnp.zeros_like(numers[m]) if first else carried[m][...]

    for mask, shard in enumerate(shard_refs):
        at = pl.multiple_of((row ^ mask) * band, band)
        image[pl.ds(at, band), :] = shard[0]
    edge = edge_refs[0][0] + edge_refs[1][0]
    blank = jnp.zeros_like(edge)
    extended[0:pad, :] = jnp.where(row >= 2, edge, blank)
    extended[pad + 2 * band :, :] = jnp.where(row >= 2, blank, edge)
    for m, rows in enumerate(rows_refs):
        at = pl.multiple_of(pad + (core ^ m) * band, ALIGN)
        extended[pl.ds(at, band), :] = rows[0]
    by_rows = jnp.dot(extended[...], image[...], preferred_element_type=F32).astype(BF16)
    warped = jnp.dot(by_rows, cols_ref[0], preferred_element_type=F32).astype(BF16)
    wide[:, TILE : TILE + side] = warped
    for b in range(INNER):
        left = TILE - reach + b
        shifted = wide[:, left : left + width]
        for half in range(2):
            stack[half, span * b : span * (b + 1), :] = shifted[band * half : band * half + span]
    for t in range(taps):
        a, b = t // INNER, t % INNER
        profile = jnp.broadcast_to(profile_ref[0, t : t + 1, :], (band, span))
        toeplitz = pltpu.roll(profile, 0, 1, stride=1, stride_axis=0).astype(BF16)
        table[band * a : band * (a + 1), span * b : span * (b + 1)] = toeplitz
    index = start + step
    weight = weight_ref[index]
    for m in range(2):
        partial = jnp.dot(table[...], stack[core ^ m], preferred_element_type=F32)
        matched = partial[0:band, 0:side]
        for a in range(1, outer):
            matched = matched + partial[band * a : band * (a + 1), INNER * a : INNER * a + side]
        matched_refs[m][0] = matched
        for q in range(tiles):
            slot = slot_ref[index * tiles + q]
            piece = (weight * matched[:, TILE * q : TILE * (q + 1)]).astype(BF16)
            numers[m][slot] += piece.astype(F32)

    if last:

        @pl.when(step == images - 1)
        def _():
            sums_refs[1][...] = numers[1][...].astype(BF16)


def match_chunk(slots, weights, row, operands, carry, start, count, taps, slot_count, last):
    pixels, _, _, _, rows, _, edge, _, _, _ = operands
    images, band, side = pixels.shape
    half = images // 2
    pad = edge.shape[1]
    span = band + 2 * pad
    outer = -(-taps // INNER)
    first = carry is None
    width = side + TILE

    def block(array):
        if array.shape[0] == images:
            place = lambda i, slot, weight, row: ((row[0] & 1) * half + start + i, 0, 0)
        elif array.shape[0] == half:
            place = lambda i, *_: (start + i, 0, 0)
        else:
            place = lambda i, *_: (i, 0, 0)
        return pl.BlockSpec((1,) + array.shape[1:], place)

    whole = lambda shape: pl.BlockSpec(shape, lambda i, *_: (0,) * len(shape))
    in_specs = [block(a) for a in operands]
    arrays = [
        pltpu.with_memory_space_constraint(a, pltpu.HBM) if a.shape[0] == images else a
        for a in operands
    ]
    aliases = {}
    numer_shape = (slot_count, band, TILE)
    matched_shape = jax.ShapeDtypeStruct((half, band, side), F32)
    if not first:
        aliases = {3 + len(arrays): 0, 4 + len(arrays): 1}
        arrays += list(carry)
        in_specs += [pl.BlockSpec(memory_space=pl.ANY)] * 2 + [whole(numer_shape)] * 2
    out_shape = [matched_shape] * 2 + [
        jax.ShapeDtypeStruct(numer_shape, F32),
        jax.ShapeDtypeStruct(numer_shape, BF16 if last else F32),
    ]
    out_specs = [block(matched_shape)] * 2 + [whole(numer_shape)] * 2
    scratch = [
        pltpu.VMEM((side, side), BF16),
        pltpu.VMEM((2 * band + 2 * pad, side), BF16),
        pltpu.VMEM((2 * band + 2 * pad, side + 3 * TILE), BF16),
        pltpu.VMEM((2, INNER * span, width), BF16),
        pltpu.VMEM((outer * band, INNER * span), BF16),
    ]
    if last:
        scratch.append(pltpu.VMEM(numer_shape, F32))
    numer_bytes = 4 * slot_count * band * TILE
    return pl.pallas_call(
        functools.partial(match_kernel, start=start, taps=taps, first=first, last=last),
        grid_spec=pltpu.PrefetchScalarGridSpec(
            num_scalar_prefetch=3,
            grid=(count,),
            in_specs=in_specs,
            out_specs=out_specs,
            scratch_shapes=scratch,
        ),
        out_shape=out_shape,
        input_output_aliases=aliases,
        compiler_params=pltpu.CompilerParams(
            vmem_limit_bytes=min(60 * MIB, 36 * MIB + (4 if first else 8) * numer_bytes)
        ),
        cost_estimate=pl.CostEstimate(
            flops=count * 2000000000, bytes_accessed=count * 1000000, transcendentals=0
        ),
    )(slots, weights, row, *arrays)


def merge_kernel(own_ref, other_ref, *part_refs):
    each = part_refs[0].shape[0]
    for m, part in enumerate(part_refs):
        boxes = slice(each * m, each * (m + 1))
        part[...] = (own_ref[boxes] + other_ref[boxes].astype(F32)).astype(BF16)


def template_kernel(denom_ref, *refs):
    part_refs, template_ref, coadd_ref = refs[:-2], refs[-2], refs[-1]
    for q in range(template_ref.shape[0]):
        total = part_refs[0][q].astype(F32)
        for part in part_refs[1:]:
            total = total + part[q].astype(F32)
        box = (total / jnp.maximum(denom_ref[q], 1.0)).astype(BF16)
        template_ref[q] = box
        coadd_ref[:, TILE * q : TILE * (q + 1)] = box


def difference_kernel(slot_ref, row_ref, own_ref, other_ref, *refs):
    template_refs, out_ref, held = refs[:-2], refs[-2], refs[-1]
    step = pl.program_id(0)
    each = template_refs[0].shape[0]
    count, _, side = own_ref.shape
    tiles = side // TILE

    @pl.when(step == 0)
    def _():
        for m, template in enumerate(template_refs):
            held[each * m : each * (m + 1)] = template[...]

    def subtract(matched_ref):
        for i in range(count):
            for q in range(tiles):
                slot = slot_ref[(step * count + i) * tiles + q]
                columns = slice(TILE * q, TILE * (q + 1))
                box = held[slot].astype(F32)
                out_ref[i, :, columns] = (matched_ref[i, :, columns] - box).astype(BF16)

    mine = (step * 2 // pl.num_programs(0)) == (row_ref[0] & 1)
    pl.when(mine)(lambda: subtract(own_ref))
    pl.when(jnp.logical_not(mine))(lambda: subtract(other_ref))


def exchange(value, axis, mask, turn=0):
    size = lax.axis_size(axis)
    pairs = [(i, i ^ mask) for i in range(size)]
    return lax.ppermute(value, axis, pairs[turn:] + pairs[:turn])


def per_device(
    images,
    warp_rows,
    warp_cols,
    psf_coef,
    taps,
    dest_patch,
    dest_block,
    weight_index,
    weight_table,
    patch_home,
):
    det_count, visit_count, band, side = images.shape
    kernel_count, tap_count = taps.shape
    reach = (tap_count - 1) // 2
    pad = -(-reach // ALIGN) * ALIGN
    span = band + 2 * pad
    tiles = side // TILE
    det_devices = lax.axis_size("det")
    mine = lax.axis_index("det")
    row = lax.axis_index("row").astype(jnp.int32)
    core = row & 1
    image_count = det_count * visit_count
    half = image_count // 2
    assert lax.axis_size("row") == 4 and image_count == 2 * half
    pixels = images.reshape(image_count, band, side)
    rows = warp_rows.reshape(image_count, band, side)
    cols = warp_cols.reshape(image_count, side, side)
    row_one = row.reshape(1)

    chunks = CHUNKS if sum(CHUNKS) == half and det_devices <= 8 else (half,)
    starts = [sum(chunks[:c]) for c in range(len(chunks))]

    def portion(array, which, first, count):
        return lax.dynamic_slice_in_dim(array, (core ^ which) * half + first, count, 0)

    far, cross = [], []
    for c, (s, n) in enumerate(zip(starts, chunks)):
        far.append(exchange(portion(pixels, 0, s, n), "row", 2, c))
        cross.append(exchange(portion(pixels, 1, s, n), "row", 3, c))
    sibling = exchange(portion(pixels, 1, 0, half), "row", 1)
    sibling_rows = exchange(portion(rows, 1, 0, half), "row", 1)
    edge_at = jnp.where(row < 2, band - pad, 0)

    def edge(which, pairs):
        part = lax.dynamic_slice(
            rows, ((core ^ which) * half, edge_at, 0), (half, pad, side)
        )
        return lax.ppermute(part, "row", pairs)

    edges = (edge(0, [(2, 0), (1, 3)]), edge(1, [(2, 1), (1, 2)]))

    with jax.named_scope("profiles"):
        scaled = (psf_coef.reshape(image_count, kernel_count)[:, :, None] * taps).astype(BF16)
        profiles = jnp.einsum(
            "nkt,ku->nut", scaled, taps.astype(BF16), preferred_element_type=F32
        )
        profiles = jnp.pad(
            profiles,
            ((0, 0), (0, -tap_count % 8), (pad - reach, span - tap_count - pad + reach)),
        )
    with jax.named_scope("targets"):
        levels = jnp.arange(weight_table.shape[0])
        weight_all = jnp.sum(
            jnp.where(weight_index[:, :, None] == levels, weight_table, 0.0), axis=2
        ).reshape(-1)
        weights = lax.dynamic_slice_in_dim(weight_all, mine * image_count + core * half, half, 0)
        patches = jnp.arange(patch_home.shape[0])
        owner = jnp.sum(jnp.where(dest_patch == patches, patch_home, 0), axis=1)
        slot_all = (owner ^ mine) * tiles + dest_block
        slots = lax.dynamic_slice_in_dim(
            slot_all, mine * image_count * tiles, image_count * tiles, 0
        )
        own_slots = lax.dynamic_slice_in_dim(slots, core * half * tiles, half * tiles, 0)
        piece_weight = jnp.repeat(weight_all, tiles)
        own = slot_all[:, None] == jnp.arange(tiles)
        denom = jnp.sum(jnp.where(own, piece_weight[:, None], 0.0), axis=0)

    carry = None
    slot_count = det_devices * tiles
    for c, (s, n) in enumerate(zip(starts, chunks)):
        operands = (
            pixels, sibling, far[c], cross[c], rows, sibling_rows, edges[0], edges[1], cols, profiles,
        )
        carry = match_chunk(
            own_slots, weights, row_one, operands, carry, s, n, tap_count, slot_count,
            c == len(chunks) - 1,
        )
    matched, matched_sent, own_sums, sums_sent = carry
    other_sums = exchange(sums_sent, "row", 1)
    box_shape = (tiles, band, TILE)
    box = jax.ShapeDtypeStruct(box_shape, BF16)
    in_vmem = pl.BlockSpec(memory_space=pltpu.VMEM)
    small = pltpu.CompilerParams(vmem_limit_bytes=4 * MIB + 16 * slot_count * band * TILE)
    parts = pl.pallas_call(
        merge_kernel,
        in_specs=[in_vmem] * 2,
        out_specs=[in_vmem] * det_devices,
        out_shape=[box] * det_devices,
        compiler_params=small,
    )(own_sums, other_sums)
    order = sorted(range(1, det_devices), key=lambda m: -m)
    received = [parts[0]] + [None] * (det_devices - 1)
    for m in order:
        received[m] = exchange(parts[m], "det", m)
    other_matched = exchange(matched_sent, "row", 1)
    template, coadd = pl.pallas_call(
        template_kernel,
        in_specs=[pl.BlockSpec(memory_space=pltpu.SMEM)] + [in_vmem] * det_devices,
        out_specs=[in_vmem] * 2,
        out_shape=[box, jax.ShapeDtypeStruct((band, side), BF16)],
        compiler_params=small,
    )(denom, *received)
    templates = [template] + [None] * (det_devices - 1)
    for m in order:
        templates[m] = exchange(template, "det", m)
    group = 3 if half % 3 == 0 else 1
    steps = half // group

    def half_block(which):
        def place(i, slot, row):
            return (jnp.clip(i - ((row[0] & 1) ^ which) * steps, 0, steps - 1), 0, 0)

        return pl.BlockSpec((group, band, side), place)

    difference = pl.pallas_call(
        difference_kernel,
        grid_spec=pltpu.PrefetchScalarGridSpec(
            num_scalar_prefetch=2,
            grid=(2 * steps,),
            in_specs=[half_block(0), half_block(1)]
            + [pl.BlockSpec(box_shape, lambda i, *_: (0, 0, 0))] * det_devices,
            out_specs=pl.BlockSpec((group, band, side), lambda i, *_: (i, 0, 0)),
            scratch_shapes=[pltpu.VMEM((slot_count, band, TILE), BF16)],
        ),
        out_shape=jax.ShapeDtypeStruct((image_count, band, side), BF16),
        compiler_params=small,
    )(slots, row_one, matched, other_matched, *templates)
    return difference.reshape(images.shape), coadd.reshape(1, band, side)


def solution(mesh):
    placed = (
        P("det", None, "row", None),
        P("det", None, "row", None),
        P("det", None, None, None),
        P("det", None, None),
        P(),
        P(),
        P(),
        P(),
        P(),
        P(),
    )
    return jax.shard_map(
        per_device,
        mesh=mesh,
        in_specs=placed,
        out_specs=(P("det", None, "row", None), P("det", "row", None)),
        check_vma=False,
    )
```

time: 139 us -> 101 us (0.73)
  Pallas kernels: 49.1 us -> 29.5 us
  waiting for transfers between devices: 35 us -> 15.7 us
  starting transfers between devices: 35.1 us -> 43.6 us
  local copies, waits for them, and re-layouts: 15.4 us -> 9.69 us
    ppermute x25 -> x26, waiting for transfers between devices: 35 us -> 15.7 us  [the longest x24 15.7 us: exchange(): return lax.ppermute(value, axis, pairs[turn:] + pairs[:turn])]
    pallas_call x4, Pallas kernels: 41.5 us -> 25.3 us  [the longest x3 25.2 us: match_chunk(): pl.pallas_call(functools.partial(match_kernel, start=start, taps=taps, fi...]
    ppermute x25 -> x26, starting transfers between devices: 35.1 us -> 43.6 us  [the longest x24 41.5 us: exchange(): return lax.ppermute(value, axis, pairs[turn:] + pairs[:turn])]
    slice x3 -> x0, local copies, waits for them, and re-layouts: 4.94 us -> none  [the longest x2 3.08 us: per_device(): far = [exchange(pixels[s:s + n], 'row', 2) for s, n in zip(starts, chunks)]]
    unnamed x58 -> x18, local copies, waits for them, and re-layouts: 4.59 us -> 0.04 us
    dynamic_slice x1 -> x8, local copies, waits for them, and re-layouts: 1.31 us -> 5.8 us  [the longest x5 3.92 us: portion(): lax.dynamic_slice_in_dim(array, (core ^ which) * half + first, count, 0)]
    pallas_call x1, Pallas kernels: 5.7 us -> 2.95 us  [per_device(): pl.pallas_call(difference_kernel, grid_spec=pltpu.PrefetchScalarGridSpec(...]
  transfers between devices with their start and end apart: 25 -> 26, of which waited for: 8 -> 5; matrix products, arithmetic and copies ran while one was open for 10% -> 9% of each run, Pallas kernels for 24% -> 20%
where the time goes in v2:
time: 101 us
  starting transfers between devices  43.6 us (43%)
  Pallas kernels  29.5 us (29%)
  waiting for transfers between devices  15.7 us (16%)
  local copies, waits for them, and re-layouts  9.69 us (10%)
    ppermute x24, starting transfers between devices, exchange(): return lax.ppermute(value, axis, pairs[turn:] + pairs[:turn])  41.5 us
    pallas_call x3, Pallas kernels, match_chunk(): pl.pallas_call(functools.partial(match_kernel, start=start, taps=taps, fi...  25.2 us
    ppermute x24, waiting for transfers between devices, exchange(): return lax.ppermute(value, axis, pairs[turn:] + pairs[:turn])  15.7 us
    dynamic_slice x5, local copies, waits for them, and re-layouts, portion(): lax.dynamic_slice_in_dim(array, (core ^ which) * half + first, count, 0)  3.92 us
    pallas_call x1, Pallas kernels, per_device(): pl.pallas_call(difference_kernel, grid_spec=pltpu.PrefetchScalarGridSpec(...  2.95 us
    ppermute x2, starting transfers between devices, edge(): return lax.ppermute(part, 'row', pairs)  2.08 us
  transfers between devices with their start and end apart: 26, of which 5 were waited for; matrix products, arithmetic and copies ran while one was open for 9% of the time, Pallas kernels for 20%

profile of v2, /device:TPU:0, one launch (start us, length us, event | category | flops | bytes accessed | tf_op | source)
XLA Modules:
  0.0 100.6 jit_solution(14952773622555370156)
XLA Ops:
  0.7 1.7 %constant_dynamic-slice_fusion.3 = (bf16[9,16,384]{2,1,0:T(8,128)(2,1)S(1)}, bf16[9,16,384]{2,1,0:T(8,128)(2,1)}) fusion(bf16[18,96,384]{2,1,0:T(8,128)(2,1)} %bitcast.22, s32[]{:T(128)S(6)} %select_n.60, s32[]{:T(128)S(6)} %select_n.64, s32[]{:T(128)S(6)} %select_n.63), kind=kLoop, calls=%fused_computation.15 | loop fusion | bytes 442380 | tf_op jit(solution)/shard_map/dynamic_slice | solution.py:257
  2.4 1.4 %collective-permute-start.4 = (bf16[9,16,384]{2,1,0:T(8,128)(2,1)}, bf16[9,16,384]{2,1,0:T(8,128)(2,1)S(1)}, u32[]{:S(2)}, u32[]{:S(2)}) collective-permute-start(bf16[9,16,384]{2,1,0:T(8,128)(2,1)} %get-tuple-element.51), channel_id=1, source_target_pairs={{2,0},{1,3},{6,4},{5,7},{10,8},{9,11},{14,12},{13,15},{18,16},{17,... | collective-permute-start | bytes 331784 | tf_op jit(solution)/shard_map/ppermute | solution.py:260
  3.8 2.0 %constant_dynamic-slice_fusion.9 = (bf16[4,96,384]{2,1,0:T(8,128)(2,1)}, bf16[4,96,384]{2,1,0:T(8,128)(2,1)}) fusion(bf16[18,96,384]{2,1,0:T(8,128)(2,1)} %bitcast.12, s32[]{:T(128)S(6)} %select_n.60, s32[]{:T(128)S(6)} %select_n.63), kind=kLoop, calls=%fused_computation.21 | loop fusion | bytes 1179656 | tf_op jit(solution)/shard_map/dynamic_slice | solution.py:246
  5.8 3.0 %collective-permute-start.8 = (bf16[4,96,384]{2,1,0:T(8,128)(2,1)}, bf16[4,96,384]{2,1,0:T(8,128)(2,1)S(1)}, u32[]{:S(2)}, u32[]{:S(2)}) collective-permute-start(bf16[4,96,384]{2,1,0:T(8,128)(2,1)} %get-tuple-element.47), channel_id=1, source_target_pairs={{0,2},{1,3},{2,0},{3,1},{4,6},{5,7},{6,4},{7,5},{8,10},{9,11},{10,... | collective-permute-start | bytes 884744 | tf_op jit(solution)/shard_map/ppermute | solution.py:209
  8.8 1.6 %collective-permute-start.9 = (bf16[4,96,384]{2,1,0:T(8,128)(2,1)}, bf16[4,96,384]{2,1,0:T(8,128)(2,1)S(1)}, u32[]{:S(2)}, u32[]{:S(2)}) collective-permute-start(bf16[4,96,384]{2,1,0:T(8,128)(2,1)} %get-tuple-element.46), channel_id=1, source_target_pairs={{0,3},{1,2},{2,1},{3,0},{4,7},{5,6},{6,5},{7,4},{8,11},{9,10},{10,... | collective-permute-start | bytes 884744 | tf_op jit(solution)/shard_map/ppermute | solution.py:209
  14.3 1.8 %pad.4.refs_9_ = f32[18,24,128]{2,1,0:T(8,128)} pad(f32[18,21,21]{2,1,0:T(8,128)} %convolution_bitcast_fusion, f32[]{:T(128)} %constant.43.clone.1), padding=0_0x0_3x6_101 | pad | bytes 252940 | tf_op jit(solution)/shard_map/profiles/jit(_pad)/pad | solution.py:269
  16.9 8.9 %collective-permute-start.6 = (bf16[3,96,384]{2,1,0:T(8,128)(2,1)S(1)}, bf16[3,96,384]{2,1,0:T(8,128)(2,1)S(1)}, u32[]{:S(2)}, u32[]{:S(2)}) collective-permute-start(bf16[3,96,384]{2,1,0:T(8,128)(2,1)S(1)} %get-tuple-element.49), channel_id=1, source_target_pairs={{1,3},{2,0},{3,1},{0,2},{5,7},{6,4},{7,5},{4,6},{9,11},{10,8},{11,... | collective-permute-start | bytes 663560 | tf_op jit(solution)/shard_map/ppermute | solution.py:209
  26.0 1.6 %collective-permute-start.2 = (bf16[2,96,384]{2,1,0:T(8,128)(2,1)S(1)}, bf16[2,96,384]{2,1,0:T(8,128)(2,1)S(1)}, u32[]{:S(2)}, u32[]{:S(2)}) collective-permute-start(bf16[2,96,384]{2,1,0:T(8,128)(2,1)S(1)} %get-tuple-element.52), channel_id=1, source_target_pairs={{2,1},{3,0},{0,3},{1,2},{6,5},{7,4},{4,7},{5,6},{10,9},{11,8},{8,1... | collective-permute-start | bytes 442376 | tf_op jit(solution)/shard_map/ppermute | solution.py:209
  27.7 10.3 %shard_map.113 = (f32[9,96,384]{2,1,0:T(8,128)S(1)}, f32[9,96,384]{2,1,0:T(8,128)}, f32[24,96,128]{2,1,0:T(8,128)S(1)}, f32[24,96,128]{2,1,0:T(8,128)S(1)}) custom-call(s32[27]{0:T(128)S(1)} %dynamic_slice.43.slot_ref, f32[9]{0:T(128)S(1)} %dynamic_slice.44.weight_ref, s32[1]{0:T(128)} %bitcast.1.row_ref, bf16[18,96,384]{2,1,0:T(8,128)(2,1)} %bitcast.13, ...), custom_call_target="tpu_custom_call" | custom-call | flops 8000000000 | bytes 4000000 | tf_op jit(solution)/shard_map/pallas_call | solution.py:143
  38.0 8.4 %shard_map.114 = (f32[9,96,384]{2,1,0:T(8,128)S(1)}, f32[9,96,384]{2,1,0:T(8,128)}, f32[24,96,128]{2,1,0:T(8,128)S(1)}, f32[24,96,128]{2,1,0:T(8,128)S(1)}) custom-call(s32[27]{0:T(128)S(1)} %dynamic_slice.43.slot_ref, f32[9]{0:T(128)S(1)} %dynamic_slice.44.weight_ref, s32[1]{0:T(128)} %bitcast.1.row_ref, ...), custom_call_target="tpu_custom_call", output_to_operand_aliasing={{0}: (13, {}), {1}: (14, {})} | custom-call | flops 6000000000 | bytes 3000000 | tf_op jit(solution)/shard_map/pallas_call | solution.py:143
  46.4 6.5 %shard_map.115 = (f32[9,96,384]{2,1,0:T(8,128)S(1)}, f32[9,96,384]{2,1,0:T(8,128)}, f32[24,96,128]{2,1,0:T(8,128)S(1)}, bf16[24,96,128]{2,1,0:T(8,128)(2,1)S(1)}) custom-call(s32[27]{0:T(128)S(1)} %dynamic_slice.43.slot_ref, f32[9]{0:T(128)S(1)} %dynamic_slice.44.weight_ref, s32[1]{0:T(128)} %bitcast.1.row_ref, ...), custom_call_target="tpu_custom_call", output_to_operand_aliasing={{0}: (13, {}), {1}: (14, {})} | custom-call | flops 4000000000 | bytes 2000000 | tf_op jit(solution)/shard_map/pallas_call | solution.py:143
  53.4 3.4 %collective-permute-done.11.other_ref = bf16[24,96,128]{2,1,0:T(8,128)(2,1)S(1)} collective-permute-done((bf16[24,96,128]{2,1,0:T(8,128)(2,1)S(1)}, bf16[24,96,128]{2,1,0:T(8,128)(2,1)S(1)}, u32[]{:S(2)}, u32[]{:S(2)}) %collective-permute-start.11) | collective-permute-done | bytes 589856 | tf_op jit(solution)/shard_map/ppermute | solution.py:209
  56.9 2.2 %collective-permute-start.12 = (bf16[3,96,128]{2,1,0:T(8,128)(2,1)S(1)}, bf16[3,96,128]{2,1,0:T(8,128)(2,1)S(1)}, u32[]{:S(2)}, u32[]{:S(2)}) collective-permute-start(bf16[3,96,128]{2,1,0:T(8,128)(2,1)S(1)} %get-tuple-element.37), channel_id=1, source_target_pairs={{0,4},{4,0},{8,12},{12,8},{16,20},{20,16},{24,28},{28,24},{1,5},{5... | collective-permute-start | bytes 221192 | tf_op jit(solution)/shard_map/ppermute | solution.py:209
  59.1 1.6 %collective-permute-start.13 = (bf16[3,96,128]{2,1,0:T(8,128)(2,1)S(1)}, bf16[3,96,128]{2,1,0:T(8,128)(2,1)S(1)}, u32[]{:S(2)}, u32[]{:S(2)}) collective-permute-start(bf16[3,96,128]{2,1,0:T(8,128)(2,1)S(1)} %get-tuple-element.38), channel_id=1, source_target_pairs={{0,8},{4,12},{8,0},{12,4},{16,24},{20,28},{24,16},{28,20},{1,9},{5... | collective-permute-start | bytes 221192 | tf_op jit(solution)/shard_map/ppermute | solution.py:209
  62.5 3.1 %collective-permute-start.15 = (bf16[3,96,128]{2,1,0:T(8,128)(2,1)S(1)}, bf16[3,96,128]{2,1,0:T(8,128)(2,1)S(1)}, u32[]{:S(2)}, u32[]{:S(2)}) collective-permute-start(bf16[3,96,128]{2,1,0:T(8,128)(2,1)S(1)} %get-tuple-element.40), channel_id=1, source_target_pairs={{0,16},{4,20},{8,24},{12,28},{16,0},{20,4},{24,8},{28,12},{1,17},{... | collective-permute-start | bytes 221192 | tf_op jit(solution)/shard_map/ppermute | solution.py:209
  66.9 3.6 %collective-permute-start.17 = (bf16[3,96,128]{2,1,0:T(8,128)(2,1)S(1)}, bf16[3,96,128]{2,1,0:T(8,128)(2,1)S(1)}, u32[]{:S(2)}, u32[]{:S(2)}) collective-permute-start(bf16[3,96,128]{2,1,0:T(8,128)(2,1)S(1)} %get-tuple-element.42), channel_id=1, source_target_pairs={{0,24},{4,28},{8,16},{12,20},{16,8},{20,12},{24,0},{28,4},{1,25},{... | collective-permute-start | bytes 221192 | tf_op jit(solution)/shard_map/ppermute | solution.py:209
  70.6 5.8 %collective-permute-done.16.refs_5_ = bf16[3,96,128]{2,1,0:T(8,128)(2,1)S(1)} collective-permute-done((bf16[3,96,128]{2,1,0:T(8,128)(2,1)S(1)}, bf16[3,96,128]{2,1,0:T(8,128)(2,1)S(1)}, u32[]{:S(2)}, u32[]{:S(2)}) %collective-permute-start.16) | collective-permute-done | bytes 73760 | tf_op jit(solution)/shard_map/ppermute | solution.py:209
  79.4 2.7 %collective-permute-start.20 = (bf16[3,96,128]{2,1,0:T(8,128)(2,1)S(1)}, bf16[3,96,128]{2,1,0:T(8,128)(2,1)S(1)}, u32[]{:S(2)}, u32[]{:S(2)}) collective-permute-start(bf16[3,96,128]{2,1,0:T(8,128)(2,1)S(1)} %get-tuple-element.44.refs_0_), channel_id=1, source_target_pairs={{0,8},{4,12},{8,0},{12,4},{16,24},{20,28},{24,16},{28,20},{1,9},{5... | collective-permute-start | bytes 221192 | tf_op jit(solution)/shard_map/ppermute | solution.py:209
  83.1 3.6 %collective-permute-start.22 = (bf16[3,96,128]{2,1,0:T(8,128)(2,1)S(1)}, bf16[3,96,128]{2,1,0:T(8,128)(2,1)S(1)}, u32[]{:S(2)}, u32[]{:S(2)}) collective-permute-start(bf16[3,96,128]{2,1,0:T(8,128)(2,1)S(1)} %get-tuple-element.44.refs_0_), channel_id=1, source_target_pairs={{0,16},{4,20},{8,24},{12,28},{16,0},{20,4},{24,8},{28,12},{1,17},{... | collective-permute-start | bytes 221192 | tf_op jit(solution)/shard_map/ppermute | solution.py:209
  87.5 1.5 %collective-permute-start.24 = (bf16[3,96,128]{2,1,0:T(8,128)(2,1)S(1)}, bf16[3,96,128]{2,1,0:T(8,128)(2,1)S(1)}, u32[]{:S(2)}, u32[]{:S(2)}) collective-permute-start(bf16[3,96,128]{2,1,0:T(8,128)(2,1)S(1)} %get-tuple-element.44.refs_0_), channel_id=1, source_target_pairs={{0,24},{4,28},{8,16},{12,20},{16,8},{20,12},{24,0},{28,4},{1,25},{... | collective-permute-start | bytes 221192 | tf_op jit(solution)/shard_map/ppermute | solution.py:209
  89.1 3.2 %collective-permute-start.25 = (bf16[3,96,128]{2,1,0:T(8,128)(2,1)S(1)}, bf16[3,96,128]{2,1,0:T(8,128)(2,1)S(1)}, u32[]{:S(2)}, u32[]{:S(2)}) collective-permute-start(bf16[3,96,128]{2,1,0:T(8,128)(2,1)S(1)} %get-tuple-element.44.refs_0_), channel_id=1, source_target_pairs={{0,28},{4,24},{8,20},{12,16},{16,12},{20,8},{24,4},{28,0},{1,29},{... | collective-permute-start | bytes 221192 | tf_op jit(solution)/shard_map/ppermute | solution.py:209
  92.4 2.4 %collective-permute-done.22.refs_4_ = bf16[3,96,128]{2,1,0:T(8,128)(2,1)S(1)} collective-permute-done((bf16[3,96,128]{2,1,0:T(8,128)(2,1)S(1)}, bf16[3,96,128]{2,1,0:T(8,128)(2,1)S(1)}, u32[]{:S(2)}, u32[]{:S(2)}) %collective-permute-start.22) | collective-permute-done | bytes 73760 | tf_op jit(solution)/shard_map/ppermute | solution.py:209
  94.8 2.9 %collective-permute-done.23.refs_5_ = bf16[3,96,128]{2,1,0:T(8,128)(2,1)S(1)} collective-permute-done((bf16[3,96,128]{2,1,0:T(8,128)(2,1)S(1)}, bf16[3,96,128]{2,1,0:T(8,128)(2,1)S(1)}, u32[]{:S(2)}, u32[]{:S(2)}) %collective-permute-start.23) | collective-permute-done | bytes 73760 | tf_op jit(solution)/shard_map/ppermute | solution.py:209
  97.7 3.0 %shard_map.118 = bf16[18,96,384]{2,1,0:T(8,128)(2,1)} custom-call(s32[54]{0:T(128)S(1)} %dynamic_slice.41.slot_ref, s32[1]{0:T(128)} %bitcast.1.row_ref, f32[9,96,384]{2,1,0:T(8,128)S(1)} %get-tuple-element.32.own_ref, f32[9,96,384]{2,1,0:T(8,128)S(1)} %collective-permute-done.10.other_ref, bf16[3,96,128]{2,1,0:T(8,128)(2,1)S(1)} %get-tuple-element.44.refs_0_, ...), custom_call_target="tpu_custom_call" | custom-call | tf_op jit(solution)/shard_map/pallas_call | solution.py:337
  (72 shorter events, 13.7 us)
Async XLA Ops:
  2.4 13.8 %collective-permute-start.4 = (bf16[9,16,384]{2,1,0:T(8,128)(2,1)}, bf16[9,16,384]{2,1,0:T(8,128)(2,1)S(1)}, u32[]{:S(2)}, u32[]{:S(2)}) collective-permute-start(bf16[9,16,384]{2,1,0:T(8,128)(2,1)} %get-tuple-element.51), channel_id=1, source_target_pairs={{2,0},{1,3},{6,4},{5,7},{10,8},{9,11},{14,12},{13,15},{18,16},{17,... | collective-permute-start | bytes 331784 | tf_op jit(solution)/shard_map/ppermute | solution.py:260
  5.8 20.1 %collective-permute-start.8 = (bf16[4,96,384]{2,1,0:T(8,128)(2,1)}, bf16[4,96,384]{2,1,0:T(8,128)(2,1)S(1)}, u32[]{:S(2)}, u32[]{:S(2)}) collective-permute-start(bf16[4,96,384]{2,1,0:T(8,128)(2,1)} %get-tuple-element.47), channel_id=1, source_target_pairs={{0,2},{1,3},{2,0},{3,1},{4,6},{5,7},{6,4},{7,5},{8,10},{9,11},{10,... | collective-permute-start | bytes 884744 | tf_op jit(solution)/shard_map/ppermute | solution.py:209
  8.8 17.0 %collective-permute-start.9 = (bf16[4,96,384]{2,1,0:T(8,128)(2,1)}, bf16[4,96,384]{2,1,0:T(8,128)(2,1)S(1)}, u32[]{:S(2)}, u32[]{:S(2)}) collective-permute-start(bf16[4,96,384]{2,1,0:T(8,128)(2,1)} %get-tuple-element.46), channel_id=1, source_target_pairs={{0,3},{1,2},{2,1},{3,0},{4,7},{5,6},{6,5},{7,4},{8,11},{9,10},{10,... | collective-permute-start | bytes 884744 | tf_op jit(solution)/shard_map/ppermute | solution.py:209
  11.3 14.8 %collective-permute-start = (bf16[9,96,384]{2,1,0:T(8,128)(2,1)}, bf16[9,96,384]{2,1,0:T(8,128)(2,1)S(1)}, u32[]{:S(2)}, u32[]{:S(2)}) collective-permute-start(bf16[9,96,384]{2,1,0:T(8,128)(2,1)} %constant_dynamic-slice_fusion.8), channel_id=1, source_target_pairs={{0,1},{1,0},{2,3},{3,2},{4,5},{5,4},{6,7},{7,6},{8,9},{9,8},{10,11... | collective-permute-start | bytes 1990664 | tf_op jit(solution)/shard_map/ppermute | solution.py:209
  12.2 15.4 %collective-permute-start.3 = (bf16[9,96,384]{2,1,0:T(8,128)(2,1)}, bf16[9,96,384]{2,1,0:T(8,128)(2,1)S(1)}, u32[]{:S(2)}, u32[]{:S(2)}) collective-permute-start(bf16[9,96,384]{2,1,0:T(8,128)(2,1)} %constant_dynamic-slice_fusion.5), channel_id=1, source_target_pairs={{0,1},{1,0},{2,3},{3,2},{4,5},{5,4},{6,7},{7,6},{8,9},{9,8},{10,11... | collective-permute-start | bytes 1990664 | tf_op jit(solution)/shard_map/ppermute | solution.py:209
  16.9 21.1 %collective-permute-start.6 = (bf16[3,96,384]{2,1,0:T(8,128)(2,1)S(1)}, bf16[3,96,384]{2,1,0:T(8,128)(2,1)S(1)}, u32[]{:S(2)}, u32[]{:S(2)}) collective-permute-start(bf16[3,96,384]{2,1,0:T(8,128)(2,1)S(1)} %get-tuple-element.49), channel_id=1, source_target_pairs={{1,3},{2,0},{3,1},{0,2},{5,7},{6,4},{7,5},{4,6},{9,11},{10,8},{11,... | collective-permute-start | bytes 663560 | tf_op jit(solution)/shard_map/ppermute | solution.py:209
  25.8 12.2 %collective-permute-start.7 = (bf16[3,96,384]{2,1,0:T(8,128)(2,1)S(1)}, bf16[3,96,384]{2,1,0:T(8,128)(2,1)S(1)}, u32[]{:S(2)}, u32[]{:S(2)}) collective-permute-start(bf16[3,96,384]{2,1,0:T(8,128)(2,1)S(1)} %get-tuple-element.48), channel_id=1, source_target_pairs={{1,2},{2,1},{3,0},{0,3},{5,6},{6,5},{7,4},{4,7},{9,10},{10,9},{11,... | collective-permute-start | bytes 663560 | tf_op jit(solution)/shard_map/ppermute | solution.py:209
  25.8 20.6 %collective-permute-start.1 = (bf16[2,96,384]{2,1,0:T(8,128)(2,1)S(1)}, bf16[2,96,384]{2,1,0:T(8,128)(2,1)S(1)}, u32[]{:S(2)}, u32[]{:S(2)}) collective-permute-start(bf16[2,96,384]{2,1,0:T(8,128)(2,1)S(1)} %get-tuple-element.53), channel_id=1, source_target_pairs={{2,0},{3,1},{0,2},{1,3},{6,4},{7,5},{4,6},{5,7},{10,8},{11,9},{8,1... | collective-permute-start | bytes 442376 | tf_op jit(solution)/shard_map/ppermute | solution.py:209
  26.0 20.4 %collective-permute-start.2 = (bf16[2,96,384]{2,1,0:T(8,128)(2,1)S(1)}, bf16[2,96,384]{2,1,0:T(8,128)(2,1)S(1)}, u32[]{:S(2)}, u32[]{:S(2)}) collective-permute-start(bf16[2,96,384]{2,1,0:T(8,128)(2,1)S(1)} %get-tuple-element.52), channel_id=1, source_target_pairs={{2,1},{3,0},{0,3},{1,2},{6,5},{7,4},{4,7},{5,6},{10,9},{11,8},{8,1... | collective-permute-start | bytes 442376 | tf_op jit(solution)/shard_map/ppermute | solution.py:209
  52.9 44.8 %collective-permute-start.10 = (f32[9,96,384]{2,1,0:T(8,128)}, f32[9,96,384]{2,1,0:T(8,128)S(1)}, u32[]{:S(2)}, u32[]{:S(2)}) collective-permute-start(f32[9,96,384]{2,1,0:T(8,128)} %get-tuple-element.33), channel_id=1, source_target_pairs={{0,1},{1,0},{2,3},{3,2},{4,5},{5,4},{6,7},{7,6},{8,9},{9,8},{10,11... | collective-permute-start | bytes 3981320 | tf_op jit(solution)/shard_map/ppermute | solution.py:209
  56.9 8.7 %collective-permute-start.12 = (bf16[3,96,128]{2,1,0:T(8,128)(2,1)S(1)}, bf16[3,96,128]{2,1,0:T(8,128)(2,1)S(1)}, u32[]{:S(2)}, u32[]{:S(2)}) collective-permute-start(bf16[3,96,128]{2,1,0:T(8,128)(2,1)S(1)} %get-tuple-element.37), channel_id=1, source_target_pairs={{0,4},{4,0},{8,12},{12,8},{16,20},{20,16},{24,28},{28,24},{1,5},{5... | collective-permute-start | bytes 221192 | tf_op jit(solution)/shard_map/ppermute | solution.py:209
  59.1 7.7 %collective-permute-start.13 = (bf16[3,96,128]{2,1,0:T(8,128)(2,1)S(1)}, bf16[3,96,128]{2,1,0:T(8,128)(2,1)S(1)}, u32[]{:S(2)}, u32[]{:S(2)}) collective-permute-start(bf16[3,96,128]{2,1,0:T(8,128)(2,1)S(1)} %get-tuple-element.38), channel_id=1, source_target_pairs={{0,8},{4,12},{8,0},{12,4},{16,24},{20,28},{24,16},{28,20},{1,9},{5... | collective-permute-start | bytes 221192 | tf_op jit(solution)/shard_map/ppermute | solution.py:209
  60.7 9.8 %collective-permute-start.14 = (bf16[3,96,128]{2,1,0:T(8,128)(2,1)S(1)}, bf16[3,96,128]{2,1,0:T(8,128)(2,1)S(1)}, u32[]{:S(2)}, u32[]{:S(2)}) collective-permute-start(bf16[3,96,128]{2,1,0:T(8,128)(2,1)S(1)} %get-tuple-element.39), channel_id=1, source_target_pairs={{0,12},{4,8},{8,4},{12,0},{16,28},{20,24},{24,20},{28,16},{1,13},{... | collective-permute-start | bytes 221192 | tf_op jit(solution)/shard_map/ppermute | solution.py:209
  62.5 8.1 %collective-permute-start.15 = (bf16[3,96,128]{2,1,0:T(8,128)(2,1)S(1)}, bf16[3,96,128]{2,1,0:T(8,128)(2,1)S(1)}, u32[]{:S(2)}, u32[]{:S(2)}) collective-permute-start(bf16[3,96,128]{2,1,0:T(8,128)(2,1)S(1)} %get-tuple-element.40), channel_id=1, source_target_pairs={{0,16},{4,20},{8,24},{12,28},{16,0},{20,4},{24,8},{28,12},{1,17},{... | collective-permute-start | bytes 221192 | tf_op jit(solution)/shard_map/ppermute | solution.py:209
  65.6 10.9 %collective-permute-start.16 = (bf16[3,96,128]{2,1,0:T(8,128)(2,1)S(1)}, bf16[3,96,128]{2,1,0:T(8,128)(2,1)S(1)}, u32[]{:S(2)}, u32[]{:S(2)}) collective-permute-start(bf16[3,96,128]{2,1,0:T(8,128)(2,1)S(1)} %get-tuple-element.41), channel_id=1, source_target_pairs={{0,20},{4,16},{8,28},{12,24},{16,4},{20,0},{24,12},{28,8},{1,21},{... | collective-permute-start | bytes 221192 | tf_op jit(solution)/shard_map/ppermute | solution.py:209
  66.9 9.6 %collective-permute-start.17 = (bf16[3,96,128]{2,1,0:T(8,128)(2,1)S(1)}, bf16[3,96,128]{2,1,0:T(8,128)(2,1)S(1)}, u32[]{:S(2)}, u32[]{:S(2)}) collective-permute-start(bf16[3,96,128]{2,1,0:T(8,128)(2,1)S(1)} %get-tuple-element.42), channel_id=1, source_target_pairs={{0,24},{4,28},{8,16},{12,20},{16,8},{20,12},{24,0},{28,4},{1,25},{... | collective-permute-start | bytes 221192 | tf_op jit(solution)/shard_map/ppermute | solution.py:209
  70.5 7.2 %collective-permute-start.18 = (bf16[3,96,128]{2,1,0:T(8,128)(2,1)S(1)}, bf16[3,96,128]{2,1,0:T(8,128)(2,1)S(1)}, u32[]{:S(2)}, u32[]{:S(2)}) collective-permute-start(bf16[3,96,128]{2,1,0:T(8,128)(2,1)S(1)} %get-tuple-element.43), channel_id=1, source_target_pairs={{0,28},{4,24},{8,20},{12,16},{16,12},{20,8},{24,4},{28,0},{1,29},{... | collective-permute-start | bytes 221192 | tf_op jit(solution)/shard_map/ppermute | solution.py:209
  78.9 7.8 %collective-permute-start.19 = (bf16[3,96,128]{2,1,0:T(8,128)(2,1)S(1)}, bf16[3,96,128]{2,1,0:T(8,128)(2,1)S(1)}, u32[]{:S(2)}, u32[]{:S(2)}) collective-permute-start(bf16[3,96,128]{2,1,0:T(8,128)(2,1)S(1)} %get-tuple-element.44.refs_0_), channel_id=1, source_target_pairs={{0,4},{4,0},{8,12},{12,8},{16,20},{20,16},{24,28},{28,24},{1,5},{5... | collective-permute-start | bytes 221192 | tf_op jit(solution)/shard_map/ppermute | solution.py:209
  79.4 8.1 %collective-permute-start.20 = (bf16[3,96,128]{2,1,0:T(8,128)(2,1)S(1)}, bf16[3,96,128]{2,1,0:T(8,128)(2,1)S(1)}, u32[]{:S(2)}, u32[]{:S(2)}) collective-permute-start(bf16[3,96,128]{2,1,0:T(8,128)(2,1)S(1)} %get-tuple-element.44.refs_0_), channel_id=1, source_target_pairs={{0,8},{4,12},{8,0},{12,4},{16,24},{20,28},{24,16},{28,20},{1,9},{5... | collective-permute-start | bytes 221192 | tf_op jit(solution)/shard_map/ppermute | solution.py:209
  82.1 7.0 %collective-permute-start.21 = (bf16[3,96,128]{2,1,0:T(8,128)(2,1)S(1)}, bf16[3,96,128]{2,1,0:T(8,128)(2,1)S(1)}, u32[]{:S(2)}, u32[]{:S(2)}) collective-permute-start(bf16[3,96,128]{2,1,0:T(8,128)(2,1)S(1)} %get-tuple-element.44.refs_0_), channel_id=1, source_target_pairs={{0,12},{4,8},{8,4},{12,0},{16,28},{20,24},{24,20},{28,16},{1,13},{... | collective-permute-start | bytes 221192 | tf_op jit(solution)/shard_map/ppermute | solution.py:209
  83.1 11.6 %collective-permute-start.22 = (bf16[3,96,128]{2,1,0:T(8,128)(2,1)S(1)}, bf16[3,96,128]{2,1,0:T(8,128)(2,1)S(1)}, u32[]{:S(2)}, u32[]{:S(2)}) collective-permute-start(bf16[3,96,128]{2,1,0:T(8,128)(2,1)S(1)} %get-tuple-element.44.refs_0_), channel_id=1, source_target_pairs={{0,16},{4,20},{8,24},{12,28},{16,0},{20,4},{24,8},{28,12},{1,17},{... | collective-permute-start | bytes 221192 | tf_op jit(solution)/shard_map/ppermute | solution.py:209
  86.7 11.0 %collective-permute-start.23 = (bf16[3,96,128]{2,1,0:T(8,128)(2,1)S(1)}, bf16[3,96,128]{2,1,0:T(8,128)(2,1)S(1)}, u32[]{:S(2)}, u32[]{:S(2)}) collective-permute-start(bf16[3,96,128]{2,1,0:T(8,128)(2,1)S(1)} %get-tuple-element.44.refs_0_), channel_id=1, source_target_pairs={{0,20},{4,16},{8,28},{12,24},{16,4},{20,0},{24,12},{28,8},{1,21},{... | collective-permute-start | bytes 221192 | tf_op jit(solution)/shard_map/ppermute | solution.py:209
  87.5 10.1 %collective-permute-start.24 = (bf16[3,96,128]{2,1,0:T(8,128)(2,1)S(1)}, bf16[3,96,128]{2,1,0:T(8,128)(2,1)S(1)}, u32[]{:S(2)}, u32[]{:S(2)}) collective-permute-start(bf16[3,96,128]{2,1,0:T(8,128)(2,1)S(1)} %get-tuple-element.44.refs_0_), channel_id=1, source_target_pairs={{0,24},{4,28},{8,16},{12,20},{16,8},{20,12},{24,0},{28,4},{1,25},{... | collective-permute-start | bytes 221192 | tf_op jit(solution)/shard_map/ppermute | solution.py:209
  89.1 8.6 %collective-permute-start.25 = (bf16[3,96,128]{2,1,0:T(8,128)(2,1)S(1)}, bf16[3,96,128]{2,1,0:T(8,128)(2,1)S(1)}, u32[]{:S(2)}, u32[]{:S(2)}) collective-permute-start(bf16[3,96,128]{2,1,0:T(8,128)(2,1)S(1)} %get-tuple-element.44.refs_0_), channel_id=1, source_target_pairs={{0,28},{4,24},{8,20},{12,16},{16,12},{20,8},{24,4},{28,0},{1,29},{... | collective-permute-start | bytes 221192 | tf_op jit(solution)/shard_map/ppermute | solution.py:209
  (11 other events, 53.2 us)

commit v3 on v2

v3 whole, which is shorter than its diff:
```python
import functools

import jax
import jax.numpy as jnp
from jax import lax
from jax.experimental import pallas as pl
from jax.experimental.pallas import tpu as pltpu
from jax.sharding import PartitionSpec as P

TILE = 128
ALIGN = 16
CHUNKS = (4, 3, 2)
BLOCK = 48
DEPTH = 256
MIB = 1024 * 1024
VMEM = 44 * MIB
F32 = jnp.float32
BF16 = jnp.bfloat16


def pack_kernel(row_ref, *refs, chunks, siblings, edges):
    count = 2 * len(chunks) + 2 * siblings + edges
    sems = refs[-1]
    outs, held = refs[-1 - 2 * count : -1 - count], refs[-1 - count : -1]
    pixels_ref, rows_ref = refs[:2]
    half = pixels_ref.shape[0] // 2
    row = row_ref[0]
    core = row & 1
    pieces = []
    if siblings:
        other = pl.ds((1 - core) * half, half)
        pieces += [rows_ref.at[other], pixels_ref.at[other]]
    for s, n in chunks:
        for which in range(2):
            pieces.append(pixels_ref.at[pl.ds((core ^ which) * half + s, n)])
    fetches = [
        pltpu.make_async_copy(piece, kept, sems.at[0, i])
        for i, (piece, kept) in enumerate(zip(pieces, held))
    ]
    stores = [
        pltpu.make_async_copy(kept, out, sems.at[1, i])
        for i, (kept, out) in enumerate(zip(held, outs))
    ]
    if edges:
        pad = outs[-1].shape[1]
        first = jnp.where(row < 2, rows_ref.shape[1] - pad, 0)
        near = pl.ds(pl.multiple_of(first, ALIGN), pad)
        holds = core == (row < 2).astype(jnp.int32)
        own = rows_ref.at[pl.ds(core * half, half), near]
        edge = pltpu.make_async_copy(own, held[-1], sems.at[0, count - 1])
        passed = pltpu.make_async_copy(refs[2].at[:, near], held[-1], sems.at[0, count - 1])
        pl.when(holds)(edge.start)
        pl.when(jnp.logical_not(holds))(passed.start)
        fetches.append(edge)
    for fetch in fetches[: len(pieces)]:
        fetch.start()
    for fetch, store in zip(fetches, stores):
        fetch.wait()
        store.start()
    for store in stores:
        store.wait()


def pack(row, pixels, rows, chunks, pad, siblings=False, sibling_rows=None, after=()):
    images, band, side = pixels.shape
    half = images // 2
    shapes = [(half, band, side)] * 2 if siblings else []
    shapes += [(n, band, side) for _, n in chunks for _ in range(2)]
    arrays = [pltpu.with_memory_space_constraint(a, pltpu.HBM) for a in (pixels, rows)]
    if sibling_rows is not None:
        shapes.append((half, pad, side))
        arrays.append(sibling_rows)
    arrays += after
    anywhere = pl.BlockSpec(memory_space=pl.ANY)
    return pl.pallas_call(
        functools.partial(
            pack_kernel, chunks=chunks, siblings=siblings, edges=sibling_rows is not None
        ),
        in_specs=[pl.BlockSpec(memory_space=pltpu.SMEM)] + [anywhere] * len(arrays),
        out_specs=[anywhere] * len(shapes),
        out_shape=[jax.ShapeDtypeStruct(shape, BF16) for shape in shapes],
        scratch_shapes=[pltpu.VMEM(shape, BF16) for shape in shapes]
        + [pltpu.SemaphoreType.DMA((2, len(shapes)))],
        compiler_params=pltpu.CompilerParams(vmem_limit_bytes=VMEM),
    )(row, *arrays)


def target_kernel(
    place_ref, patch_ref, block_ref, level_ref, table_ref, home_ref, _, slots_ref, own_ref, weights_ref, denom_ref, *, tiles
):
    mine, core = place_ref[0], place_ref[1] & 1
    visits, detectors = level_ref.shape
    pieces = slots_ref.shape[0]
    half = weights_ref.shape[0]
    first = mine * (half * 2)

    def slot_of(n):
        return (home_ref[patch_ref[n]] ^ mine) * tiles + block_ref[n]

    def place(i, _):
        slots_ref[i] = slot_of(mine * pieces + i)
        return 0

    def place_own(i, _):
        own_ref[i] = slots_ref[core * half * tiles + i]
        return 0

    def weigh(i, _):
        image = first + core * half + i
        weights_ref[i] = table_ref[level_ref[image % visits, image // visits]]
        return 0

    def add(d, sums):
        for v in range(visits):
            weight = table_ref[level_ref[v, d]]
            for q in range(tiles):
                slot = slot_of((d * visits + v) * tiles + q)
                sums = tuple(
                    total + jnp.where(slot == t, weight, 0.0) for t, total in enumerate(sums)
                )
        return sums

    lax.fori_loop(0, pieces, place, 0)
    lax.fori_loop(0, half * tiles, place_own, 0)
    lax.fori_loop(0, half, weigh, 0)
    sums = lax.fori_loop(0, detectors, add, (jnp.float32(0),) * tiles)
    for t in range(tiles):
        denom_ref[t] = sums[t]


def match_kernel(slot_ref, weight_ref, row_ref, *refs, start, taps, first, last):
    shard_refs = refs[:4]
    rows_refs = refs[4:6]
    edge_ref, cols_ref, profile_ref = refs[6:9]
    refs = refs[9:]
    if not first:
        carried = refs[2:4]
        refs = refs[4:]
    matched_refs, sums_refs = refs[:2], refs[2:4]
    refs = refs[4:]
    count, band, side = rows_refs[0].shape
    group = [refs[g : 4 * count : count] for g in range(count)]
    numers = (sums_refs[0], refs[4 * count]) if last else sums_refs
    pad = edge_ref.shape[1]
    span = BLOCK + 2 * pad
    reach = (taps - 1) // 2
    inner = DEPTH // span
    outer = -(-taps // inner)
    tiles = side // TILE
    width = side + TILE
    blocks = band // BLOCK
    row = row_ref[0]
    core = row & 1

    for m in range(2):
        numers[m][...] = jnp.zeros_like(numers[m]) if first else carried[m][...]
    for g in range(count):
        image, extended, stack, table = group[g]
        for mask, shard in enumerate(shard_refs):
            at = pl.multiple_of((row ^ mask) * band, band)
            image[pl.ds(at, band), :] = shard[g]
        edge = edge_ref[g]
        blank = jnp.zeros_like(edge)
        extended[0:pad, :] = jnp.where(row >= 2, edge, blank)
        extended[pad + 2 * band :, :] = jnp.where(row >= 2, blank, edge)
        for m, rows in enumerate(rows_refs):
            at = pl.multiple_of(pad + (core ^ m) * band, ALIGN)
            extended[pl.ds(at, band), :] = rows[g]
        by_rows = jnp.dot(extended[...], image[...], preferred_element_type=F32).astype(BF16)
        warped = jnp.dot(by_rows, cols_ref[g], preferred_element_type=F32).astype(BF16)
        ring = jnp.concatenate([warped, jnp.zeros((warped.shape[0], TILE), BF16)], axis=1)
        for b in range(inner):
            turn = (inner // 2 - b) % width
            shifted = pltpu.roll(ring, turn, 1) if turn else ring
            for k in range(2 * blocks):
                stack[k, span * b : span * (b + 1), :] = shifted[BLOCK * k : BLOCK * k + span]
        for k in range(2 * blocks):
            stack[k, span * inner :, :] = jnp.zeros((DEPTH - span * inner, width), BF16)
        profiles = None
        for b in range(inner):
            part = profile_ref[g, pl.ds(b, outer, stride=inner), :]
            part = jnp.concatenate([part, jnp.zeros((outer, DEPTH - TILE), F32)], axis=1)
            part = pltpu.roll(part, span * b, 1) if b else part
            profiles = part if profiles is None else profiles + part
        for a in range(outer):
            profile = jnp.broadcast_to(profiles[a : a + 1, :], (BLOCK, DEPTH))
            toeplitz = pltpu.roll(profile, 0, 1, stride=1, stride_axis=0)
            table[BLOCK * a : BLOCK * (a + 1), :] = toeplitz.astype(BF16)
    middle = outer // 2
    origin = inner * middle + inner // 2 - reach
    for g in range(count):
        _, _, stack, table = group[g]
        index = start + g
        weight = weight_ref[index]
        for m in range(2):
            for k in range(blocks):
                partial = jnp.dot(
                    table[...], stack[(core ^ m) * blocks + k], preferred_element_type=F32
                )
                total = None
                for a in range(outer):
                    turn = (inner * (middle - a) - origin) % width
                    part = partial[BLOCK * a : BLOCK * (a + 1)]
                    part = pltpu.roll(part, turn, 1) if turn else part
                    total = part if total is None else total + part
                matched = total[:, 0:side]
                here = slice(BLOCK * k, BLOCK * (k + 1))
                matched_refs[m][g, here, :] = matched
                for q in range(tiles):
                    slot = slot_ref[index * tiles + q]
                    piece = (weight * matched[:, TILE * q : TILE * (q + 1)]).astype(BF16)
                    numers[m][slot, here, :] += piece.astype(F32)
    if last:
        sums_refs[1][...] = numers[1][...].astype(BF16)


def match_chunk(slots, weights, row, operands, carry, start, count, taps, slot_count, last):
    pixels, rows, edge = operands[0], operands[4], operands[6]
    images, band, side = pixels.shape
    half = images // 2
    pad = edge.shape[1]
    inner = DEPTH // (BLOCK + 2 * pad)
    outer = -(-taps // inner)
    width = side + TILE
    first = carry is None

    def block(array):
        if array.shape[0] == images:
            place = lambda i, slot, weight, row: ((row[0] & 1) * half + start, 0, 0)
        elif array.shape[0] == half:
            place = lambda i, *_: (start, 0, 0)
        else:
            place = lambda i, *_: (0, 0, 0)
        return pl.BlockSpec(tuple(pl.Element(n) for n in (count,) + array.shape[1:]), place)

    whole = lambda shape: pl.BlockSpec(shape, lambda i, *_: (0,) * len(shape))
    in_specs = [block(a) for a in operands]
    arrays = [
        pltpu.with_memory_space_constraint(a, pltpu.HBM) if a.shape[0] == images else a
        for a in operands
    ]
    aliases = {}
    numer_shape = (slot_count, band, TILE)
    matched_shape = jax.ShapeDtypeStruct((half, band, side), F32)
    if not first:
        aliases = {3 + len(arrays): 0, 4 + len(arrays): 1}
        arrays += list(carry)
        in_specs += [pl.BlockSpec(memory_space=pl.ANY)] * 2 + [whole(numer_shape)] * 2
    out_shape = [matched_shape] * 2 + [
        jax.ShapeDtypeStruct(numer_shape, F32),
        jax.ShapeDtypeStruct(numer_shape, BF16 if last else F32),
    ]
    out_specs = [block(matched_shape)] * 2 + [whole(numer_shape)] * 2
    scratch = [pltpu.VMEM((side, side), BF16)] * count
    scratch += [pltpu.VMEM((2 * band + 2 * pad, side), BF16)] * count
    scratch += [pltpu.VMEM((2 * band // BLOCK, DEPTH, width), BF16)] * count
    scratch += [pltpu.VMEM((outer * BLOCK, DEPTH), BF16)] * count
    if last:
        scratch.append(pltpu.VMEM(numer_shape, F32))
    return pl.pallas_call(
        functools.partial(match_kernel, start=start, taps=taps, first=first, last=last),
        grid_spec=pltpu.PrefetchScalarGridSpec(
            num_scalar_prefetch=3,
            grid=(1,),
            in_specs=in_specs,
            out_specs=out_specs,
            scratch_shapes=scratch,
        ),
        out_shape=out_shape,
        input_output_aliases=aliases,
        compiler_params=pltpu.CompilerParams(
            vmem_limit_bytes=min(60 * MIB, max(VMEM, 20 * MIB + 16 * slot_count * band * TILE))
        ),
        cost_estimate=pl.CostEstimate(
            flops=count * 2000000000, bytes_accessed=count * 1000000, transcendentals=0
        ),
    )(slots, weights, row, *arrays)


def merge_kernel(own_ref, other_ref, *part_refs):
    each = part_refs[0].shape[0]
    for m, part in enumerate(part_refs):
        boxes = slice(each * m, each * (m + 1))
        part[...] = (own_ref[boxes] + other_ref[boxes].astype(F32)).astype(BF16)


def template_kernel(denom_ref, _, *refs):
    part_refs, template_ref, coadd_ref = refs[:-3], refs[-3], refs[-2]
    for q in range(template_ref.shape[0]):
        total = part_refs[0][q].astype(F32)
        for part in part_refs[1:]:
            total = total + part[q].astype(F32)
        box = (total / jnp.maximum(denom_ref[q], 1.0)).astype(BF16)
        template_ref[q] = box
        coadd_ref[:, TILE * q : TILE * (q + 1)] = box


def difference_kernel(slot_ref, row_ref, own_ref, other_ref, *refs, masks):
    template_refs, out_ref, held = refs[:-2], refs[-2], refs[-1]
    step = pl.program_id(0)
    each = template_refs[0].shape[0]
    count, _, side = own_ref.shape
    tiles = side // TILE

    @pl.when(step == 0)
    def _():
        for m, template in zip(masks, template_refs):
            held[each * m : each * (m + 1)] = template[...]

    def subtract(matched_ref):
        for i in range(count):
            for q in range(tiles):
                slot = slot_ref[(step * count + i) * tiles + q]
                columns = slice(TILE * q, TILE * (q + 1))
                box = held[slot].astype(F32)
                out_ref[i, :, columns] = (matched_ref[i, :, columns] - box).astype(BF16)

    mine = (step * 2 // pl.num_programs(0)) == (row_ref[0] & 1)
    pl.when(mine)(lambda: subtract(own_ref))
    pl.when(jnp.logical_not(mine))(lambda: subtract(other_ref))


def exchange(value, axis, mask):
    size = lax.axis_size(axis)
    return lax.ppermute(value, axis, [(i, i ^ mask) for i in range(size)])


def per_device(
    images,
    warp_rows,
    warp_cols,
    psf_coef,
    taps,
    dest_patch,
    dest_block,
    weight_index,
    weight_table,
    patch_home,
):
    det_count, visit_count, band, side = images.shape
    kernel_count, tap_count = taps.shape
    reach = (tap_count - 1) // 2
    pad = -(-reach // ALIGN) * ALIGN
    span = BLOCK + 2 * pad
    tiles = side // TILE
    det_devices = lax.axis_size("det")
    mine = lax.axis_index("det")
    row = lax.axis_index("row").astype(jnp.int32)
    core = row & 1
    image_count = det_count * visit_count
    half = image_count // 2
    assert lax.axis_size("row") == 4 and image_count == 2 * half
    pixels = images.reshape(image_count, band, side)
    rows = warp_rows.reshape(image_count, band, side)
    cols = warp_cols.reshape(image_count, side, side)
    row_one = row.reshape(1)

    chunks = CHUNKS if sum(CHUNKS) == half else (1,) * half
    starts = [sum(chunks[:c]) for c in range(len(chunks))]
    spans = list(zip(starts, chunks))
    far, cross = [], []

    def send(packed):
        for first, second in zip(packed[::2], packed[1::2]):
            far.append(exchange(first, "row", 2))
            cross.append(exchange(second, "row", 3))

    packed = pack(row_one, pixels, rows, spans[:1], pad, siblings=True)
    sibling_rows = exchange(packed[0], "row", 1)
    sibling = exchange(packed[1], "row", 1)
    send(packed[2:])
    packed = pack(row_one, pixels, rows, spans[1:2], pad, sibling_rows=sibling_rows)
    edge = exchange(packed[-1], "row", 2)
    send(packed[:-1])
    for c in range(2, len(chunks)):
        send(pack(row_one, pixels, rows, spans[c : c + 1], pad, after=[far[c - 2]]))

    with jax.named_scope("profiles"):
        scaled = (psf_coef.reshape(image_count, kernel_count)[:, :, None] * taps).astype(BF16)
        profiles = jnp.einsum(
            "nkt,ku->nut", scaled, taps.astype(BF16), preferred_element_type=F32
        )
        inner = DEPTH // span
        rows_kept = -(-tap_count // inner) * inner
        profiles = jnp.pad(
            profiles,
            (
                (0, 0),
                (0, rows_kept - tap_count + -rows_kept % 8),
                (pad - reach, TILE - tap_count - pad + reach),
            ),
        )
    slots, own_slots, weights, denom = pl.pallas_call(
        functools.partial(target_kernel, tiles=tiles),
        in_specs=[pl.BlockSpec(memory_space=pltpu.SMEM)] * 6
        + [pl.BlockSpec(memory_space=pl.ANY)],
        out_specs=[pl.BlockSpec(memory_space=pltpu.SMEM)] * 4,
        out_shape=[
            jax.ShapeDtypeStruct((image_count * tiles,), jnp.int32),
            jax.ShapeDtypeStruct((half * tiles,), jnp.int32),
            jax.ShapeDtypeStruct((half,), F32),
            jax.ShapeDtypeStruct((tiles,), F32),
        ],
    )(
        jnp.stack([mine.astype(jnp.int32), row]),
        dest_patch.reshape(-1),
        dest_block,
        weight_index.T,
        weight_table,
        patch_home,
        packed[-1],
    )

    carry = None
    slot_count = det_devices * tiles
    for c, (s, n) in enumerate(zip(starts, chunks)):
        operands = (
            pixels, sibling, far[c], cross[c], rows, sibling_rows, edge, cols, profiles,
        )
        carry = match_chunk(
            own_slots, weights, row_one, operands, carry, s, n, tap_count, slot_count,
            c == len(chunks) - 1,
        )
    matched, matched_sent, own_sums, sums_sent = carry
    other_sums = exchange(sums_sent, "row", 1)
    box_shape = (tiles, band, TILE)
    box = jax.ShapeDtypeStruct(box_shape, BF16)
    in_vmem = pl.BlockSpec(memory_space=pltpu.VMEM)
    small = pltpu.CompilerParams(vmem_limit_bytes=4 * MIB + 16 * slot_count * band * TILE)
    parts = pl.pallas_call(
        merge_kernel,
        in_specs=[in_vmem] * 2,
        out_specs=[in_vmem] * det_devices,
        out_shape=[box] * det_devices,
        compiler_params=small,
    )(own_sums, other_sums)
    masks = tuple(range(det_devices - 1, 0, -1)) + (0,)
    received = [exchange(parts[m], "det", m) if m else parts[m] for m in masks]
    anywhere = pl.BlockSpec(memory_space=pl.ANY)
    template, coadd, matched_sent = pl.pallas_call(
        template_kernel,
        in_specs=[pl.BlockSpec(memory_space=pltpu.SMEM), anywhere] + [in_vmem] * det_devices,
        out_specs=[in_vmem] * 2 + [anywhere],
        out_shape=[
            box,
            jax.ShapeDtypeStruct((band, side), BF16),
            jax.ShapeDtypeStruct(matched_sent.shape, F32),
        ],
        input_output_aliases={1: 2},
        compiler_params=small,
    )(denom, matched_sent, *received)
    other_matched = exchange(matched_sent, "row", 1)
    templates = [exchange(template, "det", m) if m else template for m in masks]
    group = 3 if half % 3 == 0 else 1
    steps = half // group

    def half_block(which):
        def place(i, slot, row):
            return (jnp.clip(i - ((row[0] & 1) ^ which) * steps, 0, steps - 1), 0, 0)

        return pl.BlockSpec((group, band, side), place)

    difference = pl.pallas_call(
        functools.partial(difference_kernel, masks=masks),
        grid_spec=pltpu.PrefetchScalarGridSpec(
            num_scalar_prefetch=2,
            grid=(2 * steps,),
            in_specs=[half_block(0), half_block(1)]
            + [pl.BlockSpec(box_shape, lambda i, *_: (0, 0, 0))] * det_devices,
            out_specs=pl.BlockSpec((group, band, side), lambda i, *_: (i, 0, 0)),
            scratch_shapes=[pltpu.VMEM((slot_count, band, TILE), BF16)],
        ),
        out_shape=jax.ShapeDtypeStruct((image_count, band, side), BF16),
        compiler_params=small,
    )(slots, row_one, matched, other_matched, *templates)
    return difference.reshape(images.shape), coadd.reshape(1, band, side)


def solution(mesh):
    placed = (
        P("det", None, "row", None),
        P("det", None, "row", None),
        P("det", None, None, None),
        P("det", None, None),
        P(),
        P(),
        P(),
        P(),
        P(),
        P(),
    )
    return jax.shard_map(
        per_device,
        mesh=mesh,
        in_specs=placed,
        out_specs=(P("det", None, "row", None), P("det", "row", None)),
        check_vma=False,
    )
```

time: 101 us -> 90.5 us (0.90)
  starting transfers between devices: 43.6 us -> 33.7 us
  local copies, waits for them, and re-layouts: 9.69 us -> 2.13 us
  waiting for transfers between devices: 15.7 us -> 21.9 us
    pallas_call x1 -> x5, Pallas kernels: 2.95 us -> 13.2 us  [the longest x3 5.34 us: pack(): pl.pallas_call(functools.partial(pack_kernel, chunks=chunks, siblings=sib...]
    ppermute x26 -> x25, starting transfers between devices: 43.6 us -> 33.7 us  [exchange(): return lax.ppermute(value, axis, [(i, i ^ mask) for i in range(size)])]
    pallas_call x3, Pallas kernels: 25.2 us -> 15.7 us  [match_chunk(): pl.pallas_call(functools.partial(match_kernel, start=start, taps=taps, fi...]
    ppermute x26 -> x25, waiting for transfers between devices: 15.7 us -> 21.9 us  [exchange(): return lax.ppermute(value, axis, [(i, i ^ mask) for i in range(size)])]
    dynamic_slice x9 -> x0, local copies, waits for them, and re-layouts: 5.87 us -> none  [the longest x5 3.92 us: portion(): lax.dynamic_slice_in_dim(array, (core ^ which) * half + first, count, 0)]
    broadcast_in_dim x2 -> x0, local copies, waits for them, and re-layouts: 1.8 us -> none  [the longest x1 1.09 us: per_device(): denom = jnp.sum(jnp.where(own, piece_weight[:, None], 0.0), axis=0)]
    unnamed x18 -> x14, local copies, waits for them, and re-layouts: 0.04 us -> 1.3 us
  transfers between devices with their start and end apart: 26 -> 25, of which waited for: 5 -> 8; matrix products, arithmetic and copies ran while one was open for 9% -> 2% of each run, Pallas kernels for 20% -> 22%
where the time goes in v3:
time: 90.5 us; the launch traced here: 89.7 us
  starting transfers between devices  33.7 us (37%)
  Pallas kernels  30.3 us (33%)
  waiting for transfers between devices  21.9 us (24%)
  local copies, waits for them, and re-layouts  2.13 us (2%)
    ppermute x25, starting transfers between devices, exchange(): return lax.ppermute(value, axis, [(i, i ^ mask) for i in range(size)])  33.7 us
    ppermute x25, waiting for transfers between devices, exchange(): return lax.ppermute(value, axis, [(i, i ^ mask) for i in range(size)])  21.9 us
    pallas_call x3, Pallas kernels, match_chunk(): pl.pallas_call(functools.partial(match_kernel, start=start, taps=taps, fi...  15.7 us
    pallas_call x3, Pallas kernels, pack(): pl.pallas_call(functools.partial(pack_kernel, chunks=chunks, siblings=sib...  5.34 us
    pallas_call x1, Pallas kernels, per_device(): pl.pallas_call(functools.partial(target_kernel, tiles=tiles), in_specs=[p...  4.88 us
    pallas_call x1, Pallas kernels, per_device(): pl.pallas_call(functools.partial(difference_kernel, masks=masks), grid_sp...  2.95 us
  transfers between devices with their start and end apart: 25, of which 8 were waited for; matrix products, arithmetic and copies ran while one was open for 2% of the time, Pallas kernels for 22%

profile of v3, /device:TPU:0, one launch (start us, length us, event | category | flops | bytes accessed | tf_op | source)
XLA Modules:
  0.0 89.7 jit_solution(16372637742012606463)
XLA Ops:
  0.7 2.4 %shard_map.113 = (bf16[9,96,384]{2,1,0:T(8,128)(2,1)S(1)}, bf16[9,96,384]{2,1,0:T(8,128)(2,1)S(1)}, bf16[4,96,384]{2,1,0:T(8,128)(2,1)S(1)}, bf16[4,96,384]{2,1,0:T(8,128)(2,1)}) custom-call(s32[1]{0:T(128)} %bitcast.1.row_ref, bf16[18,96,384]{2,1,0:T(8,128)(2,1)} %bitcast.14, bf16[18,96,384]{2,1,0:T(8,128)(2,1)} %bitcast.20), custom_call_target="tpu_custom_call" | custom-call | tf_op jit(solution)/shard_map/pallas_call | solution.py:75
  3.6 2.9 %collective-permute-start.2 = (bf16[4,96,384]{2,1,0:T(8,128)(2,1)S(1)}, bf16[4,96,384]{2,1,0:T(8,128)(2,1)S(1)}, u32[]{:S(2)}, u32[]{:S(2)}) collective-permute-start(bf16[4,96,384]{2,1,0:T(8,128)(2,1)S(1)} %get-tuple-element.44), channel_id=1, source_target_pairs={{0,2},{1,3},{2,0},{3,1},{4,6},{5,7},{6,4},{7,5},{8,10},{9,11},{10,... | collective-permute-start | bytes 884744 | tf_op jit(solution)/shard_map/ppermute | solution.py:325
  7.7 1.7 %shard_map.114 = (bf16[3,96,384]{2,1,0:T(8,128)(2,1)S(1)}, bf16[3,96,384]{2,1,0:T(8,128)(2,1)S(1)}, bf16[9,16,384]{2,1,0:T(8,128)(2,1)S(1)}) custom-call(s32[1]{0:T(128)} %bitcast.1.row_ref, bf16[18,96,384]{2,1,0:T(8,128)(2,1)} %bitcast.15, bf16[18,96,384]{2,1,0:T(8,128)(2,1)} %bitcast.21, bf16[9,96,384]{2,1,0:T(8,128)(2,1)S(1)} %collective-permute-done.refs_2_.refs_5_), custom_call_target="tpu_custom_call" | custom-call | tf_op jit(solution)/shard_map/pallas_call | solution.py:75
  9.4 1.5 %collective-permute-start.5 = (bf16[9,16,384]{2,1,0:T(8,128)(2,1)S(1)}, bf16[9,16,384]{2,1,0:T(8,128)(2,1)S(1)}, u32[]{:S(2)}, u32[]{:S(2)}) collective-permute-start(bf16[9,16,384]{2,1,0:T(8,128)(2,1)S(1)} %get-tuple-element.39._), channel_id=1, source_target_pairs={{0,2},{1,3},{2,0},{3,1},{4,6},{5,7},{6,4},{7,5},{8,10},{9,11},{10,... | collective-permute-start | bytes 331784 | tf_op jit(solution)/shard_map/ppermute | solution.py:325
  11.5 2.9 %collective-permute-done.2.refs_2_ = bf16[4,96,384]{2,1,0:T(8,128)(2,1)S(1)} collective-permute-done((bf16[4,96,384]{2,1,0:T(8,128)(2,1)S(1)}, bf16[4,96,384]{2,1,0:T(8,128)(2,1)S(1)}, u32[]{:S(2)}, u32[]{:S(2)}) %collective-permute-start.2) | collective-permute-done | bytes 294944 | tf_op jit(solution)/shard_map/ppermute | solution.py:325
  15.7 2.1 %collective-permute-start.3 = (bf16[2,96,384]{2,1,0:T(8,128)(2,1)S(1)}, bf16[2,96,384]{2,1,0:T(8,128)(2,1)S(1)}, u32[]{:S(2)}, u32[]{:S(2)}) collective-permute-start(bf16[2,96,384]{2,1,0:T(8,128)(2,1)S(1)} %get-tuple-element.45), channel_id=1, source_target_pairs={{0,2},{1,3},{2,0},{3,1},{4,6},{5,7},{6,4},{7,5},{8,10},{9,11},{10,... | collective-permute-start | bytes 442376 | tf_op jit(solution)/shard_map/ppermute | solution.py:325
  17.8 4.9 %shard_map.115 = (s32[54]{0:T(128)}, s32[27]{0:T(128)}, f32[9]{0:T(128)}, f32[3]{0:T(128)}) custom-call(s32[2]{0:T(128)} %pad_add_fusion.place_ref, s32[432]{0:T(512)} %bitcast.30, s32[432]{0:T(512)} %block_ref.1, s32[3,48]{1,0:T(4,128)} %bitcast.31, f32[8]{0:T(128)} %table_ref.1, s32[8]{0:T(128)} %home_ref.1, bf16[9,16,384]{2,1,0:T(8,128)(2,1)} %copy-done), custom_call_target="tpu_custom_call" | custom-call | tf_op jit(solution)/shard_map/pallas_call | solution.py:393
  22.9 1.7 %collective-permute-start.7 = (bf16[3,96,384]{2,1,0:T(8,128)(2,1)S(1)}, bf16[3,96,384]{2,1,0:T(8,128)(2,1)S(1)}, u32[]{:S(2)}, u32[]{:S(2)}) collective-permute-start(bf16[3,96,384]{2,1,0:T(8,128)(2,1)S(1)} %get-tuple-element.48), channel_id=1, source_target_pairs={{0,3},{1,2},{2,1},{3,0},{4,7},{5,6},{6,5},{7,4},{8,11},{9,10},{10,... | collective-permute-start | bytes 663560 | tf_op jit(solution)/shard_map/ppermute | solution.py:325
  25.9 6.3 %shard_map.117 = (f32[9,96,384]{2,1,0:T(8,128)S(1)}, f32[9,96,384]{2,1,0:T(8,128)S(1)}, f32[24,96,128]{2,1,0:T(8,128)S(1)}, f32[24,96,128]{2,1,0:T(8,128)S(1)}) custom-call(s32[27]{0:T(128)S(1)} %copy-done.3, f32[9]{0:T(128)S(1)} %copy-done.4, s32[1]{0:T(128)} %bitcast.1.row_ref, bf16[18,96,384]{2,1,0:T(8,128)(2,1)} %bitcast.17, ...), custom_call_target="tpu_custom_call" | custom-call | flops 8000000000 | bytes 4000000 | tf_op jit(solution)/shard_map/pallas_call | solution.py:260
  32.2 1.9 %collective-permute-done.6.refs_2_ = bf16[3,96,384]{2,1,0:T(8,128)(2,1)S(1)} collective-permute-done((bf16[3,96,384]{2,1,0:T(8,128)(2,1)S(1)}, bf16[3,96,384]{2,1,0:T(8,128)(2,1)S(1)}, u32[]{:S(2)}, u32[]{:S(2)}) %collective-permute-start.6) | collective-permute-done | bytes 221216 | tf_op jit(solution)/shard_map/ppermute | solution.py:325
  34.1 3.6 %collective-permute-done.7.refs_3_ = bf16[3,96,384]{2,1,0:T(8,128)(2,1)S(1)} collective-permute-done((bf16[3,96,384]{2,1,0:T(8,128)(2,1)S(1)}, bf16[3,96,384]{2,1,0:T(8,128)(2,1)S(1)}, u32[]{:S(2)}, u32[]{:S(2)}) %collective-permute-start.7) | collective-permute-done | bytes 221216 | tf_op jit(solution)/shard_map/ppermute | solution.py:325
  37.8 5.2 %shard_map.118 = (f32[9,96,384]{2,1,0:T(8,128)S(1)}, f32[9,96,384]{2,1,0:T(8,128)S(1)}, f32[24,96,128]{2,1,0:T(8,128)S(1)}, f32[24,96,128]{2,1,0:T(8,128)S(1)}) custom-call(s32[27]{0:T(128)S(1)} %copy-done.3, f32[9]{0:T(128)S(1)} %copy-done.4, s32[1]{0:T(128)} %bitcast.1.row_ref, ...), custom_call_target="tpu_custom_call", output_to_operand_aliasing={{0}: (12, {}), {1}: (13, {})} | custom-call | flops 6000000000 | bytes 3000000 | tf_op jit(solution)/shard_map/pallas_call | solution.py:260
  43.0 4.2 %shard_map.119 = (f32[9,96,384]{2,1,0:T(8,128)S(1)}, f32[9,96,384]{2,1,0:T(8,128)S(1)}, f32[24,96,128]{2,1,0:T(8,128)S(1)}, bf16[24,96,128]{2,1,0:T(8,128)(2,1)S(1)}) custom-call(s32[27]{0:T(128)S(1)} %copy-done.3, f32[9]{0:T(128)S(1)} %copy-done.4, s32[1]{0:T(128)} %bitcast.1.row_ref, ...), custom_call_target="tpu_custom_call", output_to_operand_aliasing={{0}: (12, {}), {1}: (13, {})} | custom-call | flops 4000000000 | bytes 2000000 | tf_op jit(solution)/shard_map/pallas_call | solution.py:260
  47.7 1.6 %collective-permute-done.9.other_ref = bf16[24,96,128]{2,1,0:T(8,128)(2,1)S(1)} collective-permute-done((bf16[24,96,128]{2,1,0:T(8,128)(2,1)S(1)}, bf16[24,96,128]{2,1,0:T(8,128)(2,1)S(1)}, u32[]{:S(2)}, u32[]{:S(2)}) %collective-permute-start.9) | collective-permute-done | bytes 589856 | tf_op jit(solution)/shard_map/ppermute | solution.py:325
  49.5 4.8 %collective-permute-start.10 = (bf16[3,96,128]{2,1,0:T(8,128)(2,1)S(1)}, bf16[3,96,128]{2,1,0:T(8,128)(2,1)S(1)}, u32[]{:S(2)}, u32[]{:S(2)}) collective-permute-start(bf16[3,96,128]{2,1,0:T(8,128)(2,1)S(1)} %get-tuple-element.63), channel_id=1, source_target_pairs={{0,28},{4,24},{8,20},{12,16},{16,12},{20,8},{24,4},{28,0},{1,29},{... | collective-permute-start | bytes 221192 | tf_op jit(solution)/shard_map/ppermute | solution.py:325
  55.3 2.0 %collective-permute-start.13 = (bf16[3,96,128]{2,1,0:T(8,128)(2,1)S(1)}, bf16[3,96,128]{2,1,0:T(8,128)(2,1)S(1)}, u32[]{:S(2)}, u32[]{:S(2)}) collective-permute-start(bf16[3,96,128]{2,1,0:T(8,128)(2,1)S(1)} %get-tuple-element.66), channel_id=1, source_target_pairs={{0,16},{4,20},{8,24},{12,28},{16,0},{20,4},{24,8},{28,12},{1,17},{... | collective-permute-start | bytes 221192 | tf_op jit(solution)/shard_map/ppermute | solution.py:325
  57.3 2.3 %collective-permute-start.14 = (bf16[3,96,128]{2,1,0:T(8,128)(2,1)S(1)}, bf16[3,96,128]{2,1,0:T(8,128)(2,1)S(1)}, u32[]{:S(2)}, u32[]{:S(2)}) collective-permute-start(bf16[3,96,128]{2,1,0:T(8,128)(2,1)S(1)} %get-tuple-element.67), channel_id=1, source_target_pairs={{0,12},{4,8},{8,4},{12,0},{16,28},{20,24},{24,20},{28,16},{1,13},{... | collective-permute-start | bytes 221192 | tf_op jit(solution)/shard_map/ppermute | solution.py:325
  61.9 4.4 %collective-permute-done.12.refs_2_ = bf16[3,96,128]{2,1,0:T(8,128)(2,1)S(1)} collective-permute-done((bf16[3,96,128]{2,1,0:T(8,128)(2,1)S(1)}, bf16[3,96,128]{2,1,0:T(8,128)(2,1)S(1)}, u32[]{:S(2)}, u32[]{:S(2)}) %collective-permute-start.12) | collective-permute-done | bytes 73760 | tf_op jit(solution)/shard_map/ppermute | solution.py:325
  69.1 1.8 %collective-permute-start.23 = (bf16[3,96,128]{2,1,0:T(8,128)(2,1)S(1)}, bf16[3,96,128]{2,1,0:T(8,128)(2,1)S(1)}, u32[]{:S(2)}, u32[]{:S(2)}) collective-permute-start(bf16[3,96,128]{2,1,0:T(8,128)(2,1)S(1)} %get-tuple-element.72.refs_7_), channel_id=1, source_target_pairs={{0,8},{4,12},{8,0},{12,4},{16,24},{20,28},{24,16},{28,20},{1,9},{5... | collective-permute-start | bytes 221192 | tf_op jit(solution)/shard_map/ppermute | solution.py:325
  72.4 3.0 %collective-permute-start.21 = (bf16[3,96,128]{2,1,0:T(8,128)(2,1)S(1)}, bf16[3,96,128]{2,1,0:T(8,128)(2,1)S(1)}, u32[]{:S(2)}, u32[]{:S(2)}) collective-permute-start(bf16[3,96,128]{2,1,0:T(8,128)(2,1)S(1)} %get-tuple-element.72.refs_7_), channel_id=1, source_target_pairs={{0,16},{4,20},{8,24},{12,28},{16,0},{20,4},{24,8},{28,12},{1,17},{... | collective-permute-start | bytes 221192 | tf_op jit(solution)/shard_map/ppermute | solution.py:325
  76.6 2.2 %collective-permute-start.19 = (bf16[3,96,128]{2,1,0:T(8,128)(2,1)S(1)}, bf16[3,96,128]{2,1,0:T(8,128)(2,1)S(1)}, u32[]{:S(2)}, u32[]{:S(2)}) collective-permute-start(bf16[3,96,128]{2,1,0:T(8,128)(2,1)S(1)} %get-tuple-element.72.refs_7_), channel_id=1, source_target_pairs={{0,24},{4,28},{8,16},{12,20},{16,8},{20,12},{24,0},{28,4},{1,25},{... | collective-permute-start | bytes 221192 | tf_op jit(solution)/shard_map/ppermute | solution.py:325
  78.7 2.6 %collective-permute-start.18 = (bf16[3,96,128]{2,1,0:T(8,128)(2,1)S(1)}, bf16[3,96,128]{2,1,0:T(8,128)(2,1)S(1)}, u32[]{:S(2)}, u32[]{:S(2)}) collective-permute-start(bf16[3,96,128]{2,1,0:T(8,128)(2,1)S(1)} %get-tuple-element.72.refs_7_), channel_id=1, source_target_pairs={{0,28},{4,24},{8,20},{12,16},{16,12},{20,8},{24,4},{28,0},{1,29},{... | collective-permute-start | bytes 221192 | tf_op jit(solution)/shard_map/ppermute | solution.py:325
  81.3 5.5 %collective-permute-done.20.refs_2_ = bf16[3,96,128]{2,1,0:T(8,128)(2,1)S(1)} collective-permute-done((bf16[3,96,128]{2,1,0:T(8,128)(2,1)S(1)}, bf16[3,96,128]{2,1,0:T(8,128)(2,1)S(1)}, u32[]{:S(2)}, u32[]{:S(2)}) %collective-permute-start.20) | collective-permute-done | bytes 73760 | tf_op jit(solution)/shard_map/ppermute | solution.py:325
  86.8 2.9 %shard_map.122 = bf16[18,96,384]{2,1,0:T(8,128)(2,1)} custom-call(s32[54]{0:T(128)S(1)} %copy-done.1, s32[1]{0:T(128)} %bitcast.1.row_ref, f32[9,96,384]{2,1,0:T(8,128)S(1)} %get-tuple-element.58.own_ref, f32[9,96,384]{2,1,0:T(8,128)S(1)} %collective-permute-done.17.other_ref, bf16[3,96,128]{2,1,0:T(8,128)(2,1)S(1)} %collective-permute-done.18.refs_0_, ...), custom_call_target="tpu_custom_call" | custom-call | tf_op jit(solution)/shard_map/pallas_call | solution.py:463
  (54 shorter events, 14.3 us)
Async XLA Ops:
  3.0 4.7 %collective-permute-start = (bf16[9,96,384]{2,1,0:T(8,128)(2,1)S(1)}, bf16[9,96,384]{2,1,0:T(8,128)(2,1)S(1)}, u32[]{:S(2)}, u32[]{:S(2)}) collective-permute-start(bf16[9,96,384]{2,1,0:T(8,128)(2,1)S(1)} %get-tuple-element.38), channel_id=1, source_target_pairs={{0,1},{1,0},{2,3},{3,2},{4,5},{5,4},{6,7},{7,6},{8,9},{9,8},{10,11... | collective-permute-start | bytes 1990664 | tf_op jit(solution)/shard_map/ppermute | solution.py:325
  3.6 19.3 %collective-permute-start.1 = (bf16[9,96,384]{2,1,0:T(8,128)(2,1)S(1)}, bf16[9,96,384]{2,1,0:T(8,128)(2,1)S(1)}, u32[]{:S(2)}, u32[]{:S(2)}) collective-permute-start(bf16[9,96,384]{2,1,0:T(8,128)(2,1)S(1)} %get-tuple-element.43), channel_id=1, source_target_pairs={{0,1},{1,0},{2,3},{3,2},{4,5},{5,4},{6,7},{7,6},{8,9},{9,8},{10,11... | collective-permute-start | bytes 1990664 | tf_op jit(solution)/shard_map/ppermute | solution.py:325
  3.6 10.7 %collective-permute-start.2 = (bf16[4,96,384]{2,1,0:T(8,128)(2,1)S(1)}, bf16[4,96,384]{2,1,0:T(8,128)(2,1)S(1)}, u32[]{:S(2)}, u32[]{:S(2)}) collective-permute-start(bf16[4,96,384]{2,1,0:T(8,128)(2,1)S(1)} %get-tuple-element.44), channel_id=1, source_target_pairs={{0,2},{1,3},{2,0},{3,1},{4,6},{5,7},{6,4},{7,5},{8,10},{9,11},{10,... | collective-permute-start | bytes 884744 | tf_op jit(solution)/shard_map/ppermute | solution.py:325
  6.6 16.1 %collective-permute-start.8 = (bf16[4,96,384]{2,1,0:T(8,128)(2,1)}, bf16[4,96,384]{2,1,0:T(8,128)(2,1)}, u32[]{:S(2)}, u32[]{:S(2)}) collective-permute-start(bf16[4,96,384]{2,1,0:T(8,128)(2,1)} %get-tuple-element.49), channel_id=1, source_target_pairs={{0,3},{1,2},{2,1},{3,0},{4,7},{5,6},{6,5},{7,4},{8,11},{9,10},{10,... | collective-permute-start | bytes 884744 | tf_op jit(solution)/shard_map/ppermute | solution.py:325
  9.4 15.2 %collective-permute-start.5 = (bf16[9,16,384]{2,1,0:T(8,128)(2,1)S(1)}, bf16[9,16,384]{2,1,0:T(8,128)(2,1)S(1)}, u32[]{:S(2)}, u32[]{:S(2)}) collective-permute-start(bf16[9,16,384]{2,1,0:T(8,128)(2,1)S(1)} %get-tuple-element.39._), channel_id=1, source_target_pairs={{0,2},{1,3},{2,0},{3,1},{4,6},{5,7},{6,4},{7,5},{8,10},{9,11},{10,... | collective-permute-start | bytes 331784 | tf_op jit(solution)/shard_map/ppermute | solution.py:325
  15.7 27.3 %collective-permute-start.3 = (bf16[2,96,384]{2,1,0:T(8,128)(2,1)S(1)}, bf16[2,96,384]{2,1,0:T(8,128)(2,1)S(1)}, u32[]{:S(2)}, u32[]{:S(2)}) collective-permute-start(bf16[2,96,384]{2,1,0:T(8,128)(2,1)S(1)} %get-tuple-element.45), channel_id=1, source_target_pairs={{0,2},{1,3},{2,0},{3,1},{4,6},{5,7},{6,4},{7,5},{8,10},{9,11},{10,... | collective-permute-start | bytes 442376 | tf_op jit(solution)/shard_map/ppermute | solution.py:325
  17.8 25.2 %collective-permute-start.4 = (bf16[2,96,384]{2,1,0:T(8,128)(2,1)S(1)}, bf16[2,96,384]{2,1,0:T(8,128)(2,1)S(1)}, u32[]{:S(2)}, u32[]{:S(2)}) collective-permute-start(bf16[2,96,384]{2,1,0:T(8,128)(2,1)S(1)} %get-tuple-element.46), channel_id=1, source_target_pairs={{0,3},{1,2},{2,1},{3,0},{4,7},{5,6},{6,5},{7,4},{8,11},{9,10},{10,... | collective-permute-start | bytes 442376 | tf_op jit(solution)/shard_map/ppermute | solution.py:325
  22.7 11.4 %collective-permute-start.6 = (bf16[3,96,384]{2,1,0:T(8,128)(2,1)S(1)}, bf16[3,96,384]{2,1,0:T(8,128)(2,1)S(1)}, u32[]{:S(2)}, u32[]{:S(2)}) collective-permute-start(bf16[3,96,384]{2,1,0:T(8,128)(2,1)S(1)} %get-tuple-element.47), channel_id=1, source_target_pairs={{0,2},{1,3},{2,0},{3,1},{4,6},{5,7},{6,4},{7,5},{8,10},{9,11},{10,... | collective-permute-start | bytes 663560 | tf_op jit(solution)/shard_map/ppermute | solution.py:325
  22.9 14.9 %collective-permute-start.7 = (bf16[3,96,384]{2,1,0:T(8,128)(2,1)S(1)}, bf16[3,96,384]{2,1,0:T(8,128)(2,1)S(1)}, u32[]{:S(2)}, u32[]{:S(2)}) collective-permute-start(bf16[3,96,384]{2,1,0:T(8,128)(2,1)S(1)} %get-tuple-element.48), channel_id=1, source_target_pairs={{0,3},{1,2},{2,1},{3,0},{4,7},{5,6},{6,5},{7,4},{8,11},{9,10},{10,... | collective-permute-start | bytes 663560 | tf_op jit(solution)/shard_map/ppermute | solution.py:325
  49.5 10.1 %collective-permute-start.10 = (bf16[3,96,128]{2,1,0:T(8,128)(2,1)S(1)}, bf16[3,96,128]{2,1,0:T(8,128)(2,1)S(1)}, u32[]{:S(2)}, u32[]{:S(2)}) collective-permute-start(bf16[3,96,128]{2,1,0:T(8,128)(2,1)S(1)} %get-tuple-element.63), channel_id=1, source_target_pairs={{0,28},{4,24},{8,20},{12,16},{16,12},{20,8},{24,4},{28,0},{1,29},{... | collective-permute-start | bytes 221192 | tf_op jit(solution)/shard_map/ppermute | solution.py:325
  54.3 7.0 %collective-permute-start.11 = (bf16[3,96,128]{2,1,0:T(8,128)(2,1)S(1)}, bf16[3,96,128]{2,1,0:T(8,128)(2,1)S(1)}, u32[]{:S(2)}, u32[]{:S(2)}) collective-permute-start(bf16[3,96,128]{2,1,0:T(8,128)(2,1)S(1)} %get-tuple-element.64), channel_id=1, source_target_pairs={{0,24},{4,28},{8,16},{12,20},{16,8},{20,12},{24,0},{28,4},{1,25},{... | collective-permute-start | bytes 221192 | tf_op jit(solution)/shard_map/ppermute | solution.py:325
  54.5 11.7 %collective-permute-start.12 = (bf16[3,96,128]{2,1,0:T(8,128)(2,1)S(1)}, bf16[3,96,128]{2,1,0:T(8,128)(2,1)S(1)}, u32[]{:S(2)}, u32[]{:S(2)}) collective-permute-start(bf16[3,96,128]{2,1,0:T(8,128)(2,1)S(1)} %get-tuple-element.65), channel_id=1, source_target_pairs={{0,20},{4,16},{8,28},{12,24},{16,4},{20,0},{24,12},{28,8},{1,21},{... | collective-permute-start | bytes 221192 | tf_op jit(solution)/shard_map/ppermute | solution.py:325
  55.3 12.0 %collective-permute-start.13 = (bf16[3,96,128]{2,1,0:T(8,128)(2,1)S(1)}, bf16[3,96,128]{2,1,0:T(8,128)(2,1)S(1)}, u32[]{:S(2)}, u32[]{:S(2)}) collective-permute-start(bf16[3,96,128]{2,1,0:T(8,128)(2,1)S(1)} %get-tuple-element.66), channel_id=1, source_target_pairs={{0,16},{4,20},{8,24},{12,28},{16,0},{20,4},{24,8},{28,12},{1,17},{... | collective-permute-start | bytes 221192 | tf_op jit(solution)/shard_map/ppermute | solution.py:325
  57.3 10.0 %collective-permute-start.14 = (bf16[3,96,128]{2,1,0:T(8,128)(2,1)S(1)}, bf16[3,96,128]{2,1,0:T(8,128)(2,1)S(1)}, u32[]{:S(2)}, u32[]{:S(2)}) collective-permute-start(bf16[3,96,128]{2,1,0:T(8,128)(2,1)S(1)} %get-tuple-element.67), channel_id=1, source_target_pairs={{0,12},{4,8},{8,4},{12,0},{16,28},{20,24},{24,20},{28,16},{1,13},{... | collective-permute-start | bytes 221192 | tf_op jit(solution)/shard_map/ppermute | solution.py:325
  59.6 7.7 %collective-permute-start.15 = (bf16[3,96,128]{2,1,0:T(8,128)(2,1)S(1)}, bf16[3,96,128]{2,1,0:T(8,128)(2,1)S(1)}, u32[]{:S(2)}, u32[]{:S(2)}) collective-permute-start(bf16[3,96,128]{2,1,0:T(8,128)(2,1)S(1)} %get-tuple-element.68), channel_id=1, source_target_pairs={{0,8},{4,12},{8,0},{12,4},{16,24},{20,28},{24,16},{28,20},{1,9},{5... | collective-permute-start | bytes 221192 | tf_op jit(solution)/shard_map/ppermute | solution.py:325
  61.3 6.0 %collective-permute-start.16 = (bf16[3,96,128]{2,1,0:T(8,128)(2,1)S(1)}, bf16[3,96,128]{2,1,0:T(8,128)(2,1)S(1)}, u32[]{:S(2)}, u32[]{:S(2)}) collective-permute-start(bf16[3,96,128]{2,1,0:T(8,128)(2,1)S(1)} %get-tuple-element.69), channel_id=1, source_target_pairs={{0,4},{4,0},{8,12},{12,8},{16,20},{20,16},{24,28},{28,24},{1,5},{5... | collective-permute-start | bytes 221192 | tf_op jit(solution)/shard_map/ppermute | solution.py:325
  68.6 18.2 %collective-permute-start.17 = (f32[9,96,384]{2,1,0:T(8,128)S(1)}, f32[9,96,384]{2,1,0:T(8,128)S(1)}, u32[]{:S(2)}, u32[]{:S(2)}) collective-permute-start(f32[9,96,384]{2,1,0:T(8,128)S(1)} %get-tuple-element.71), channel_id=1, source_target_pairs={{0,1},{1,0},{2,3},{3,2},{4,5},{5,4},{6,7},{7,6},{8,9},{9,8},{10,11... | collective-permute-start | bytes 3981320 | tf_op jit(solution)/shard_map/ppermute | solution.py:325
  68.6 6.8 %collective-permute-start.24 = (bf16[3,96,128]{2,1,0:T(8,128)(2,1)S(1)}, bf16[3,96,128]{2,1,0:T(8,128)(2,1)S(1)}, u32[]{:S(2)}, u32[]{:S(2)}) collective-permute-start(bf16[3,96,128]{2,1,0:T(8,128)(2,1)S(1)} %get-tuple-element.72.refs_7_), channel_id=1, source_target_pairs={{0,4},{4,0},{8,12},{12,8},{16,20},{20,16},{24,28},{28,24},{1,5},{5... | collective-permute-start | bytes 221192 | tf_op jit(solution)/shard_map/ppermute | solution.py:325
  69.1 7.4 %collective-permute-start.23 = (bf16[3,96,128]{2,1,0:T(8,128)(2,1)S(1)}, bf16[3,96,128]{2,1,0:T(8,128)(2,1)S(1)}, u32[]{:S(2)}, u32[]{:S(2)}) collective-permute-start(bf16[3,96,128]{2,1,0:T(8,128)(2,1)S(1)} %get-tuple-element.72.refs_7_), channel_id=1, source_target_pairs={{0,8},{4,12},{8,0},{12,4},{16,24},{20,28},{24,16},{28,20},{1,9},{5... | collective-permute-start | bytes 221192 | tf_op jit(solution)/shard_map/ppermute | solution.py:325
  71.0 7.8 %collective-permute-start.22 = (bf16[3,96,128]{2,1,0:T(8,128)(2,1)S(1)}, bf16[3,96,128]{2,1,0:T(8,128)(2,1)S(1)}, u32[]{:S(2)}, u32[]{:S(2)}) collective-permute-start(bf16[3,96,128]{2,1,0:T(8,128)(2,1)S(1)} %get-tuple-element.72.refs_7_), channel_id=1, source_target_pairs={{0,12},{4,8},{8,4},{12,0},{16,28},{20,24},{24,20},{28,16},{1,13},{... | collective-permute-start | bytes 221192 | tf_op jit(solution)/shard_map/ppermute | solution.py:325
  72.4 9.0 %collective-permute-start.21 = (bf16[3,96,128]{2,1,0:T(8,128)(2,1)S(1)}, bf16[3,96,128]{2,1,0:T(8,128)(2,1)S(1)}, u32[]{:S(2)}, u32[]{:S(2)}) collective-permute-start(bf16[3,96,128]{2,1,0:T(8,128)(2,1)S(1)} %get-tuple-element.72.refs_7_), channel_id=1, source_target_pairs={{0,16},{4,20},{8,24},{12,28},{16,0},{20,4},{24,8},{28,12},{1,17},{... | collective-permute-start | bytes 221192 | tf_op jit(solution)/shard_map/ppermute | solution.py:325
  75.4 11.4 %collective-permute-start.20 = (bf16[3,96,128]{2,1,0:T(8,128)(2,1)S(1)}, bf16[3,96,128]{2,1,0:T(8,128)(2,1)S(1)}, u32[]{:S(2)}, u32[]{:S(2)}) collective-permute-start(bf16[3,96,128]{2,1,0:T(8,128)(2,1)S(1)} %get-tuple-element.72.refs_7_), channel_id=1, source_target_pairs={{0,20},{4,16},{8,28},{12,24},{16,4},{20,0},{24,12},{28,8},{1,21},{... | collective-permute-start | bytes 221192 | tf_op jit(solution)/shard_map/ppermute | solution.py:325
  76.6 10.2 %collective-permute-start.19 = (bf16[3,96,128]{2,1,0:T(8,128)(2,1)S(1)}, bf16[3,96,128]{2,1,0:T(8,128)(2,1)S(1)}, u32[]{:S(2)}, u32[]{:S(2)}) collective-permute-start(bf16[3,96,128]{2,1,0:T(8,128)(2,1)S(1)} %get-tuple-element.72.refs_7_), channel_id=1, source_target_pairs={{0,24},{4,28},{8,16},{12,20},{16,8},{20,12},{24,0},{28,4},{1,25},{... | collective-permute-start | bytes 221192 | tf_op jit(solution)/shard_map/ppermute | solution.py:325
  78.7 8.0 %collective-permute-start.18 = (bf16[3,96,128]{2,1,0:T(8,128)(2,1)S(1)}, bf16[3,96,128]{2,1,0:T(8,128)(2,1)S(1)}, u32[]{:S(2)}, u32[]{:S(2)}) collective-permute-start(bf16[3,96,128]{2,1,0:T(8,128)(2,1)S(1)} %get-tuple-element.72.refs_7_), channel_id=1, source_target_pairs={{0,28},{4,24},{8,20},{12,16},{16,12},{20,8},{24,4},{28,0},{1,29},{... | collective-permute-start | bytes 221192 | tf_op jit(solution)/shard_map/ppermute | solution.py:325
  (8 other events, 78.9 us)

commit v4 on v3

v4 whole, which is shorter than its diff:
```python
import functools

import jax
import jax.numpy as jnp
from jax import lax
from jax.experimental import pallas as pl
from jax.experimental.pallas import tpu as pltpu
from jax.sharding import PartitionSpec as P

TILE = 128
ALIGN = 16
CHUNKS = (4, 3, 2)
BLOCK = 48
DEPTH = 256
MIB = 1024 * 1024
VMEM = 20 * MIB
F32 = jnp.float32
BF16 = jnp.bfloat16


def pack_kernel(row_ref, *refs, chunks, siblings, edges):
    count = 2 * len(chunks) + siblings + edges
    sems = refs[-1]
    outs, held = refs[-1 - 2 * count : -1 - count], refs[-1 - count : -1]
    pixels_ref, rows_ref = refs[:2]
    half = pixels_ref.shape[0] // 2
    row = row_ref[0]
    core = row & 1
    pieces = []
    kept = list(held)
    if siblings:
        other = pl.ds((1 - core) * half, half)
        pieces += [rows_ref.at[other], pixels_ref.at[other]]
        kept[:1] = [held[0].at[pl.ds(0, half)], held[0].at[pl.ds(half, half)]]
    for s, n in chunks:
        for which in range(2):
            pieces.append(pixels_ref.at[pl.ds((core ^ which) * half + s, n)])
    fetches = [
        pltpu.make_async_copy(piece, place, sems.at[0, i])
        for i, (piece, place) in enumerate(zip(pieces, kept))
    ]
    stores = [
        pltpu.make_async_copy(place, out, sems.at[1, i])
        for i, (place, out) in enumerate(zip(held, outs))
    ]
    if edges:
        pad = outs[-1].shape[1]
        first = jnp.where(row < 2, rows_ref.shape[1] - pad, 0)
        near = pl.ds(pl.multiple_of(first, ALIGN), pad)
        holds = core == (row < 2).astype(jnp.int32)
        own = rows_ref.at[pl.ds(core * half, half), near]
        edge = pltpu.make_async_copy(own, held[-1], sems.at[0, count])
        passed = pltpu.make_async_copy(
            refs[2].at[pl.ds(0, half), near], held[-1], sems.at[0, count]
        )
        pl.when(holds)(edge.start)
        pl.when(jnp.logical_not(holds))(passed.start)
        fetches.append(edge)
    for fetch in fetches[: len(pieces)]:
        fetch.start()
    if siblings:
        fetches.pop(0).wait()
    for fetch, store in zip(fetches, stores):
        fetch.wait()
        store.start()
    for store in stores:
        store.wait()


def pack(row, pixels, rows, chunks, pad, siblings=False, sibling=None, after=()):
    images, band, side = pixels.shape
    half = images // 2
    shapes = [(images, band, side)] if siblings else []
    shapes += [(n, band, side) for _, n in chunks for _ in range(2)]
    arrays = [pltpu.with_memory_space_constraint(a, pltpu.HBM) for a in (pixels, rows)]
    if sibling is not None:
        shapes.append((half, pad, side))
        arrays.append(sibling)
    arrays += after
    anywhere = pl.BlockSpec(memory_space=pl.ANY)
    return pl.pallas_call(
        functools.partial(
            pack_kernel, chunks=chunks, siblings=siblings, edges=sibling is not None
        ),
        in_specs=[pl.BlockSpec(memory_space=pltpu.SMEM)] + [anywhere] * len(arrays),
        out_specs=[anywhere] * len(shapes),
        out_shape=[jax.ShapeDtypeStruct(shape, BF16) for shape in shapes],
        scratch_shapes=[pltpu.VMEM(shape, BF16) for shape in shapes]
        + [pltpu.SemaphoreType.DMA((2, len(shapes) + 1))],
        compiler_params=pltpu.CompilerParams(vmem_limit_bytes=VMEM),
    )(row, *arrays)


def target_kernel(
    place_ref, patch_ref, block_ref, level_ref, table_ref, home_ref, *refs, tiles
):
    large_refs = refs[:4]
    slots_ref, own_ref, weights_ref, denom_ref = refs[5:9]
    kept_refs, sems = refs[9:13], refs[13]
    mine, core = place_ref[0], place_ref[1] & 1
    visits, detectors = level_ref.shape
    pieces = slots_ref.shape[0]
    half = weights_ref.shape[0]
    first = mine * (half * 2)
    copies = [
        pltpu.make_async_copy(large.at[pl.ds(core * half, half)], kept, sems.at[i])
        for i, (large, kept) in enumerate(zip(large_refs, kept_refs))
    ]
    for copy in copies:
        copy.start()

    def slot_of(n):
        return (home_ref[patch_ref[n]] ^ mine) * tiles + block_ref[n]

    def place(i, _):
        slots_ref[i] = slot_of(mine * pieces + i)
        return 0

    def place_own(i, _):
        own_ref[i] = slots_ref[core * half * tiles + i]
        return 0

    def weigh(i, _):
        image = first + core * half + i
        weights_ref[i] = table_ref[level_ref[image % visits, image // visits]]
        return 0

    def add(d, sums):
        for v in range(visits):
            weight = table_ref[level_ref[v, d]]
            for q in range(tiles):
                slot = slot_of((d * visits + v) * tiles + q)
                sums = tuple(
                    total + jnp.where(slot == t, weight, 0.0) for t, total in enumerate(sums)
                )
        return sums

    lax.fori_loop(0, pieces, place, 0)
    lax.fori_loop(0, half * tiles, place_own, 0)
    lax.fori_loop(0, half, weigh, 0)
    sums = lax.fori_loop(0, detectors, add, (jnp.float32(0),) * tiles)
    for t in range(tiles):
        denom_ref[t] = sums[t]
    for copy in copies:
        copy.wait()


def match_kernel(slot_ref, weight_ref, row_ref, *refs, start, count, taps, halves, first, warp, send):
    profile_ref, refs = refs[0], refs[1:]
    if warp:
        pixels_ref, rows_ref, cols_ref, sibling_ref, far_ref, cross_ref, edge_ref = refs[:7]
        refs = refs[7:]
    else:
        warped_ref, refs = refs[0], refs[1:]
    if not first:
        refs = refs[2 * len(halves) :]
    matched_refs = dict(zip(halves, refs))
    refs = refs[len(halves) :]
    numers = dict(zip(halves, refs))
    refs = refs[len(halves) :]
    if send:
        sent_ref, warped_ref, refs = refs[0], refs[1], refs[2:]
    elif warp:
        warped_ref, refs = refs[-1], refs[:-1]
    tables, refs = refs[:count], refs[count:]
    stacks = {m: refs[count * i : count * (i + 1)] for i, m in enumerate(halves)}
    refs = refs[count * len(halves) :]
    _, band, side = matched_refs[halves[0]].shape
    pad = (warped_ref.shape[1] - 2 * band) // 2
    span = BLOCK + 2 * pad
    reach = (taps - 1) // 2
    inner = DEPTH // span
    outer = -(-taps // inner)
    tiles = side // TILE
    width = side + TILE
    blocks = band // BLOCK
    row = row_ref[0]
    core = row & 1

    if first:
        for numer in numers.values():
            numer[...] = jnp.zeros_like(numer)
    if warp:
        for g in range(count):
            image, extended = refs[g], refs[count + g]
            index = start + g
            shards = (pixels_ref.at[index], sibling_ref.at[sibling_ref.shape[0] // 2 + index])
            for mask, shard in enumerate(shards + (far_ref.at[g], cross_ref.at[g])):
                at = pl.multiple_of((row ^ mask) * band, band)
                image[pl.ds(at, band), :] = shard[...]
            edge = edge_ref[index]
            blank = jnp.zeros_like(edge)
            extended[0:pad, :] = jnp.where(row >= 2, edge, blank)
            extended[pad + 2 * band :, :] = jnp.where(row >= 2, blank, edge)
            for which, rows in enumerate((rows_ref, sibling_ref)):
                at = pl.multiple_of(pad + (core ^ which) * band, ALIGN)
                extended[pl.ds(at, band), :] = rows[index]
    for g in range(count):
        profiles = None
        for b in range(inner):
            part = profile_ref[start + g, pl.ds(b, outer, stride=inner), :]
            part = jnp.concatenate([part, jnp.zeros((outer, DEPTH - TILE), F32)], axis=1)
            part = pltpu.roll(part, span * b, 1) if b else part
            profiles = part if profiles is None else profiles + part
        for a in range(outer):
            profile = jnp.broadcast_to(profiles[a : a + 1, :], (BLOCK, DEPTH))
            toeplitz = pltpu.roll(profile, 0, 1, stride=1, stride_axis=0)
            tables[g][BLOCK * a : BLOCK * (a + 1), :] = toeplitz.astype(BF16)
    for g in range(count):
        if warp:
            image, extended = refs[g], refs[count + g]
            by_rows = jnp.dot(extended[...], image[...], preferred_element_type=F32).astype(BF16)
            warped = jnp.dot(by_rows, cols_ref[start + g], preferred_element_type=F32)
            warped_ref[g] = warped.astype(BF16)
        for m in halves:
            at = pl.multiple_of((core ^ m) * band, band)
            ring = warped_ref[g, pl.ds(at, band + 2 * pad), :]
            ring = jnp.concatenate([ring, jnp.zeros((band + 2 * pad, TILE), BF16)], axis=1)
            stack = stacks[m][g]
            stack[:, span * inner :, :] = jnp.zeros((blocks, DEPTH - span * inner, width), BF16)
            for b in range(inner):
                turn = (inner // 2 - b) % width
                shifted = pltpu.roll(ring, turn, 1) if turn else ring
                for k in range(blocks):
                    stack[k, span * b : span * (b + 1), :] = shifted[BLOCK * k : BLOCK * k + span]
    middle = outer // 2
    origin = inner * middle + inner // 2 - reach
    for m in halves:
        for g in range(count):
            index = start + g
            weight = weight_ref[index]
            for k in range(blocks):
                partial = jnp.dot(tables[g][...], stacks[m][g][k], preferred_element_type=F32)
                total = None
                for a in range(outer):
                    turn = (inner * (middle - a) - origin) % width
                    part = partial[BLOCK * a : BLOCK * (a + 1)]
                    part = pltpu.roll(part, turn, 1) if turn else part
                    total = part if total is None else total + part
                matched = total[:, 0:side]
                here = slice(BLOCK * k, BLOCK * (k + 1))
                matched_refs[m][index, here, :] = matched
                for q in range(tiles):
                    slot = slot_ref[index * tiles + q]
                    piece = (weight * matched[:, TILE * q : TILE * (q + 1)]).astype(BF16)
                    numers[m][slot, here, :] += piece.astype(F32)
    if send:
        sent_ref[...] = numers[1][...].astype(BF16)


def match_chunk(scalars, profiles, operands, carry, start, count, taps, slot_count, halves, send=False):
    warp = len(operands) > 1
    if warp:
        half, band, side = operands[0].shape
        tall = 2 * band + 2 * operands[-1].shape[1]
    else:
        _, tall, side = operands[0].shape
        half, band, _ = carry[0].shape
    inner = DEPTH // (BLOCK + tall - 2 * band)
    outer = -(-taps // inner)
    width = side + TILE
    blocks = band // BLOCK
    first = carry is None
    in_vmem = pl.BlockSpec(memory_space=pltpu.VMEM)
    arrays = list(scalars) + [profiles] + list(operands)
    in_specs = [pl.BlockSpec(memory_space=pltpu.SMEM)] * 3 + [in_vmem] * (len(operands) + 1)
    aliases = {}
    if not first:
        aliases = {len(arrays) + i: i for i in range(len(carry))}
        arrays += list(carry)
        in_specs += [in_vmem] * len(carry)
    matched = jax.ShapeDtypeStruct((half, band, side), F32)
    numer_shape = (slot_count, band, TILE)
    out_shape = [matched] * len(halves) + [jax.ShapeDtypeStruct(numer_shape, F32)] * len(halves)
    if send:
        out_shape.append(jax.ShapeDtypeStruct(numer_shape, BF16))
        out_shape.append(jax.ShapeDtypeStruct((count, tall, side), BF16))
    scratch = [pltpu.VMEM((outer * BLOCK, DEPTH), BF16)] * count
    scratch += [pltpu.VMEM((blocks, DEPTH, width), BF16)] * (count * len(halves))
    if warp:
        scratch += [pltpu.VMEM((side, side), BF16)] * count
        scratch += [pltpu.VMEM((tall, side), BF16)] * count
        if not send:
            scratch.append(pltpu.VMEM((count, tall, side), BF16))
    return pl.pallas_call(
        functools.partial(
            match_kernel,
            start=start,
            count=count,
            taps=taps,
            halves=halves,
            first=first,
            warp=warp,
            send=send,
        ),
        in_specs=in_specs,
        out_specs=[in_vmem] * len(out_shape),
        scratch_shapes=scratch,
        out_shape=out_shape,
        input_output_aliases=aliases,
        compiler_params=pltpu.CompilerParams(vmem_limit_bytes=VMEM),
        cost_estimate=pl.CostEstimate(
            flops=count * 1000000000 * len(halves), bytes_accessed=count * 1000000, transcendentals=0
        ),
    )(*arrays)


def merge_kernel(own_ref, other_ref, *part_refs):
    each = part_refs[0].shape[0]
    for m, part in enumerate(part_refs):
        boxes = slice(each * m, each * (m + 1))
        part[...] = (own_ref[boxes] + other_ref[boxes].astype(F32)).astype(BF16)


def template_kernel(denom_ref, _, *refs):
    part_refs, template_ref, coadd_ref = refs[:-3], refs[-3], refs[-2]
    for q in range(template_ref.shape[0]):
        total = part_refs[0][q].astype(F32)
        for part in part_refs[1:]:
            total = total + part[q].astype(F32)
        box = (total / jnp.maximum(denom_ref[q], 1.0)).astype(BF16)
        template_ref[q] = box
        coadd_ref[:, TILE * q : TILE * (q + 1)] = box


def difference_kernel(slot_ref, row_ref, own_ref, other_ref, *refs, masks):
    template_refs, out_ref, held = refs[:-2], refs[-2], refs[-1]
    step = pl.program_id(0)
    each = template_refs[0].shape[0]
    count, _, side = own_ref.shape
    tiles = side // TILE

    @pl.when(step == 0)
    def _():
        for m, template in zip(masks, template_refs):
            held[each * m : each * (m + 1)] = template[...]

    def subtract(matched_ref):
        for i in range(count):
            for q in range(tiles):
                slot = slot_ref[(step * count + i) * tiles + q]
                columns = slice(TILE * q, TILE * (q + 1))
                box = held[slot].astype(F32)
                out_ref[i, :, columns] = (matched_ref[i, :, columns] - box).astype(BF16)

    mine = (step * 2 // pl.num_programs(0)) == (row_ref[0] & 1)
    pl.when(mine)(lambda: subtract(own_ref))
    pl.when(jnp.logical_not(mine))(lambda: subtract(other_ref))


def exchange(value, axis, mask):
    size = lax.axis_size(axis)
    return lax.ppermute(value, axis, [(i, i ^ mask) for i in range(size)])


def per_device(
    images,
    warp_rows,
    warp_cols,
    psf_coef,
    taps,
    dest_patch,
    dest_block,
    weight_index,
    weight_table,
    patch_home,
):
    det_count, visit_count, band, side = images.shape
    kernel_count, tap_count = taps.shape
    reach = (tap_count - 1) // 2
    pad = -(-reach // ALIGN) * ALIGN
    span = BLOCK + 2 * pad
    tiles = side // TILE
    det_devices = lax.axis_size("det")
    mine = lax.axis_index("det")
    row = lax.axis_index("row").astype(jnp.int32)
    core = row & 1
    image_count = det_count * visit_count
    half = image_count // 2
    assert lax.axis_size("row") == 4 and image_count == 2 * half
    pixels = images.reshape(image_count, band, side)
    rows = warp_rows.reshape(image_count, band, side)
    cols = warp_cols.reshape(image_count, side, side)
    row_one = row.reshape(1)

    chunks = CHUNKS if sum(CHUNKS) == half else (1,) * half
    starts = [sum(chunks[:c]) for c in range(len(chunks))]
    spans = list(zip(starts, chunks))
    far, cross = [], []

    def send(packed):
        for first, second in zip(packed[::2], packed[1::2]):
            far.append(exchange(first, "row", 2))
            cross.append(exchange(second, "row", 3))

    packed = pack(row_one, pixels, rows, spans[:1], pad, siblings=True)
    sibling = exchange(packed[0], "row", 1)
    send(packed[1:])
    packed = pack(row_one, pixels, rows, spans[2:], pad, sibling=sibling)
    edge = exchange(packed[-1], "row", 2)
    send(pack(row_one, pixels, rows, spans[1:2], pad, after=[far[0]]))
    send(packed[:-1])

    with jax.named_scope("profiles"):
        scaled = (psf_coef.reshape(image_count, kernel_count)[:, :, None] * taps).astype(BF16)
        profiles = jnp.einsum(
            "nkt,ku->nut", scaled, taps.astype(BF16), preferred_element_type=F32
        )
        inner = DEPTH // span
        rows_kept = -(-tap_count // inner) * inner
        profiles = jnp.pad(
            profiles,
            (
                (0, 0),
                (0, rows_kept - tap_count + -rows_kept % 8),
                (pad - reach, TILE - tap_count - pad + reach),
            ),
        )
    anywhere = pl.BlockSpec(memory_space=pl.ANY)
    in_vmem = pl.BlockSpec(memory_space=pltpu.VMEM)
    large = (pixels, rows, cols, profiles)
    slots, own_slots, weights, denom, *kept = pl.pallas_call(
        functools.partial(target_kernel, tiles=tiles),
        in_specs=[pl.BlockSpec(memory_space=pltpu.SMEM)] * 6 + [anywhere] * 5,
        out_specs=[pl.BlockSpec(memory_space=pltpu.SMEM)] * 4 + [in_vmem] * 4,
        out_shape=[
            jax.ShapeDtypeStruct((image_count * tiles,), jnp.int32),
            jax.ShapeDtypeStruct((half * tiles,), jnp.int32),
            jax.ShapeDtypeStruct((half,), F32),
            jax.ShapeDtypeStruct((tiles,), F32),
        ]
        + [jax.ShapeDtypeStruct((half,) + a.shape[1:], a.dtype) for a in large],
        scratch_shapes=[pltpu.SemaphoreType.DMA((len(large),))],
        compiler_params=pltpu.CompilerParams(vmem_limit_bytes=VMEM),
    )(
        jnp.stack([mine.astype(jnp.int32), row]),
        dest_patch.reshape(-1),
        dest_block,
        weight_index.T,
        weight_table,
        patch_home,
        *[pltpu.with_memory_space_constraint(a, pltpu.HBM) for a in large],
        packed[-1],
    )

    carry = None
    slot_count = det_devices * tiles
    scalars = (own_slots, weights, row_one)
    common = (tap_count, slot_count)
    for c, (s, n) in enumerate(spans):
        operands = tuple(kept[:3]) + (sibling, far[c], cross[c], edge)
        if c < len(spans) - 1:
            carry = match_chunk(scalars, kept[3], operands, carry, s, n, *common, (0, 1))
    matched_sent, _, sums_sent, warped = match_chunk(
        scalars, kept[3], operands, carry[1::2], s, n, *common, (1,), send=True
    )
    other_sums = exchange(sums_sent, "row", 1)
    matched, own_sums = match_chunk(
        scalars, kept[3], (warped,), carry[0::2], s, n, *common, (0,)
    )
    box_shape = (tiles, band, TILE)
    box = jax.ShapeDtypeStruct(box_shape, BF16)
    small = pltpu.CompilerParams(vmem_limit_bytes=4 * MIB + 16 * slot_count * band * TILE)
    parts = pl.pallas_call(
        merge_kernel,
        in_specs=[in_vmem] * 2,
        out_specs=[in_vmem] * det_devices,
        out_shape=[box] * det_devices,
        compiler_params=small,
    )(own_sums, other_sums)
    masks = tuple(range(det_devices - 1, 0, -1)) + (0,)
    received = [exchange(parts[m], "det", m) if m else parts[m] for m in masks]
    template, coadd, matched_sent = pl.pallas_call(
        template_kernel,
        in_specs=[pl.BlockSpec(memory_space=pltpu.SMEM), anywhere] + [in_vmem] * det_devices,
        out_specs=[in_vmem] * 2 + [anywhere],
        out_shape=[
            box,
            jax.ShapeDtypeStruct((band, side), BF16),
            jax.ShapeDtypeStruct(matched_sent.shape, F32),
        ],
        input_output_aliases={1: 2},
        compiler_params=small,
    )(denom, matched_sent, *received)
    other_matched = exchange(matched_sent, "row", 1)
    evens = tuple(range(det_devices - 2, 0, -2))
    passed = {0: template}
    for m in evens:
        passed[m] = exchange(template, "det", m)
    for m in evens + (0,):
        passed[m ^ 1] = exchange(passed[m], "det", 1)
    templates = [passed[m] for m in masks]
    group = 3 if half % 3 == 0 else 1
    steps = half // group

    def half_block(which):
        def place(i, slot, row):
            return (jnp.clip(i - ((row[0] & 1) ^ which) * steps, 0, steps - 1), 0, 0)

        return pl.BlockSpec((group, band, side), place)

    difference = pl.pallas_call(
        functools.partial(difference_kernel, masks=masks),
        grid_spec=pltpu.PrefetchScalarGridSpec(
            num_scalar_prefetch=2,
            grid=(2 * steps,),
            in_specs=[half_block(0), half_block(1)]
            + [pl.BlockSpec(box_shape, lambda i, *_: (0, 0, 0))] * det_devices,
            out_specs=pl.BlockSpec((group, band, side), lambda i, *_: (i, 0, 0)),
            scratch_shapes=[pltpu.VMEM((slot_count, band, TILE), BF16)],
        ),
        out_shape=jax.ShapeDtypeStruct((image_count, band, side), BF16),
        compiler_params=small,
    )(slots, row_one, matched, other_matched, *templates)
    return difference.reshape(images.shape), coadd.reshape(1, band, side)


def solution(mesh):
    placed = (
        P("det", None, "row", None),
        P("det", None, "row", None),
        P("det", None, None, None),
        P("det", None, None),
        P(),
        P(),
        P(),
        P(),
        P(),
        P(),
    )
    return jax.shard_map(
        per_device,
        mesh=mesh,
        in_specs=placed,
        out_specs=(P("det", None, "row", None), P("det", "row", None)),
        check_vma=False,
    )
```

time: 90.5 us -> 81 us (0.90)
  starting transfers between devices: 33.7 us -> 29.2 us
  Pallas kernels: 30.3 us -> 27.1 us
  waiting for transfers between devices: 21.9 us -> 20.8 us
    ppermute x25 -> x24, starting transfers between devices: 33.7 us -> 29.2 us  [exchange(): return lax.ppermute(value, axis, [(i, i ^ mask) for i in range(size)])]
    pallas_call x3 -> x4, Pallas kernels: 15.7 us -> 12.7 us  [match_chunk(): pl.pallas_call(functools.partial(match_kernel, start=start, count=count,...]
    unnamed x14 -> x10, local copies, waits for them, and re-layouts: 1.3 us -> 0.02 us
    ppermute x25 -> x24, waiting for transfers between devices: 21.9 us -> 20.8 us  [exchange(): return lax.ppermute(value, axis, [(i, i ^ mask) for i in range(size)])]
  transfers between devices with their start and end apart: 25 -> 24, of which waited for: 8 -> 10; matrix products, arithmetic and copies ran while one was open for 2% -> 3% of each run, Pallas kernels for 22% -> 23%
where the time goes in v4:
time: 81 us; the launch traced here: 80.6 us
  starting transfers between devices  29.2 us (36%)
  Pallas kernels  27.1 us (33%)
  waiting for transfers between devices  20.8 us (26%)
  local copies, waits for them, and re-layouts  1.55 us (2%)
  matrix products  1.05 us (1%)
    ppermute x24, starting transfers between devices, exchange(): return lax.ppermute(value, axis, [(i, i ^ mask) for i in range(size)])  29.2 us
    ppermute x24, waiting for transfers between devices, exchange(): return lax.ppermute(value, axis, [(i, i ^ mask) for i in range(size)])  20.8 us
    pallas_call x4, Pallas kernels, match_chunk(): pl.pallas_call(functools.partial(match_kernel, start=start, count=count,...  12.7 us
    pallas_call x3, Pallas kernels, pack(): pl.pallas_call(functools.partial(pack_kernel, chunks=chunks, siblings=sib...  5.19 us
    pallas_call x1, Pallas kernels, per_device(): pl.pallas_call(functools.partial(target_kernel, tiles=tiles), in_specs=[p...  4.88 us
    pallas_call x1, Pallas kernels, per_device(): pl.pallas_call(functools.partial(difference_kernel, masks=masks), grid_sp...  2.94 us
  transfers between devices with their start and end apart: 24, of which 10 were waited for; matrix products, arithmetic and copies ran while one was open for 3% of the time, Pallas kernels for 23%

profile of v4, /device:TPU:0, one launch (start us, length us, event | category | flops | bytes accessed | tf_op | source)
XLA Modules:
  0.0 80.6 jit_solution(9731700850495119332)
XLA Ops:
  0.6 2.2 %shard_map.113 = (bf16[18,96,384]{2,1,0:T(8,128)(2,1)S(1)}, bf16[4,96,384]{2,1,0:T(8,128)(2,1)}, bf16[4,96,384]{2,1,0:T(8,128)(2,1)S(1)}) custom-call(s32[1]{0:T(128)} %bitcast.1.row_ref, bf16[18,96,384]{2,1,0:T(8,128)(2,1)} %bitcast.16, bf16[18,96,384]{2,1,0:T(8,128)(2,1)} %bitcast.20), custom_call_target="tpu_custom_call" | custom-call | tf_op jit(solution)/shard_map/pallas_call | solution.py:81
  3.3 2.6 %collective-permute-start.4 = (bf16[4,96,384]{2,1,0:T(8,128)(2,1)}, bf16[4,96,384]{2,1,0:T(8,128)(2,1)S(1)}, u32[]{:S(2)}, u32[]{:S(2)}) collective-permute-start(bf16[4,96,384]{2,1,0:T(8,128)(2,1)} %get-tuple-element.53), channel_id=1, source_target_pairs={{0,2},{1,3},{2,0},{3,1},{4,6},{5,7},{6,4},{7,5},{8,10},{9,11},{10,... | collective-permute-start | bytes 884744 | tf_op jit(solution)/shard_map/ppermute | solution.py:353
  8.6 1.5 %shard_map.114 = (bf16[2,96,384]{2,1,0:T(8,128)(2,1)S(1)}, bf16[2,96,384]{2,1,0:T(8,128)(2,1)S(1)}, bf16[9,16,384]{2,1,0:T(8,128)(2,1)S(1)}) custom-call(s32[1]{0:T(128)} %bitcast.1.row_ref, bf16[18,96,384]{2,1,0:T(8,128)(2,1)} %bitcast.17, bf16[18,96,384]{2,1,0:T(8,128)(2,1)} %bitcast.21, bf16[18,96,384]{2,1,0:T(8,128)(2,1)S(1)} %collective-permute-done.refs_2_.refs_4_), custom_call_target="tpu_custom_call" | custom-call | tf_op jit(solution)/shard_map/pallas_call | solution.py:81
  10.1 1.8 %collective-permute-start.3 = (bf16[9,16,384]{2,1,0:T(8,128)(2,1)S(1)}, bf16[9,16,384]{2,1,0:T(8,128)(2,1)S(1)}, u32[]{:S(2)}, u32[]{:S(2)}) collective-permute-start(bf16[9,16,384]{2,1,0:T(8,128)(2,1)S(1)} %get-tuple-element.43.refs_4_), channel_id=1, source_target_pairs={{0,2},{1,3},{2,0},{3,1},{4,6},{5,7},{6,4},{7,5},{8,10},{9,11},{10,... | collective-permute-start | bytes 331784 | tf_op jit(solution)/shard_map/ppermute | solution.py:353
  12.0 2.0 %collective-permute-done.4.refs_2_.refs_5_ = bf16[4,96,384]{2,1,0:T(8,128)(2,1)S(1)} collective-permute-done((bf16[4,96,384]{2,1,0:T(8,128)(2,1)}, bf16[4,96,384]{2,1,0:T(8,128)(2,1)S(1)}, u32[]{:S(2)}, u32[]{:S(2)}) %collective-permute-start.4) | collective-permute-done | bytes 294944 | tf_op jit(solution)/shard_map/ppermute | solution.py:353
  14.0 1.5 %shard_map.116 = (bf16[3,96,384]{2,1,0:T(8,128)(2,1)S(1)}, bf16[3,96,384]{2,1,0:T(8,128)(2,1)S(1)}) custom-call(s32[1]{0:T(128)} %bitcast.1.row_ref, bf16[18,96,384]{2,1,0:T(8,128)(2,1)} %bitcast.18, bf16[18,96,384]{2,1,0:T(8,128)(2,1)} %bitcast.22, bf16[4,96,384]{2,1,0:T(8,128)(2,1)S(1)} %collective-permute-done.4.refs_2_.refs_5_), custom_call_target="tpu_custom_call" | custom-call | tf_op jit(solution)/shard_map/pallas_call | solution.py:81
  15.5 2.0 %collective-permute-start.5 = (bf16[3,96,384]{2,1,0:T(8,128)(2,1)S(1)}, bf16[3,96,384]{2,1,0:T(8,128)(2,1)S(1)}, u32[]{:S(2)}, u32[]{:S(2)}) collective-permute-start(bf16[3,96,384]{2,1,0:T(8,128)(2,1)S(1)} %get-tuple-element.54), channel_id=1, source_target_pairs={{0,2},{1,3},{2,0},{3,1},{4,6},{5,7},{6,4},{7,5},{8,10},{9,11},{10,... | collective-permute-start | bytes 663560 | tf_op jit(solution)/shard_map/ppermute | solution.py:353
  18.1 4.9 %shard_map.115 = (s32[54]{0:T(128)S(1)}, s32[27]{0:T(128)S(1)}, f32[9]{0:T(128)S(1)}, f32[3]{0:T(128)S(1)}, bf16[9,96,384]{2,1,0:T(8,128)(2,1)S(1)}, /*index=5*/...) custom-call(s32[2]{0:T(128)S(1)} %pad_add_fusion.place_ref, s32[432]{0:T(512)S(1)} %bitcast.14, ...), custom_call_target="tpu_custom_call" | custom-call | tf_op jit(solution)/shard_map/pallas_call | solution.py:422
  24.3 5.0 %shard_map.117 = (f32[9,96,384]{2,1,0:T(8,128)S(1)}, f32[9,96,384]{2,1,0:T(8,128)S(1)}, f32[24,96,128]{2,1,0:T(8,128)S(1)}, f32[24,96,128]{2,1,0:T(8,128)S(1)}) custom-call(s32[27]{0:T(128)S(1)} %get-tuple-element.45.slot_ref, f32[9]{0:T(128)S(1)} %get-tuple-element.46.weight_ref, s32[1]{0:T(128)} %bitcast.1.row_ref, ...), custom_call_target="tpu_custom_call" | custom-call | flops 8000000000 | bytes 4000000 | tf_op jit(solution)/shard_map/pallas_call | solution.py:285
  29.3 2.3 %collective-permute-done.6.refs_6_ = bf16[3,96,384]{2,1,0:T(8,128)(2,1)S(1)} collective-permute-done((bf16[3,96,384]{2,1,0:T(8,128)(2,1)S(1)}, bf16[3,96,384]{2,1,0:T(8,128)(2,1)S(1)}, u32[]{:S(2)}, u32[]{:S(2)}) %collective-permute-start.6) | collective-permute-done | bytes 221216 | tf_op jit(solution)/shard_map/ppermute | solution.py:353
  31.7 3.9 %shard_map.118 = (f32[9,96,384]{2,1,0:T(8,128)S(1)}, f32[9,96,384]{2,1,0:T(8,128)S(1)}, f32[24,96,128]{2,1,0:T(8,128)S(1)}, f32[24,96,128]{2,1,0:T(8,128)S(1)}) custom-call(s32[27]{0:T(128)S(1)} %get-tuple-element.45.slot_ref, f32[9]{0:T(128)S(1)} %get-tuple-element.46.weight_ref, ...), custom_call_target="tpu_custom_call", output_to_operand_aliasing={{0}: (11, {}), {1}: (12, {}), {2}: (13, {}), {3}: (14, {})} | custom-call | flops 6000000000 | bytes 3000000 | tf_op jit(solution)/shard_map/pallas_call | solution.py:285
  35.6 2.4 %collective-permute-done.2.refs_6_ = bf16[2,96,384]{2,1,0:T(8,128)(2,1)S(1)} collective-permute-done((bf16[2,96,384]{2,1,0:T(8,128)(2,1)S(1)}, bf16[2,96,384]{2,1,0:T(8,128)(2,1)S(1)}, u32[]{:S(2)}, u32[]{:S(2)}) %collective-permute-start.2) | collective-permute-done | bytes 147488 | tf_op jit(solution)/shard_map/ppermute | solution.py:353
  38.0 2.2 %shard_map.119 = (f32[9,96,384]{2,1,0:T(8,128)S(1)}, f32[24,96,128]{2,1,0:T(8,128)S(1)}, bf16[24,96,128]{2,1,0:T(8,128)(2,1)S(1)}, bf16[2,224,384]{2,1,0:T(8,128)(2,1)S(1)}) custom-call(s32[27]{0:T(128)S(1)} %get-tuple-element.45.slot_ref, f32[9]{0:T(128)S(1)} %get-tuple-element.46.weight_ref, ...), custom_call_target="tpu_custom_call", output_to_operand_aliasing={{0}: (11, {}), {1}: (12, {})} | custom-call | flops 2000000000 | bytes 2000000 | tf_op jit(solution)/shard_map/pallas_call | solution.py:285
  40.4 1.7 %shard_map.120 = (f32[9,96,384]{2,1,0:T(8,128)S(1)}, f32[24,96,128]{2,1,0:T(8,128)S(1)}) custom-call(s32[27]{0:T(128)S(1)} %get-tuple-element.45.slot_ref, f32[9]{0:T(128)S(1)} %get-tuple-element.46.weight_ref, s32[1]{0:T(128)} %bitcast.1.row_ref, f32[9,24,128]{2,1,0:T(8,128)S(1)} %get-tuple-element.47.refs_0_, ...), custom_call_target="tpu_custom_call", output_to_operand_aliasing={{0}: (5, {}), {1}: (6, {})} | custom-call | flops 2000000000 | bytes 2000000 | tf_op jit(solution)/shard_map/pallas_call | solution.py:285
  42.3 4.6 %collective-permute-start.9 = (bf16[3,96,128]{2,1,0:T(8,128)(2,1)S(1)}, bf16[3,96,128]{2,1,0:T(8,128)(2,1)S(1)}, u32[]{:S(2)}, u32[]{:S(2)}) collective-permute-start(bf16[3,96,128]{2,1,0:T(8,128)(2,1)S(1)} %get-tuple-element.71), channel_id=1, source_target_pairs={{0,28},{4,24},{8,20},{12,16},{16,12},{20,8},{24,4},{28,0},{1,29},{... | collective-permute-start | bytes 221192 | tf_op jit(solution)/shard_map/ppermute | solution.py:353
  48.0 2.1 %collective-permute-start.12 = (bf16[3,96,128]{2,1,0:T(8,128)(2,1)S(1)}, bf16[3,96,128]{2,1,0:T(8,128)(2,1)S(1)}, u32[]{:S(2)}, u32[]{:S(2)}) collective-permute-start(bf16[3,96,128]{2,1,0:T(8,128)(2,1)S(1)} %get-tuple-element.74), channel_id=1, source_target_pairs={{0,16},{4,20},{8,24},{12,28},{16,0},{20,4},{24,8},{28,12},{1,17},{... | collective-permute-start | bytes 221192 | tf_op jit(solution)/shard_map/ppermute | solution.py:353
  50.0 2.2 %collective-permute-start.13 = (bf16[3,96,128]{2,1,0:T(8,128)(2,1)S(1)}, bf16[3,96,128]{2,1,0:T(8,128)(2,1)S(1)}, u32[]{:S(2)}, u32[]{:S(2)}) collective-permute-start(bf16[3,96,128]{2,1,0:T(8,128)(2,1)S(1)} %get-tuple-element.75), channel_id=1, source_target_pairs={{0,12},{4,8},{8,4},{12,0},{16,28},{20,24},{24,20},{28,16},{1,13},{... | collective-permute-start | bytes 221192 | tf_op jit(solution)/shard_map/ppermute | solution.py:353
  54.5 4.4 %collective-permute-done.11.refs_2_ = bf16[3,96,128]{2,1,0:T(8,128)(2,1)S(1)} collective-permute-done((bf16[3,96,128]{2,1,0:T(8,128)(2,1)S(1)}, bf16[3,96,128]{2,1,0:T(8,128)(2,1)S(1)}, u32[]{:S(2)}, u32[]{:S(2)}) %collective-permute-start.11) | collective-permute-done | bytes 73760 | tf_op jit(solution)/shard_map/ppermute | solution.py:353
  61.2 2.4 %collective-permute-start.21 = (bf16[3,96,128]{2,1,0:T(8,128)(2,1)S(1)}, bf16[3,96,128]{2,1,0:T(8,128)(2,1)S(1)}, u32[]{:S(2)}, u32[]{:S(2)}) collective-permute-start(bf16[3,96,128]{2,1,0:T(8,128)(2,1)S(1)} %get-tuple-element.80.refs_7_), channel_id=1, source_target_pairs={{0,8},{4,12},{8,0},{12,4},{16,24},{20,28},{24,16},{28,20},{1,9},{5... | collective-permute-start | bytes 221192 | tf_op jit(solution)/shard_map/ppermute | solution.py:353
  66.6 1.5 %collective-permute-start.22 = (bf16[3,96,128]{2,1,0:T(8,128)(2,1)S(1)}, bf16[3,96,128]{2,1,0:T(8,128)(2,1)S(1)}, u32[]{:S(2)}, u32[]{:S(2)}) collective-permute-start(bf16[3,96,128]{2,1,0:T(8,128)(2,1)S(1)} %collective-permute-done.21.refs_5_), channel_id=1, source_target_pairs={{0,4},{4,0},{8,12},{12,8},{16,20},{20,16},{24,28},{28,24},{1,5},{5... | collective-permute-start | bytes 221192 | tf_op jit(solution)/shard_map/ppermute | solution.py:353
  68.1 4.4 %collective-permute-done.19.refs_3_ = bf16[3,96,128]{2,1,0:T(8,128)(2,1)S(1)} collective-permute-done((bf16[3,96,128]{2,1,0:T(8,128)(2,1)S(1)}, bf16[3,96,128]{2,1,0:T(8,128)(2,1)S(1)}, u32[]{:S(2)}, u32[]{:S(2)}) %collective-permute-start.19) | collective-permute-done | bytes 73760 | tf_op jit(solution)/shard_map/ppermute | solution.py:353
  72.5 2.0 %collective-permute-start.18 = (bf16[3,96,128]{2,1,0:T(8,128)(2,1)S(1)}, bf16[3,96,128]{2,1,0:T(8,128)(2,1)S(1)}, u32[]{:S(2)}, u32[]{:S(2)}) collective-permute-start(bf16[3,96,128]{2,1,0:T(8,128)(2,1)S(1)} %collective-permute-done.17.refs_1_), channel_id=1, source_target_pairs={{0,4},{4,0},{8,12},{12,8},{16,20},{20,16},{24,28},{28,24},{1,5},{5... | collective-permute-start | bytes 221192 | tf_op jit(solution)/shard_map/ppermute | solution.py:353
  74.6 2.3 %collective-permute-done.20.refs_2_ = bf16[3,96,128]{2,1,0:T(8,128)(2,1)S(1)} collective-permute-done((bf16[3,96,128]{2,1,0:T(8,128)(2,1)S(1)}, bf16[3,96,128]{2,1,0:T(8,128)(2,1)S(1)}, u32[]{:S(2)}, u32[]{:S(2)}) %collective-permute-start.20) | collective-permute-done | bytes 73760 | tf_op jit(solution)/shard_map/ppermute | solution.py:353
  77.7 2.9 %shard_map.123 = bf16[18,96,384]{2,1,0:T(8,128)(2,1)} custom-call(s32[54]{0:T(128)S(1)} %get-tuple-element.44.slot_ref, s32[1]{0:T(128)} %bitcast.1.row_ref, f32[9,96,384]{2,1,0:T(8,128)S(1)} %get-tuple-element.66.own_ref, f32[9,96,384]{2,1,0:T(8,128)S(1)} %collective-permute-done.16.other_ref, bf16[3,96,128]{2,1,0:T(8,128)(2,1)S(1)} %collective-permute-done.18.refs_0_, ...), custom_call_target="tpu_custom_call" | custom-call | tf_op jit(solution)/shard_map/pallas_call | solution.py:502
  (49 shorter events, 14.9 us)
Async XLA Ops:
  2.8 5.8 %collective-permute-start = (bf16[18,96,384]{2,1,0:T(8,128)(2,1)S(1)}, bf16[18,96,384]{2,1,0:T(8,128)(2,1)S(1)}, u32[]{:S(2)}, u32[]{:S(2)}) collective-permute-start(bf16[18,96,384]{2,1,0:T(8,128)(2,1)S(1)} %get-tuple-element.42), channel_id=1, source_target_pairs={{0,1},{1,0},{2,3},{3,2},{4,5},{5,4},{6,7},{7,6},{8,9},{9,8},{10,11... | collective-permute-start | bytes 3981320 | tf_op jit(solution)/shard_map/ppermute | solution.py:353
  3.3 10.7 %collective-permute-start.4 = (bf16[4,96,384]{2,1,0:T(8,128)(2,1)}, bf16[4,96,384]{2,1,0:T(8,128)(2,1)S(1)}, u32[]{:S(2)}, u32[]{:S(2)}) collective-permute-start(bf16[4,96,384]{2,1,0:T(8,128)(2,1)} %get-tuple-element.53), channel_id=1, source_target_pairs={{0,2},{1,3},{2,0},{3,1},{4,6},{5,7},{6,4},{7,5},{8,10},{9,11},{10,... | collective-permute-start | bytes 884744 | tf_op jit(solution)/shard_map/ppermute | solution.py:353
  5.9 17.1 %collective-permute-start.7 = (bf16[4,96,384]{2,1,0:T(8,128)(2,1)S(1)}, bf16[4,96,384]{2,1,0:T(8,128)(2,1)S(1)}, u32[]{:S(2)}, u32[]{:S(2)}) collective-permute-start(bf16[4,96,384]{2,1,0:T(8,128)(2,1)S(1)} %get-tuple-element.56), channel_id=1, source_target_pairs={{0,3},{1,2},{2,1},{3,0},{4,7},{5,6},{6,5},{7,4},{8,11},{9,10},{10,... | collective-permute-start | bytes 884744 | tf_op jit(solution)/shard_map/ppermute | solution.py:353
  10.1 14.2 %collective-permute-start.3 = (bf16[9,16,384]{2,1,0:T(8,128)(2,1)S(1)}, bf16[9,16,384]{2,1,0:T(8,128)(2,1)S(1)}, u32[]{:S(2)}, u32[]{:S(2)}) collective-permute-start(bf16[9,16,384]{2,1,0:T(8,128)(2,1)S(1)} %get-tuple-element.43.refs_4_), channel_id=1, source_target_pairs={{0,2},{1,3},{2,0},{3,1},{4,6},{5,7},{6,4},{7,5},{8,10},{9,11},{10,... | collective-permute-start | bytes 331784 | tf_op jit(solution)/shard_map/ppermute | solution.py:353
  15.5 13.8 %collective-permute-start.5 = (bf16[3,96,384]{2,1,0:T(8,128)(2,1)S(1)}, bf16[3,96,384]{2,1,0:T(8,128)(2,1)S(1)}, u32[]{:S(2)}, u32[]{:S(2)}) collective-permute-start(bf16[3,96,384]{2,1,0:T(8,128)(2,1)S(1)} %get-tuple-element.54), channel_id=1, source_target_pairs={{0,2},{1,3},{2,0},{3,1},{4,6},{5,7},{6,4},{7,5},{8,10},{9,11},{10,... | collective-permute-start | bytes 663560 | tf_op jit(solution)/shard_map/ppermute | solution.py:353
  17.6 14.1 %collective-permute-start.6 = (bf16[3,96,384]{2,1,0:T(8,128)(2,1)S(1)}, bf16[3,96,384]{2,1,0:T(8,128)(2,1)S(1)}, u32[]{:S(2)}, u32[]{:S(2)}) collective-permute-start(bf16[3,96,384]{2,1,0:T(8,128)(2,1)S(1)} %get-tuple-element.55), channel_id=1, source_target_pairs={{0,3},{1,2},{2,1},{3,0},{4,7},{5,6},{6,5},{7,4},{8,11},{9,10},{10,... | collective-permute-start | bytes 663560 | tf_op jit(solution)/shard_map/ppermute | solution.py:353
  17.6 18.0 %collective-permute-start.1 = (bf16[2,96,384]{2,1,0:T(8,128)(2,1)S(1)}, bf16[2,96,384]{2,1,0:T(8,128)(2,1)S(1)}, u32[]{:S(2)}, u32[]{:S(2)}) collective-permute-start(bf16[2,96,384]{2,1,0:T(8,128)(2,1)S(1)} %get-tuple-element.51), channel_id=1, source_target_pairs={{0,2},{1,3},{2,0},{3,1},{4,6},{5,7},{6,4},{7,5},{8,10},{9,11},{10,... | collective-permute-start | bytes 442376 | tf_op jit(solution)/shard_map/ppermute | solution.py:353
  23.0 14.9 %collective-permute-start.2 = (bf16[2,96,384]{2,1,0:T(8,128)(2,1)S(1)}, bf16[2,96,384]{2,1,0:T(8,128)(2,1)S(1)}, u32[]{:S(2)}, u32[]{:S(2)}) collective-permute-start(bf16[2,96,384]{2,1,0:T(8,128)(2,1)S(1)} %get-tuple-element.52), channel_id=1, source_target_pairs={{0,3},{1,2},{2,1},{3,0},{4,7},{5,6},{6,5},{7,4},{8,11},{9,10},{10,... | collective-permute-start | bytes 442376 | tf_op jit(solution)/shard_map/ppermute | solution.py:353
  40.2 2.1 %collective-permute-start.8 = (bf16[24,96,128]{2,1,0:T(8,128)(2,1)S(1)}, bf16[24,96,128]{2,1,0:T(8,128)(2,1)S(1)}, u32[]{:S(2)}, u32[]{:S(2)}) collective-permute-start(bf16[24,96,128]{2,1,0:T(8,128)(2,1)S(1)} %get-tuple-element.70), channel_id=1, source_target_pairs={{0,1},{1,0},{2,3},{3,2},{4,5},{5,4},{6,7},{7,6},{8,9},{9,8},{10,11... | collective-permute-start | bytes 1769480 | tf_op jit(solution)/shard_map/ppermute | solution.py:353
  42.3 9.9 %collective-permute-start.9 = (bf16[3,96,128]{2,1,0:T(8,128)(2,1)S(1)}, bf16[3,96,128]{2,1,0:T(8,128)(2,1)S(1)}, u32[]{:S(2)}, u32[]{:S(2)}) collective-permute-start(bf16[3,96,128]{2,1,0:T(8,128)(2,1)S(1)} %get-tuple-element.71), channel_id=1, source_target_pairs={{0,28},{4,24},{8,20},{12,16},{16,12},{20,8},{24,4},{28,0},{1,29},{... | collective-permute-start | bytes 221192 | tf_op jit(solution)/shard_map/ppermute | solution.py:353
  47.0 7.0 %collective-permute-start.10 = (bf16[3,96,128]{2,1,0:T(8,128)(2,1)S(1)}, bf16[3,96,128]{2,1,0:T(8,128)(2,1)S(1)}, u32[]{:S(2)}, u32[]{:S(2)}) collective-permute-start(bf16[3,96,128]{2,1,0:T(8,128)(2,1)S(1)} %get-tuple-element.72), channel_id=1, source_target_pairs={{0,24},{4,28},{8,16},{12,20},{16,8},{20,12},{24,0},{28,4},{1,25},{... | collective-permute-start | bytes 221192 | tf_op jit(solution)/shard_map/ppermute | solution.py:353
  47.2 11.7 %collective-permute-start.11 = (bf16[3,96,128]{2,1,0:T(8,128)(2,1)S(1)}, bf16[3,96,128]{2,1,0:T(8,128)(2,1)S(1)}, u32[]{:S(2)}, u32[]{:S(2)}) collective-permute-start(bf16[3,96,128]{2,1,0:T(8,128)(2,1)S(1)} %get-tuple-element.73), channel_id=1, source_target_pairs={{0,20},{4,16},{8,28},{12,24},{16,4},{20,0},{24,12},{28,8},{1,21},{... | collective-permute-start | bytes 221192 | tf_op jit(solution)/shard_map/ppermute | solution.py:353
  48.0 11.9 %collective-permute-start.12 = (bf16[3,96,128]{2,1,0:T(8,128)(2,1)S(1)}, bf16[3,96,128]{2,1,0:T(8,128)(2,1)S(1)}, u32[]{:S(2)}, u32[]{:S(2)}) collective-permute-start(bf16[3,96,128]{2,1,0:T(8,128)(2,1)S(1)} %get-tuple-element.74), channel_id=1, source_target_pairs={{0,16},{4,20},{8,24},{12,28},{16,0},{20,4},{24,8},{28,12},{1,17},{... | collective-permute-start | bytes 221192 | tf_op jit(solution)/shard_map/ppermute | solution.py:353
  50.0 9.9 %collective-permute-start.13 = (bf16[3,96,128]{2,1,0:T(8,128)(2,1)S(1)}, bf16[3,96,128]{2,1,0:T(8,128)(2,1)S(1)}, u32[]{:S(2)}, u32[]{:S(2)}) collective-permute-start(bf16[3,96,128]{2,1,0:T(8,128)(2,1)S(1)} %get-tuple-element.75), channel_id=1, source_target_pairs={{0,12},{4,8},{8,4},{12,0},{16,28},{20,24},{24,20},{28,16},{1,13},{... | collective-permute-start | bytes 221192 | tf_op jit(solution)/shard_map/ppermute | solution.py:353
  52.3 7.6 %collective-permute-start.14 = (bf16[3,96,128]{2,1,0:T(8,128)(2,1)S(1)}, bf16[3,96,128]{2,1,0:T(8,128)(2,1)S(1)}, u32[]{:S(2)}, u32[]{:S(2)}) collective-permute-start(bf16[3,96,128]{2,1,0:T(8,128)(2,1)S(1)} %get-tuple-element.76), channel_id=1, source_target_pairs={{0,8},{4,12},{8,0},{12,4},{16,24},{20,28},{24,16},{28,20},{1,9},{5... | collective-permute-start | bytes 221192 | tf_op jit(solution)/shard_map/ppermute | solution.py:353
  53.9 6.0 %collective-permute-start.15 = (bf16[3,96,128]{2,1,0:T(8,128)(2,1)S(1)}, bf16[3,96,128]{2,1,0:T(8,128)(2,1)S(1)}, u32[]{:S(2)}, u32[]{:S(2)}) collective-permute-start(bf16[3,96,128]{2,1,0:T(8,128)(2,1)S(1)} %get-tuple-element.77), channel_id=1, source_target_pairs={{0,4},{4,0},{8,12},{12,8},{16,20},{20,16},{24,28},{28,24},{1,5},{5... | collective-permute-start | bytes 221192 | tf_op jit(solution)/shard_map/ppermute | solution.py:353
  61.2 16.5 %collective-permute-start.16 = (f32[9,96,384]{2,1,0:T(8,128)S(1)}, f32[9,96,384]{2,1,0:T(8,128)S(1)}, u32[]{:S(2)}, u32[]{:S(2)}) collective-permute-start(f32[9,96,384]{2,1,0:T(8,128)S(1)} %get-tuple-element.79), channel_id=1, source_target_pairs={{0,1},{1,0},{2,3},{3,2},{4,5},{5,4},{6,7},{7,6},{8,9},{9,8},{10,11... | collective-permute-start | bytes 3981320 | tf_op jit(solution)/shard_map/ppermute | solution.py:353
  61.2 5.4 %collective-permute-start.21 = (bf16[3,96,128]{2,1,0:T(8,128)(2,1)S(1)}, bf16[3,96,128]{2,1,0:T(8,128)(2,1)S(1)}, u32[]{:S(2)}, u32[]{:S(2)}) collective-permute-start(bf16[3,96,128]{2,1,0:T(8,128)(2,1)S(1)} %get-tuple-element.80.refs_7_), channel_id=1, source_target_pairs={{0,8},{4,12},{8,0},{12,4},{16,24},{20,28},{24,16},{28,20},{1,9},{5... | collective-permute-start | bytes 221192 | tf_op jit(solution)/shard_map/ppermute | solution.py:353
  63.6 8.9 %collective-permute-start.19 = (bf16[3,96,128]{2,1,0:T(8,128)(2,1)S(1)}, bf16[3,96,128]{2,1,0:T(8,128)(2,1)S(1)}, u32[]{:S(2)}, u32[]{:S(2)}) collective-permute-start(bf16[3,96,128]{2,1,0:T(8,128)(2,1)S(1)} %get-tuple-element.80.refs_7_), channel_id=1, source_target_pairs={{0,16},{4,20},{8,24},{12,28},{16,0},{20,4},{24,8},{28,12},{1,17},{... | collective-permute-start | bytes 221192 | tf_op jit(solution)/shard_map/ppermute | solution.py:353
  65.0 7.5 %collective-permute-start.17 = (bf16[3,96,128]{2,1,0:T(8,128)(2,1)S(1)}, bf16[3,96,128]{2,1,0:T(8,128)(2,1)S(1)}, u32[]{:S(2)}, u32[]{:S(2)}) collective-permute-start(bf16[3,96,128]{2,1,0:T(8,128)(2,1)S(1)} %get-tuple-element.80.refs_7_), channel_id=1, source_target_pairs={{0,24},{4,28},{8,16},{12,20},{16,8},{20,12},{24,0},{28,4},{1,25},{... | collective-permute-start | bytes 221192 | tf_op jit(solution)/shard_map/ppermute | solution.py:353
  66.0 8.5 %collective-permute-start.23 = (bf16[3,96,128]{2,1,0:T(8,128)(2,1)S(1)}, bf16[3,96,128]{2,1,0:T(8,128)(2,1)S(1)}, u32[]{:S(2)}, u32[]{:S(2)}) collective-permute-start(bf16[3,96,128]{2,1,0:T(8,128)(2,1)S(1)} %get-tuple-element.80.refs_7_), channel_id=1, source_target_pairs={{0,4},{4,0},{8,12},{12,8},{16,20},{20,16},{24,28},{28,24},{1,5},{5... | collective-permute-start | bytes 221192 | tf_op jit(solution)/shard_map/ppermute | solution.py:353
  66.6 8.0 %collective-permute-start.22 = (bf16[3,96,128]{2,1,0:T(8,128)(2,1)S(1)}, bf16[3,96,128]{2,1,0:T(8,128)(2,1)S(1)}, u32[]{:S(2)}, u32[]{:S(2)}) collective-permute-start(bf16[3,96,128]{2,1,0:T(8,128)(2,1)S(1)} %collective-permute-done.21.refs_5_), channel_id=1, source_target_pairs={{0,4},{4,0},{8,12},{12,8},{16,20},{20,16},{24,28},{28,24},{1,5},{5... | collective-permute-start | bytes 221192 | tf_op jit(solution)/shard_map/ppermute | solution.py:353
  72.5 4.4 %collective-permute-start.20 = (bf16[3,96,128]{2,1,0:T(8,128)(2,1)S(1)}, bf16[3,96,128]{2,1,0:T(8,128)(2,1)S(1)}, u32[]{:S(2)}, u32[]{:S(2)}) collective-permute-start(bf16[3,96,128]{2,1,0:T(8,128)(2,1)S(1)} %collective-permute-done.19.refs_3_), channel_id=1, source_target_pairs={{0,4},{4,0},{8,12},{12,8},{16,20},{20,16},{24,28},{28,24},{1,5},{5... | collective-permute-start | bytes 221192 | tf_op jit(solution)/shard_map/ppermute | solution.py:353
  72.5 5.1 %collective-permute-start.18 = (bf16[3,96,128]{2,1,0:T(8,128)(2,1)S(1)}, bf16[3,96,128]{2,1,0:T(8,128)(2,1)S(1)}, u32[]{:S(2)}, u32[]{:S(2)}) collective-permute-start(bf16[3,96,128]{2,1,0:T(8,128)(2,1)S(1)} %collective-permute-done.17.refs_1_), channel_id=1, source_target_pairs={{0,4},{4,0},{8,12},{12,8},{16,20},{20,16},{24,28},{28,24},{1,5},{5... | collective-permute-start | bytes 221192 | tf_op jit(solution)/shard_map/ppermute | solution.py:353
  (5 other events, 30.6 us)

commit v5 on v4

--- a/solution.py
+++ b/solution.py
@@ -309,7 +309,11 @@
     each = part_refs[0].shape[0]
     for m, part in enumerate(part_refs):
         boxes = slice(each * m, each * (m + 1))
-        part[...] = (own_ref[boxes] + other_ref[boxes].astype(F32)).astype(BF16)
+        part[...] = (own_ref[boxes] + other_ref[boxes].astype(F32)).astype(part.dtype)
+
+
+def add_kernel(own_ref, other_ref, total_ref):
+    total_ref[...] = (own_ref[...] + other_ref[...].astype(F32)).astype(BF16)
 
 
 def template_kernel(denom_ref, _, *refs):
@@ -323,29 +327,36 @@
         coadd_ref[:, TILE * q : TILE * (q + 1)] = box
 
 
-def difference_kernel(slot_ref, row_ref, own_ref, other_ref, *refs, masks):
-    template_refs, out_ref, held = refs[:-2], refs[-2], refs[-1]
-    step = pl.program_id(0)
+def difference_kernel(slot_ref, row_ref, own_ref, other_ref, *refs, group):
+    template_refs, out_ref = refs[:-4], refs[-4]
+    held, ready, sems = refs[-3:]
     each = template_refs[0].shape[0]
-    count, _, side = own_ref.shape
+    half, _, side = own_ref.shape
     tiles = side // TILE
-
-    @pl.when(step == 0)
-    def _():
-        for m, template in zip(masks, template_refs):
-            held[each * m : each * (m + 1)] = template[...]
-
-    def subtract(matched_ref):
-        for i in range(count):
-            for q in range(tiles):
-                slot = slot_ref[(step * count + i) * tiles + q]
-                columns = slice(TILE * q, TILE * (q + 1))
-                box = held[slot].astype(F32)
-                out_ref[i, :, columns] = (matched_ref[i, :, columns] - box).astype(BF16)
-
-    mine = (step * 2 // pl.num_programs(0)) == (row_ref[0] & 1)
-    pl.when(mine)(lambda: subtract(own_ref))
-    pl.when(jnp.logical_not(mine))(lambda: subtract(other_ref))
+    core = row_ref[0] & 1
+    for m, template in enumerate(template_refs):
+        held[each * m : each * (m + 1)] = template[...]
+    copies = []
+    for which, matched_ref in enumerate((own_ref, other_ref)):
+        for first in range(0, half, group):
+            at = (core ^ which) * half + first
+            for i in range(group):
+                for q in range(tiles):
+                    slot = slot_ref[(at + i) * tiles + q]
+                    columns = slice(TILE * q, TILE * (q + 1))
+                    box = held[slot].astype(F32)
+                    value = (matched_ref[first + i, :, columns] - box).astype(BF16)
+                    ready[which * half + first + i, :, columns] = value
+            copies.append(
+                pltpu.make_async_copy(
+                    ready.at[pl.ds(which * half + first, group)],
+                    out_ref.at[pl.ds(at, group)],
+                    sems.at[len(copies)],
+                )
+            )
+            copies[-1].start()
+    for copy in copies:
+        copy.wait()
 
 
 def exchange(value, axis, mask):
@@ -465,14 +476,26 @@
         merge_kernel,
         in_specs=[in_vmem] * 2,
         out_specs=[in_vmem] * det_devices,
-        out_shape=[box] * det_devices,
+        out_shape=[
+            jax.ShapeDtypeStruct(box_shape, BF16 if m % 2 else F32) for m in range(det_devices)
+        ],
         compiler_params=small,
     )(own_sums, other_sums)
-    masks = tuple(range(det_devices - 1, 0, -1)) + (0,)
-    received = [exchange(parts[m], "det", m) if m else parts[m] for m in masks]
+    evens = tuple(range(det_devices - 2, 0, -2))
+    across = {m: exchange(parts[m ^ 1], "det", 1) for m in evens + (0,)}
+    received = [parts[0], across[0]]
+    for m in evens:
+        total = pl.pallas_call(
+            add_kernel,
+            in_specs=[in_vmem] * 2,
+            out_specs=in_vmem,
+            out_shape=box,
+            compiler_params=small,
+        )(parts[m], across[m])
+        received.append(exchange(total, "det", m))
     template, coadd, matched_sent = pl.pallas_call(
         template_kernel,
-        in_specs=[pl.BlockSpec(memory_space=pltpu.SMEM), anywhere] + [in_vmem] * det_devices,
+        in_specs=[pl.BlockSpec(memory_space=pltpu.SMEM), anywhere] + [in_vmem] * len(received),
         out_specs=[in_vmem] * 2 + [anywhere],
         out_shape=[
             box,
@@ -483,32 +506,22 @@
         compiler_params=small,
     )(denom, matched_sent, *received)
     other_matched = exchange(matched_sent, "row", 1)
-    evens = tuple(range(det_devices - 2, 0, -2))
     passed = {0: template}
     for m in evens:
         passed[m] = exchange(template, "det", m)
     for m in evens + (0,):
         passed[m ^ 1] = exchange(passed[m], "det", 1)
-    templates = [passed[m] for m in masks]
+    templates = [passed[m] for m in range(det_devices)]
     group = 3 if half % 3 == 0 else 1
-    steps = half // group
-
-    def half_block(which):
-        def place(i, slot, row):
-            return (jnp.clip(i - ((row[0] & 1) ^ which) * steps, 0, steps - 1), 0, 0)
-
-        return pl.BlockSpec((group, band, side), place)
-
     difference = pl.pallas_call(
-        functools.partial(difference_kernel, masks=masks),
-        grid_spec=pltpu.PrefetchScalarGridSpec(
-            num_scalar_prefetch=2,
-            grid=(2 * steps,),
-            in_specs=[half_block(0), half_block(1)]
-            + [pl.BlockSpec(box_shape, lambda i, *_: (0, 0, 0))] * det_devices,
-            out_specs=pl.BlockSpec((group, band, side), lambda i, *_: (i, 0, 0)),
-            scratch_shapes=[pltpu.VMEM((slot_count, band, TILE), BF16)],
-        ),
+        functools.partial(difference_kernel, group=group),
+        in_specs=[pl.BlockSpec(memory_space=pltpu.SMEM)] * 2 + [in_vmem] * (2 + det_devices),
+        out_specs=anywhere,
+        scratch_shapes=[
+            pltpu.VMEM((slot_count, band, TILE), BF16),
+            pltpu.VMEM((image_count, band, side), BF16),
+            pltpu.SemaphoreType.DMA((image_count // group,)),
+        ],
         out_shape=jax.ShapeDtypeStruct((image_count, band, side), BF16),
         compiler_params=small,
     )(slots, row_one, matched, other_matched, *templates)

time: 81 us -> 76.1 us (0.940)
  waiting for transfers between devices: 20.8 us -> 17.2 us
  Pallas kernels: 27.1 us -> 25.9 us
    ppermute x24, waiting for transfers between devices: 20.8 us -> 17.2 us  [exchange(): return lax.ppermute(value, axis, [(i, i ^ mask) for i in range(size)])]
    pallas_call x1 -> x4, Pallas kernels: 2.94 us -> 1.78 us  [the longest x1 1.73 us: per_device(): pl.pallas_call(functools.partial(difference_kernel, group=group), in_spec...]
  transfers between devices with their start and end apart: 24 -> 24, of which waited for: 10 -> 12; matrix products, arithmetic and copies ran while one was open for 3% -> 3% of each run, Pallas kernels for 23% -> 24%
where the time goes in v5:
time: 76.1 us; the launch traced here: 75.8 us
  starting transfers between devices  29.2 us (38%)
  Pallas kernels  25.9 us (34%)
  waiting for transfers between devices  17.2 us (23%)
  local copies, waits for them, and re-layouts  1.55 us (2%)
  matrix products  1.05 us (1%)
  between operations  0.78 us (1%)
    ppermute x24, starting transfers between devices, exchange(): return lax.ppermute(value, axis, [(i, i ^ mask) for i in range(size)])  29.2 us
    ppermute x24, waiting for transfers between devices, exchange(): return lax.ppermute(value, axis, [(i, i ^ mask) for i in range(size)])  17.2 us
    pallas_call x4, Pallas kernels, match_chunk(): pl.pallas_call(functools.partial(match_kernel, start=start, count=count,...  12.7 us
    pallas_call x3, Pallas kernels, pack(): pl.pallas_call(functools.partial(pack_kernel, chunks=chunks, siblings=sib...  5.19 us
    pallas_call x1, Pallas kernels, per_device(): pl.pallas_call(functools.partial(target_kernel, tiles=tiles), in_specs=[p...  4.88 us
    pallas_call x1, Pallas kernels, per_device(): pl.pallas_call(functools.partial(difference_kernel, group=group), in_spec...  1.73 us
  transfers between devices with their start and end apart: 24, of which 12 were waited for; matrix products, arithmetic and copies ran while one was open for 3% of the time, Pallas kernels for 24%

profile of v5, /device:TPU:0, one launch (start us, length us, event | category | flops | bytes accessed | tf_op | source)
XLA Modules:
  0.0 75.8 jit_solution(16476787544951754419)
XLA Ops:
  0.6 2.2 %shard_map.113 = (bf16[18,96,384]{2,1,0:T(8,128)(2,1)S(1)}, bf16[4,96,384]{2,1,0:T(8,128)(2,1)}, bf16[4,96,384]{2,1,0:T(8,128)(2,1)S(1)}) custom-call(s32[1]{0:T(128)} %bitcast.1.row_ref, bf16[18,96,384]{2,1,0:T(8,128)(2,1)} %bitcast.16, bf16[18,96,384]{2,1,0:T(8,128)(2,1)} %bitcast.20), custom_call_target="tpu_custom_call" | custom-call | tf_op jit(solution)/shard_map/pallas_call | solution.py:81
  3.3 2.6 %collective-permute-start.4 = (bf16[4,96,384]{2,1,0:T(8,128)(2,1)}, bf16[4,96,384]{2,1,0:T(8,128)(2,1)S(1)}, u32[]{:S(2)}, u32[]{:S(2)}) collective-permute-start(bf16[4,96,384]{2,1,0:T(8,128)(2,1)} %get-tuple-element.53), channel_id=1, source_target_pairs={{0,2},{1,3},{2,0},{3,1},{4,6},{5,7},{6,4},{7,5},{8,10},{9,11},{10,... | collective-permute-start | bytes 884744 | tf_op jit(solution)/shard_map/ppermute | solution.py:364
  10.1 1.8 %collective-permute-start.3 = (bf16[9,16,384]{2,1,0:T(8,128)(2,1)S(1)}, bf16[9,16,384]{2,1,0:T(8,128)(2,1)S(1)}, u32[]{:S(2)}, u32[]{:S(2)}) collective-permute-start(bf16[9,16,384]{2,1,0:T(8,128)(2,1)S(1)} %get-tuple-element.43.refs_4_), channel_id=1, source_target_pairs={{0,2},{1,3},{2,0},{3,1},{4,6},{5,7},{6,4},{7,5},{8,10},{9,11},{10,... | collective-permute-start | bytes 331784 | tf_op jit(solution)/shard_map/ppermute | solution.py:364
  12.0 2.0 %collective-permute-done.4.refs_2_.refs_5_ = bf16[4,96,384]{2,1,0:T(8,128)(2,1)S(1)} collective-permute-done((bf16[4,96,384]{2,1,0:T(8,128)(2,1)}, bf16[4,96,384]{2,1,0:T(8,128)(2,1)S(1)}, u32[]{:S(2)}, u32[]{:S(2)}) %collective-permute-start.4) | collective-permute-done | bytes 294944 | tf_op jit(solution)/shard_map/ppermute | solution.py:364
  15.5 2.0 %collective-permute-start.5 = (bf16[3,96,384]{2,1,0:T(8,128)(2,1)S(1)}, bf16[3,96,384]{2,1,0:T(8,128)(2,1)S(1)}, u32[]{:S(2)}, u32[]{:S(2)}) collective-permute-start(bf16[3,96,384]{2,1,0:T(8,128)(2,1)S(1)} %get-tuple-element.54), channel_id=1, source_target_pairs={{0,2},{1,3},{2,0},{3,1},{4,6},{5,7},{6,4},{7,5},{8,10},{9,11},{10,... | collective-permute-start | bytes 663560 | tf_op jit(solution)/shard_map/ppermute | solution.py:364
  18.1 4.9 %shard_map.115 = (s32[54]{0:T(128)S(1)}, s32[27]{0:T(128)S(1)}, f32[9]{0:T(128)S(1)}, f32[3]{0:T(128)S(1)}, bf16[9,96,384]{2,1,0:T(8,128)(2,1)S(1)}, /*index=5*/...) custom-call(s32[2]{0:T(128)S(1)} %pad_add_fusion.place_ref, s32[432]{0:T(512)S(1)} %bitcast.14, ...), custom_call_target="tpu_custom_call" | custom-call | tf_op jit(solution)/shard_map/pallas_call | solution.py:433
  24.3 5.0 %shard_map.117 = (f32[9,96,384]{2,1,0:T(8,128)S(1)}, f32[9,96,384]{2,1,0:T(8,128)S(1)}, f32[24,96,128]{2,1,0:T(8,128)S(1)}, f32[24,96,128]{2,1,0:T(8,128)S(1)}) custom-call(s32[27]{0:T(128)S(1)} %get-tuple-element.45.slot_ref, f32[9]{0:T(128)S(1)} %get-tuple-element.46.weight_ref, s32[1]{0:T(128)} %bitcast.1.row_ref, ...), custom_call_target="tpu_custom_call" | custom-call | flops 8000000000 | bytes 4000000 | tf_op jit(solution)/shard_map/pallas_call | solution.py:285
  29.4 2.3 %collective-permute-done.6.refs_6_ = bf16[3,96,384]{2,1,0:T(8,128)(2,1)S(1)} collective-permute-done((bf16[3,96,384]{2,1,0:T(8,128)(2,1)S(1)}, bf16[3,96,384]{2,1,0:T(8,128)(2,1)S(1)}, u32[]{:S(2)}, u32[]{:S(2)}) %collective-permute-start.6) | collective-permute-done | bytes 221216 | tf_op jit(solution)/shard_map/ppermute | solution.py:364
  31.7 3.9 %shard_map.118 = (f32[9,96,384]{2,1,0:T(8,128)S(1)}, f32[9,96,384]{2,1,0:T(8,128)S(1)}, f32[24,96,128]{2,1,0:T(8,128)S(1)}, f32[24,96,128]{2,1,0:T(8,128)S(1)}) custom-call(s32[27]{0:T(128)S(1)} %get-tuple-element.45.slot_ref, f32[9]{0:T(128)S(1)} %get-tuple-element.46.weight_ref, ...), custom_call_target="tpu_custom_call", output_to_operand_aliasing={{0}: (11, {}), {1}: (12, {}), {2}: (13, {}), {3}: (14, {})} | custom-call | flops 6000000000 | bytes 3000000 | tf_op jit(solution)/shard_map/pallas_call | solution.py:285
  35.5 2.4 %collective-permute-done.2.refs_6_ = bf16[2,96,384]{2,1,0:T(8,128)(2,1)S(1)} collective-permute-done((bf16[2,96,384]{2,1,0:T(8,128)(2,1)S(1)}, bf16[2,96,384]{2,1,0:T(8,128)(2,1)S(1)}, u32[]{:S(2)}, u32[]{:S(2)}) %collective-permute-start.2) | collective-permute-done | bytes 147488 | tf_op jit(solution)/shard_map/ppermute | solution.py:364
  38.0 2.2 %shard_map.119 = (f32[9,96,384]{2,1,0:T(8,128)S(1)}, f32[24,96,128]{2,1,0:T(8,128)S(1)}, bf16[24,96,128]{2,1,0:T(8,128)(2,1)S(1)}, bf16[2,224,384]{2,1,0:T(8,128)(2,1)S(1)}) custom-call(s32[27]{0:T(128)S(1)} %get-tuple-element.45.slot_ref, f32[9]{0:T(128)S(1)} %get-tuple-element.46.weight_ref, ...), custom_call_target="tpu_custom_call", output_to_operand_aliasing={{0}: (11, {}), {1}: (12, {})} | custom-call | flops 2000000000 | bytes 2000000 | tf_op jit(solution)/shard_map/pallas_call | solution.py:285
  40.4 1.7 %shard_map.120 = (f32[9,96,384]{2,1,0:T(8,128)S(1)}, f32[24,96,128]{2,1,0:T(8,128)S(1)}) custom-call(s32[27]{0:T(128)S(1)} %get-tuple-element.45.slot_ref, f32[9]{0:T(128)S(1)} %get-tuple-element.46.weight_ref, s32[1]{0:T(128)} %bitcast.1.row_ref, f32[9,24,128]{2,1,0:T(8,128)S(1)} %get-tuple-element.47.refs_0_, ...), custom_call_target="tpu_custom_call", output_to_operand_aliasing={{0}: (5, {}), {1}: (6, {})} | custom-call | flops 2000000000 | bytes 2000000 | tf_op jit(solution)/shard_map/pallas_call | solution.py:285
  42.3 1.6 %collective-permute-start.10 = (bf16[3,96,128]{2,1,0:T(8,128)(2,1)S(1)}, bf16[3,96,128]{2,1,0:T(8,128)(2,1)S(1)}, u32[]{:S(2)}, u32[]{:S(2)}) collective-permute-start(bf16[3,96,128]{2,1,0:T(8,128)(2,1)S(1)} %get-tuple-element.74), channel_id=1, source_target_pairs={{0,4},{4,0},{8,12},{12,8},{16,20},{20,16},{24,28},{28,24},{1,5},{5... | collective-permute-start | bytes 221192 | tf_op jit(solution)/shard_map/ppermute | solution.py:364
  44.4 1.5 %collective-permute-start.14 = (bf16[3,96,128]{2,1,0:T(8,128)(2,1)S(1)}, bf16[3,96,128]{2,1,0:T(8,128)(2,1)S(1)}, u32[]{:S(2)}, u32[]{:S(2)}) collective-permute-start(bf16[3,96,128]{2,1,0:T(8,128)(2,1)S(1)} %get-tuple-element.78), channel_id=1, source_target_pairs={{0,4},{4,0},{8,12},{12,8},{16,20},{20,16},{24,28},{28,24},{1,5},{5... | collective-permute-start | bytes 221192 | tf_op jit(solution)/shard_map/ppermute | solution.py:364
  47.1 3.9 %collective-permute-start.11 = (bf16[3,96,128]{2,1,0:T(8,128)(2,1)S(1)}, bf16[3,96,128]{2,1,0:T(8,128)(2,1)S(1)}, u32[]{:S(2)}, u32[]{:S(2)}) collective-permute-start(bf16[3,96,128]{2,1,0:T(8,128)(2,1)S(1)} %shard_map.122), channel_id=1, source_target_pairs={{0,24},{4,28},{8,16},{12,20},{16,8},{20,12},{24,0},{28,4},{1,25},{... | collective-permute-start | bytes 221192 | tf_op jit(solution)/shard_map/ppermute | solution.py:364
  51.8 1.6 %collective-permute-start.15 = (bf16[3,96,128]{2,1,0:T(8,128)(2,1)S(1)}, bf16[3,96,128]{2,1,0:T(8,128)(2,1)S(1)}, u32[]{:S(2)}, u32[]{:S(2)}) collective-permute-start(bf16[3,96,128]{2,1,0:T(8,128)(2,1)S(1)} %shard_map.124), channel_id=1, source_target_pairs={{0,8},{4,12},{8,0},{12,4},{16,24},{20,28},{24,16},{28,20},{1,9},{5... | collective-permute-start | bytes 221192 | tf_op jit(solution)/shard_map/ppermute | solution.py:364
  54.2 2.6 %collective-permute-done.13.refs_3_ = bf16[3,96,128]{2,1,0:T(8,128)(2,1)S(1)} collective-permute-done((bf16[3,96,128]{2,1,0:T(8,128)(2,1)S(1)}, bf16[3,96,128]{2,1,0:T(8,128)(2,1)S(1)}, u32[]{:S(2)}, u32[]{:S(2)}) %collective-permute-start.13) | collective-permute-done | bytes 73760 | tf_op jit(solution)/shard_map/ppermute | solution.py:364
  58.4 2.9 %collective-permute-start.22 = (bf16[3,96,128]{2,1,0:T(8,128)(2,1)S(1)}, bf16[3,96,128]{2,1,0:T(8,128)(2,1)S(1)}, u32[]{:S(2)}, u32[]{:S(2)}) collective-permute-start(bf16[3,96,128]{2,1,0:T(8,128)(2,1)S(1)} %get-tuple-element.80.refs_0_), channel_id=1, source_target_pairs={{0,24},{4,28},{8,16},{12,20},{16,8},{20,12},{24,0},{28,4},{1,25},{... | collective-permute-start | bytes 221192 | tf_op jit(solution)/shard_map/ppermute | solution.py:364
  61.2 1.5 %collective-permute-start.18 = (bf16[3,96,128]{2,1,0:T(8,128)(2,1)S(1)}, bf16[3,96,128]{2,1,0:T(8,128)(2,1)S(1)}, u32[]{:S(2)}, u32[]{:S(2)}) collective-permute-start(bf16[3,96,128]{2,1,0:T(8,128)(2,1)S(1)} %get-tuple-element.80.refs_0_), channel_id=1, source_target_pairs={{0,8},{4,12},{8,0},{12,4},{16,24},{20,28},{24,16},{28,20},{1,9},{5... | collective-permute-start | bytes 221192 | tf_op jit(solution)/shard_map/ppermute | solution.py:364
  62.7 1.7 %collective-permute-start.17 = (bf16[3,96,128]{2,1,0:T(8,128)(2,1)S(1)}, bf16[3,96,128]{2,1,0:T(8,128)(2,1)S(1)}, u32[]{:S(2)}, u32[]{:S(2)}) collective-permute-start(bf16[3,96,128]{2,1,0:T(8,128)(2,1)S(1)} %get-tuple-element.80.refs_0_), channel_id=1, source_target_pairs={{0,4},{4,0},{8,12},{12,8},{16,20},{20,16},{24,28},{28,24},{1,5},{5... | collective-permute-start | bytes 221192 | tf_op jit(solution)/shard_map/ppermute | solution.py:364
  65.2 1.7 %collective-permute-start.23 = (bf16[3,96,128]{2,1,0:T(8,128)(2,1)S(1)}, bf16[3,96,128]{2,1,0:T(8,128)(2,1)S(1)}, u32[]{:S(2)}, u32[]{:S(2)}) collective-permute-start(bf16[3,96,128]{2,1,0:T(8,128)(2,1)S(1)} %collective-permute-done.22.refs_6_), channel_id=1, source_target_pairs={{0,4},{4,0},{8,12},{12,8},{16,20},{20,16},{24,28},{28,24},{1,5},{5... | collective-permute-start | bytes 221192 | tf_op jit(solution)/shard_map/ppermute | solution.py:364
  68.0 1.7 %collective-permute-start.21 = (bf16[3,96,128]{2,1,0:T(8,128)(2,1)S(1)}, bf16[3,96,128]{2,1,0:T(8,128)(2,1)S(1)}, u32[]{:S(2)}, u32[]{:S(2)}) collective-permute-start(bf16[3,96,128]{2,1,0:T(8,128)(2,1)S(1)} %collective-permute-done.20.refs_4_), channel_id=1, source_target_pairs={{0,4},{4,0},{8,12},{12,8},{16,20},{20,16},{24,28},{28,24},{1,5},{5... | collective-permute-start | bytes 221192 | tf_op jit(solution)/shard_map/ppermute | solution.py:364
  70.0 2.7 %collective-permute-done.21.refs_5_ = bf16[3,96,128]{2,1,0:T(8,128)(2,1)S(1)} collective-permute-done((bf16[3,96,128]{2,1,0:T(8,128)(2,1)S(1)}, bf16[3,96,128]{2,1,0:T(8,128)(2,1)S(1)}, u32[]{:S(2)}, u32[]{:S(2)}) %collective-permute-start.21) | collective-permute-done | bytes 73760 | tf_op jit(solution)/shard_map/ppermute | solution.py:364
  74.0 1.7 %shard_map.126 = bf16[18,96,384]{2,1,0:T(8,128)(2,1)} custom-call(s32[54]{0:T(128)S(1)} %get-tuple-element.44.slot_ref, s32[1]{0:T(128)} %bitcast.1.row_ref, f32[9,96,384]{2,1,0:T(8,128)S(1)} %get-tuple-element.66.own_ref, f32[9,96,384]{2,1,0:T(8,128)S(1)} %collective-permute-done.16.other_ref, bf16[3,96,128]{2,1,0:T(8,128)(2,1)S(1)} %get-tuple-element.80.refs_0_, ...), custom_call_target="tpu_custom_call" | custom-call | tf_op jit(solution)/shard_map/pallas_call | solution.py:516
  (52 shorter events, 16.9 us)
Async XLA Ops:
  2.8 5.8 %collective-permute-start = (bf16[18,96,384]{2,1,0:T(8,128)(2,1)S(1)}, bf16[18,96,384]{2,1,0:T(8,128)(2,1)S(1)}, u32[]{:S(2)}, u32[]{:S(2)}) collective-permute-start(bf16[18,96,384]{2,1,0:T(8,128)(2,1)S(1)} %get-tuple-element.42), channel_id=1, source_target_pairs={{0,1},{1,0},{2,3},{3,2},{4,5},{5,4},{6,7},{7,6},{8,9},{9,8},{10,11... | collective-permute-start | bytes 3981320 | tf_op jit(solution)/shard_map/ppermute | solution.py:364
  3.3 10.7 %collective-permute-start.4 = (bf16[4,96,384]{2,1,0:T(8,128)(2,1)}, bf16[4,96,384]{2,1,0:T(8,128)(2,1)S(1)}, u32[]{:S(2)}, u32[]{:S(2)}) collective-permute-start(bf16[4,96,384]{2,1,0:T(8,128)(2,1)} %get-tuple-element.53), channel_id=1, source_target_pairs={{0,2},{1,3},{2,0},{3,1},{4,6},{5,7},{6,4},{7,5},{8,10},{9,11},{10,... | collective-permute-start | bytes 884744 | tf_op jit(solution)/shard_map/ppermute | solution.py:364
  5.9 17.1 %collective-permute-start.7 = (bf16[4,96,384]{2,1,0:T(8,128)(2,1)S(1)}, bf16[4,96,384]{2,1,0:T(8,128)(2,1)S(1)}, u32[]{:S(2)}, u32[]{:S(2)}) collective-permute-start(bf16[4,96,384]{2,1,0:T(8,128)(2,1)S(1)} %get-tuple-element.56), channel_id=1, source_target_pairs={{0,3},{1,2},{2,1},{3,0},{4,7},{5,6},{6,5},{7,4},{8,11},{9,10},{10,... | collective-permute-start | bytes 884744 | tf_op jit(solution)/shard_map/ppermute | solution.py:364
  10.1 14.2 %collective-permute-start.3 = (bf16[9,16,384]{2,1,0:T(8,128)(2,1)S(1)}, bf16[9,16,384]{2,1,0:T(8,128)(2,1)S(1)}, u32[]{:S(2)}, u32[]{:S(2)}) collective-permute-start(bf16[9,16,384]{2,1,0:T(8,128)(2,1)S(1)} %get-tuple-element.43.refs_4_), channel_id=1, source_target_pairs={{0,2},{1,3},{2,0},{3,1},{4,6},{5,7},{6,4},{7,5},{8,10},{9,11},{10,... | collective-permute-start | bytes 331784 | tf_op jit(solution)/shard_map/ppermute | solution.py:364
  15.5 13.8 %collective-permute-start.5 = (bf16[3,96,384]{2,1,0:T(8,128)(2,1)S(1)}, bf16[3,96,384]{2,1,0:T(8,128)(2,1)S(1)}, u32[]{:S(2)}, u32[]{:S(2)}) collective-permute-start(bf16[3,96,384]{2,1,0:T(8,128)(2,1)S(1)} %get-tuple-element.54), channel_id=1, source_target_pairs={{0,2},{1,3},{2,0},{3,1},{4,6},{5,7},{6,4},{7,5},{8,10},{9,11},{10,... | collective-permute-start | bytes 663560 | tf_op jit(solution)/shard_map/ppermute | solution.py:364
  17.6 14.1 %collective-permute-start.6 = (bf16[3,96,384]{2,1,0:T(8,128)(2,1)S(1)}, bf16[3,96,384]{2,1,0:T(8,128)(2,1)S(1)}, u32[]{:S(2)}, u32[]{:S(2)}) collective-permute-start(bf16[3,96,384]{2,1,0:T(8,128)(2,1)S(1)} %get-tuple-element.55), channel_id=1, source_target_pairs={{0,3},{1,2},{2,1},{3,0},{4,7},{5,6},{6,5},{7,4},{8,11},{9,10},{10,... | collective-permute-start | bytes 663560 | tf_op jit(solution)/shard_map/ppermute | solution.py:364
  17.6 18.0 %collective-permute-start.1 = (bf16[2,96,384]{2,1,0:T(8,128)(2,1)S(1)}, bf16[2,96,384]{2,1,0:T(8,128)(2,1)S(1)}, u32[]{:S(2)}, u32[]{:S(2)}) collective-permute-start(bf16[2,96,384]{2,1,0:T(8,128)(2,1)S(1)} %get-tuple-element.51), channel_id=1, source_target_pairs={{0,2},{1,3},{2,0},{3,1},{4,6},{5,7},{6,4},{7,5},{8,10},{9,11},{10,... | collective-permute-start | bytes 442376 | tf_op jit(solution)/shard_map/ppermute | solution.py:364
  23.0 14.9 %collective-permute-start.2 = (bf16[2,96,384]{2,1,0:T(8,128)(2,1)S(1)}, bf16[2,96,384]{2,1,0:T(8,128)(2,1)S(1)}, u32[]{:S(2)}, u32[]{:S(2)}) collective-permute-start(bf16[2,96,384]{2,1,0:T(8,128)(2,1)S(1)} %get-tuple-element.52), channel_id=1, source_target_pairs={{0,3},{1,2},{2,1},{3,0},{4,7},{5,6},{6,5},{7,4},{8,11},{9,10},{10,... | collective-permute-start | bytes 442376 | tf_op jit(solution)/shard_map/ppermute | solution.py:364
  40.2 2.1 %collective-permute-start.8 = (bf16[24,96,128]{2,1,0:T(8,128)(2,1)S(1)}, bf16[24,96,128]{2,1,0:T(8,128)(2,1)S(1)}, u32[]{:S(2)}, u32[]{:S(2)}) collective-permute-start(bf16[24,96,128]{2,1,0:T(8,128)(2,1)S(1)} %get-tuple-element.70), channel_id=1, source_target_pairs={{0,1},{1,0},{2,3},{3,2},{4,5},{5,4},{6,7},{7,6},{8,9},{9,8},{10,11... | collective-permute-start | bytes 1769480 | tf_op jit(solution)/shard_map/ppermute | solution.py:364
  42.3 4.7 %collective-permute-start.10 = (bf16[3,96,128]{2,1,0:T(8,128)(2,1)S(1)}, bf16[3,96,128]{2,1,0:T(8,128)(2,1)S(1)}, u32[]{:S(2)}, u32[]{:S(2)}) collective-permute-start(bf16[3,96,128]{2,1,0:T(8,128)(2,1)S(1)} %get-tuple-element.74), channel_id=1, source_target_pairs={{0,4},{4,0},{8,12},{12,8},{16,20},{20,16},{24,28},{28,24},{1,5},{5... | collective-permute-start | bytes 221192 | tf_op jit(solution)/shard_map/ppermute | solution.py:364
  43.9 7.1 %collective-permute-start.12 = (bf16[3,96,128]{2,1,0:T(8,128)(2,1)S(1)}, bf16[3,96,128]{2,1,0:T(8,128)(2,1)S(1)}, u32[]{:S(2)}, u32[]{:S(2)}) collective-permute-start(bf16[3,96,128]{2,1,0:T(8,128)(2,1)S(1)} %get-tuple-element.76), channel_id=1, source_target_pairs={{0,4},{4,0},{8,12},{12,8},{16,20},{20,16},{24,28},{28,24},{1,5},{5... | collective-permute-start | bytes 221192 | tf_op jit(solution)/shard_map/ppermute | solution.py:364
  44.4 7.3 %collective-permute-start.14 = (bf16[3,96,128]{2,1,0:T(8,128)(2,1)S(1)}, bf16[3,96,128]{2,1,0:T(8,128)(2,1)S(1)}, u32[]{:S(2)}, u32[]{:S(2)}) collective-permute-start(bf16[3,96,128]{2,1,0:T(8,128)(2,1)S(1)} %get-tuple-element.78), channel_id=1, source_target_pairs={{0,4},{4,0},{8,12},{12,8},{16,20},{20,16},{24,28},{28,24},{1,5},{5... | collective-permute-start | bytes 221192 | tf_op jit(solution)/shard_map/ppermute | solution.py:364
  46.0 7.5 %collective-permute-start.9 = (bf16[3,96,128]{2,1,0:T(8,128)(2,1)S(1)}, bf16[3,96,128]{2,1,0:T(8,128)(2,1)S(1)}, u32[]{:S(2)}, u32[]{:S(2)}) collective-permute-start(bf16[3,96,128]{2,1,0:T(8,128)(2,1)S(1)} %get-tuple-element.72), channel_id=1, source_target_pairs={{0,4},{4,0},{8,12},{12,8},{16,20},{20,16},{24,28},{28,24},{1,5},{5... | collective-permute-start | bytes 221192 | tf_op jit(solution)/shard_map/ppermute | solution.py:364
  47.1 7.1 %collective-permute-start.11 = (bf16[3,96,128]{2,1,0:T(8,128)(2,1)S(1)}, bf16[3,96,128]{2,1,0:T(8,128)(2,1)S(1)}, u32[]{:S(2)}, u32[]{:S(2)}) collective-permute-start(bf16[3,96,128]{2,1,0:T(8,128)(2,1)S(1)} %shard_map.122), channel_id=1, source_target_pairs={{0,24},{4,28},{8,16},{12,20},{16,8},{20,12},{24,0},{28,4},{1,25},{... | collective-permute-start | bytes 221192 | tf_op jit(solution)/shard_map/ppermute | solution.py:364
  51.0 5.8 %collective-permute-start.13 = (bf16[3,96,128]{2,1,0:T(8,128)(2,1)S(1)}, bf16[3,96,128]{2,1,0:T(8,128)(2,1)S(1)}, u32[]{:S(2)}, u32[]{:S(2)}) collective-permute-start(bf16[3,96,128]{2,1,0:T(8,128)(2,1)S(1)} %shard_map.123), channel_id=1, source_target_pairs={{0,16},{4,20},{8,24},{12,28},{16,0},{20,4},{24,8},{28,12},{1,17},{... | collective-permute-start | bytes 221192 | tf_op jit(solution)/shard_map/ppermute | solution.py:364
  51.8 5.4 %collective-permute-start.15 = (bf16[3,96,128]{2,1,0:T(8,128)(2,1)S(1)}, bf16[3,96,128]{2,1,0:T(8,128)(2,1)S(1)}, u32[]{:S(2)}, u32[]{:S(2)}) collective-permute-start(bf16[3,96,128]{2,1,0:T(8,128)(2,1)S(1)} %shard_map.124), channel_id=1, source_target_pairs={{0,8},{4,12},{8,0},{12,4},{16,24},{20,28},{24,16},{28,20},{1,9},{5... | collective-permute-start | bytes 221192 | tf_op jit(solution)/shard_map/ppermute | solution.py:364
  58.4 15.7 %collective-permute-start.16 = (f32[9,96,384]{2,1,0:T(8,128)S(1)}, f32[9,96,384]{2,1,0:T(8,128)S(1)}, u32[]{:S(2)}, u32[]{:S(2)}) collective-permute-start(f32[9,96,384]{2,1,0:T(8,128)S(1)} %get-tuple-element.79), channel_id=1, source_target_pairs={{0,1},{1,0},{2,3},{3,2},{4,5},{5,4},{6,7},{7,6},{8,9},{9,8},{10,11... | collective-permute-start | bytes 3981320 | tf_op jit(solution)/shard_map/ppermute | solution.py:364
  58.4 6.9 %collective-permute-start.22 = (bf16[3,96,128]{2,1,0:T(8,128)(2,1)S(1)}, bf16[3,96,128]{2,1,0:T(8,128)(2,1)S(1)}, u32[]{:S(2)}, u32[]{:S(2)}) collective-permute-start(bf16[3,96,128]{2,1,0:T(8,128)(2,1)S(1)} %get-tuple-element.80.refs_0_), channel_id=1, source_target_pairs={{0,24},{4,28},{8,16},{12,20},{16,8},{20,12},{24,0},{28,4},{1,25},{... | collective-permute-start | bytes 221192 | tf_op jit(solution)/shard_map/ppermute | solution.py:364
  61.2 6.8 %collective-permute-start.20 = (bf16[3,96,128]{2,1,0:T(8,128)(2,1)S(1)}, bf16[3,96,128]{2,1,0:T(8,128)(2,1)S(1)}, u32[]{:S(2)}, u32[]{:S(2)}) collective-permute-start(bf16[3,96,128]{2,1,0:T(8,128)(2,1)S(1)} %get-tuple-element.80.refs_0_), channel_id=1, source_target_pairs={{0,16},{4,20},{8,24},{12,28},{16,0},{20,4},{24,8},{28,12},{1,17},{... | collective-permute-start | bytes 221192 | tf_op jit(solution)/shard_map/ppermute | solution.py:364
  61.2 8.4 %collective-permute-start.18 = (bf16[3,96,128]{2,1,0:T(8,128)(2,1)S(1)}, bf16[3,96,128]{2,1,0:T(8,128)(2,1)S(1)}, u32[]{:S(2)}, u32[]{:S(2)}) collective-permute-start(bf16[3,96,128]{2,1,0:T(8,128)(2,1)S(1)} %get-tuple-element.80.refs_0_), channel_id=1, source_target_pairs={{0,8},{4,12},{8,0},{12,4},{16,24},{20,28},{24,16},{28,20},{1,9},{5... | collective-permute-start | bytes 221192 | tf_op jit(solution)/shard_map/ppermute | solution.py:364
  62.7 7.3 %collective-permute-start.17 = (bf16[3,96,128]{2,1,0:T(8,128)(2,1)S(1)}, bf16[3,96,128]{2,1,0:T(8,128)(2,1)S(1)}, u32[]{:S(2)}, u32[]{:S(2)}) collective-permute-start(bf16[3,96,128]{2,1,0:T(8,128)(2,1)S(1)} %get-tuple-element.80.refs_0_), channel_id=1, source_target_pairs={{0,4},{4,0},{8,12},{12,8},{16,20},{20,16},{24,28},{28,24},{1,5},{5... | collective-permute-start | bytes 221192 | tf_op jit(solution)/shard_map/ppermute | solution.py:364
  65.2 4.8 %collective-permute-start.23 = (bf16[3,96,128]{2,1,0:T(8,128)(2,1)S(1)}, bf16[3,96,128]{2,1,0:T(8,128)(2,1)S(1)}, u32[]{:S(2)}, u32[]{:S(2)}) collective-permute-start(bf16[3,96,128]{2,1,0:T(8,128)(2,1)S(1)} %collective-permute-done.22.refs_6_), channel_id=1, source_target_pairs={{0,4},{4,0},{8,12},{12,8},{16,20},{20,16},{24,28},{28,24},{1,5},{5... | collective-permute-start | bytes 221192 | tf_op jit(solution)/shard_map/ppermute | solution.py:364
  68.0 4.8 %collective-permute-start.21 = (bf16[3,96,128]{2,1,0:T(8,128)(2,1)S(1)}, bf16[3,96,128]{2,1,0:T(8,128)(2,1)S(1)}, u32[]{:S(2)}, u32[]{:S(2)}) collective-permute-start(bf16[3,96,128]{2,1,0:T(8,128)(2,1)S(1)} %collective-permute-done.20.refs_4_), channel_id=1, source_target_pairs={{0,4},{4,0},{8,12},{12,8},{16,20},{20,16},{24,28},{28,24},{1,5},{5... | collective-permute-start | bytes 221192 | tf_op jit(solution)/shard_map/ppermute | solution.py:364
  69.7 4.4 %collective-permute-start.19 = (bf16[3,96,128]{2,1,0:T(8,128)(2,1)S(1)}, bf16[3,96,128]{2,1,0:T(8,128)(2,1)S(1)}, u32[]{:S(2)}, u32[]{:S(2)}) collective-permute-start(bf16[3,96,128]{2,1,0:T(8,128)(2,1)S(1)} %collective-permute-done.18.refs_2_), channel_id=1, source_target_pairs={{0,4},{4,0},{8,12},{12,8},{16,20},{20,16},{24,28},{28,24},{1,5},{5... | collective-permute-start | bytes 221192 | tf_op jit(solution)/shard_map/ppermute | solution.py:364
  (5 other events, 30.6 us)

commit v6 on v5

--- a/solution.py
+++ b/solution.py
@@ -18,75 +18,57 @@
 BF16 = jnp.bfloat16
 
 
-def pack_kernel(row_ref, *refs, chunks, siblings, edges):
-    count = 2 * len(chunks) + siblings + edges
+def pack_kernel(row_ref, *refs, chunks, edges):
     sems = refs[-1]
-    outs, held = refs[-1 - 2 * count : -1 - count], refs[-1 - count : -1]
+    outs = list(refs[-1 - 2 * len(chunks) - edges : -1])
     pixels_ref, rows_ref = refs[:2]
     half = pixels_ref.shape[0] // 2
     row = row_ref[0]
     core = row & 1
     pieces = []
-    kept = list(held)
-    if siblings:
-        other = pl.ds((1 - core) * half, half)
-        pieces += [rows_ref.at[other], pixels_ref.at[other]]
-        kept[:1] = [held[0].at[pl.ds(0, half)], held[0].at[pl.ds(half, half)]]
     for s, n in chunks:
         for which in range(2):
             pieces.append(pixels_ref.at[pl.ds((core ^ which) * half + s, n)])
-    fetches = [
-        pltpu.make_async_copy(piece, place, sems.at[0, i])
-        for i, (piece, place) in enumerate(zip(pieces, kept))
+    copies = [
+        pltpu.make_async_copy(piece, out, sems.at[i]) for i, (piece, out) in enumerate(zip(pieces, outs))
     ]
-    stores = [
-        pltpu.make_async_copy(place, out, sems.at[1, i])
-        for i, (place, out) in enumerate(zip(held, outs))
-    ]
+    for copy in copies:
+        copy.start()
     if edges:
         pad = outs[-1].shape[1]
         first = jnp.where(row < 2, rows_ref.shape[1] - pad, 0)
         near = pl.ds(pl.multiple_of(first, ALIGN), pad)
         holds = core == (row < 2).astype(jnp.int32)
         own = rows_ref.at[pl.ds(core * half, half), near]
-        edge = pltpu.make_async_copy(own, held[-1], sems.at[0, count])
+        edge = pltpu.make_async_copy(own, outs[-1], sems.at[len(pieces)])
         passed = pltpu.make_async_copy(
-            refs[2].at[pl.ds(0, half), near], held[-1], sems.at[0, count]
+            refs[2].at[pl.ds(core * half, half), near], outs[-1], sems.at[len(pieces)]
         )
         pl.when(holds)(edge.start)
         pl.when(jnp.logical_not(holds))(passed.start)
-        fetches.append(edge)
-    for fetch in fetches[: len(pieces)]:
-        fetch.start()
-    if siblings:
-        fetches.pop(0).wait()
-    for fetch, store in zip(fetches, stores):
-        fetch.wait()
-        store.start()
-    for store in stores:
-        store.wait()
-
-
-def pack(row, pixels, rows, chunks, pad, siblings=False, sibling=None, after=()):
+        copies.append(edge)
+    for copy in copies:
+        copy.wait()
+
+
+def pack(row, pixels, rows, chunks, pad, sibling_rows=None, after=()):
     images, band, side = pixels.shape
     half = images // 2
-    shapes = [(images, band, side)] if siblings else []
-    shapes += [(n, band, side) for _, n in chunks for _ in range(2)]
+    shapes = [(n, band, side) for _, n in chunks for _ in range(2)]
     arrays = [pltpu.with_memory_space_constraint(a, pltpu.HBM) for a in (pixels, rows)]
-    if sibling is not None:
+    if sibling_rows is not None:
         shapes.append((half, pad, side))
-        arrays.append(sibling)
+        arrays.append(sibling_rows)
     arrays += after
     anywhere = pl.BlockSpec(memory_space=pl.ANY)
     return pl.pallas_call(
         functools.partial(
-            pack_kernel, chunks=chunks, siblings=siblings, edges=sibling is not None
+            pack_kernel, chunks=chunks, edges=sibling_rows is not None
         ),
         in_specs=[pl.BlockSpec(memory_space=pltpu.SMEM)] + [anywhere] * len(arrays),
-        out_specs=[anywhere] * len(shapes),
+        out_specs=[pl.BlockSpec(memory_space=pltpu.VMEM)] * len(shapes),
         out_shape=[jax.ShapeDtypeStruct(shape, BF16) for shape in shapes],
-        scratch_shapes=[pltpu.VMEM(shape, BF16) for shape in shapes]
-        + [pltpu.SemaphoreType.DMA((2, len(shapes) + 1))],
+        scratch_shapes=[pltpu.SemaphoreType.DMA((len(shapes) + 2,))],
         compiler_params=pltpu.CompilerParams(vmem_limit_bytes=VMEM),
     )(row, *arrays)
 
@@ -148,8 +130,8 @@
 def match_kernel(slot_ref, weight_ref, row_ref, *refs, start, count, taps, halves, first, warp, send):
     profile_ref, refs = refs[0], refs[1:]
     if warp:
-        pixels_ref, rows_ref, cols_ref, sibling_ref, far_ref, cross_ref, edge_ref = refs[:7]
-        refs = refs[7:]
+        pixels_ref, rows_ref, cols_ref, passed_ref, passed_rows_ref, far_ref, cross_ref, edge_ref = refs[:8]
+        refs = refs[8:]
     else:
         warped_ref, refs = refs[0], refs[1:]
     if not first:
@@ -184,7 +166,8 @@
         for g in range(count):
             image, extended = refs[g], refs[count + g]
             index = start + g
-            shards = (pixels_ref.at[index], sibling_ref.at[sibling_ref.shape[0] // 2 + index])
+            there = core * pixels_ref.shape[0] + index
+            shards = (pixels_ref.at[index], passed_ref.at[there])
             for mask, shard in enumerate(shards + (far_ref.at[g], cross_ref.at[g])):
                 at = pl.multiple_of((row ^ mask) * band, band)
                 image[pl.ds(at, band), :] = shard[...]
@@ -192,9 +175,9 @@
             blank = jnp.zeros_like(edge)
             extended[0:pad, :] = jnp.where(row >= 2, edge, blank)
             extended[pad + 2 * band :, :] = jnp.where(row >= 2, blank, edge)
-            for which, rows in enumerate((rows_ref, sibling_ref)):
+            for which, rows in enumerate((rows_ref.at[index], passed_rows_ref.at[there])):
                 at = pl.multiple_of(pad + (core ^ which) * band, ALIGN)
-                extended[pl.ds(at, band), :] = rows[index]
+                extended[pl.ds(at, band), :] = rows[...]
     for g in range(count):
         profiles = None
         for b in range(inner):
@@ -317,24 +300,28 @@
 
 
 def template_kernel(denom_ref, _, *refs):
-    part_refs, template_ref, coadd_ref = refs[:-3], refs[-3], refs[-2]
+    part_refs, template_ref = refs[:-2], refs[-2]
     for q in range(template_ref.shape[0]):
         total = part_refs[0][q].astype(F32)
         for part in part_refs[1:]:
             total = total + part[q].astype(F32)
         box = (total / jnp.maximum(denom_ref[q], 1.0)).astype(BF16)
         template_ref[q] = box
-        coadd_ref[:, TILE * q : TILE * (q + 1)] = box
-
-
-def difference_kernel(slot_ref, row_ref, own_ref, other_ref, *refs, group):
+
+
+def coadd_kernel(template_ref, coadd_ref):
+    for q in range(template_ref.shape[0]):
+        coadd_ref[:, TILE * q : TILE * (q + 1)] = template_ref[q]
+
+
+def difference_kernel(slot_ref, row_ref, own_ref, other_ref, *refs, group, masks):
     template_refs, out_ref = refs[:-4], refs[-4]
     held, ready, sems = refs[-3:]
     each = template_refs[0].shape[0]
     half, _, side = own_ref.shape
     tiles = side // TILE
     core = row_ref[0] & 1
-    for m, template in enumerate(template_refs):
+    for m, template in zip(masks, template_refs):
         held[each * m : each * (m + 1)] = template[...]
     copies = []
     for which, matched_ref in enumerate((own_ref, other_ref)):
@@ -404,12 +391,12 @@
             far.append(exchange(first, "row", 2))
             cross.append(exchange(second, "row", 3))
 
-    packed = pack(row_one, pixels, rows, spans[:1], pad, siblings=True)
-    sibling = exchange(packed[0], "row", 1)
-    send(packed[1:])
-    packed = pack(row_one, pixels, rows, spans[2:], pad, sibling=sibling)
+    send(pack(row_one, pixels, rows, spans[:1], pad))
+    sibling_rows = exchange(rows, "row", 1)
+    sibling_pixels = exchange(pixels, "row", 1)
+    packed = pack(row_one, pixels, rows, spans[-1:], pad, sibling_rows=sibling_rows)
     edge = exchange(packed[-1], "row", 2)
-    send(pack(row_one, pixels, rows, spans[1:2], pad, after=[far[0]]))
+    send(pack(row_one, pixels, rows, spans[1:-1], pad, after=[far[0]]))
     send(packed[:-1])
 
     with jax.named_scope("profiles"):
@@ -459,7 +446,7 @@
     scalars = (own_slots, weights, row_one)
     common = (tap_count, slot_count)
     for c, (s, n) in enumerate(spans):
-        operands = tuple(kept[:3]) + (sibling, far[c], cross[c], edge)
+        operands = tuple(kept[:3]) + (sibling_pixels, sibling_rows, far[c], cross[c], edge)
         if c < len(spans) - 1:
             carry = match_chunk(scalars, kept[3], operands, carry, s, n, *common, (0, 1))
     matched_sent, _, sums_sent, warped = match_chunk(
@@ -481,7 +468,7 @@
         ],
         compiler_params=small,
     )(own_sums, other_sums)
-    evens = tuple(range(det_devices - 2, 0, -2))
+    evens = tuple(range(2, det_devices, 2))
     across = {m: exchange(parts[m ^ 1], "det", 1) for m in evens + (0,)}
     received = [parts[0], across[0]]
     for m in evens:
@@ -493,16 +480,15 @@
             compiler_params=small,
         )(parts[m], across[m])
         received.append(exchange(total, "det", m))
-    template, coadd, matched_sent = pl.pallas_call(
+    template, matched_sent = pl.pallas_call(
         template_kernel,
         in_specs=[pl.BlockSpec(memory_space=pltpu.SMEM), anywhere] + [in_vmem] * len(received),
-        out_specs=[in_vmem] * 2 + [anywhere],
+        out_specs=[in_vmem, anywhere],
         out_shape=[
             box,
-            jax.ShapeDtypeStruct((band, side), BF16),
             jax.ShapeDtypeStruct(matched_sent.shape, F32),
         ],
-        input_output_aliases={1: 2},
+        input_output_aliases={1: 1},
         compiler_params=small,
     )(denom, matched_sent, *received)
     other_matched = exchange(matched_sent, "row", 1)
@@ -511,10 +497,18 @@
         passed[m] = exchange(template, "det", m)
     for m in evens + (0,):
         passed[m ^ 1] = exchange(passed[m], "det", 1)
-    templates = [passed[m] for m in range(det_devices)]
+    masks = tuple(range(det_devices - 1, -1, -1))
+    templates = [passed[m] for m in masks]
+    coadd = pl.pallas_call(
+        coadd_kernel,
+        in_specs=[in_vmem],
+        out_specs=in_vmem,
+        out_shape=jax.ShapeDtypeStruct((band, side), BF16),
+        compiler_params=small,
+    )(template)
     group = 3 if half % 3 == 0 else 1
     difference = pl.pallas_call(
-        functools.partial(difference_kernel, group=group),
+        functools.partial(difference_kernel, group=group, masks=masks),
         in_specs=[pl.BlockSpec(memory_space=pltpu.SMEM)] * 2 + [in_vmem] * (2 + det_devices),
         out_specs=anywhere,
         scratch_shapes=[

time: 76.1 us -> 74.9 us (0.984)
  waiting for transfers between devices: 17.2 us -> 15.6 us
  starting transfers between devices: 29.2 us -> 30.7 us
  Pallas kernels: 25.9 us -> 24.7 us
    ppermute x24 -> x25, waiting for transfers between devices: 17.2 us -> 15.6 us  [exchange(): return lax.ppermute(value, axis, [(i, i ^ mask) for i in range(size)])]
    ppermute x24 -> x25, starting transfers between devices: 29.2 us -> 30.7 us  [exchange(): return lax.ppermute(value, axis, [(i, i ^ mask) for i in range(size)])]
    pallas_call x4 -> x5, Pallas kernels: 6.91 us -> 6.27 us  [the longest x3 3.9 us: pack(): pl.pallas_call(functools.partial(pack_kernel, chunks=chunks, edges=siblin...]
  transfers between devices with their start and end apart: 24 -> 25, of which waited for: 12 -> 9; matrix products, arithmetic and copies ran while one was open for 3% -> 4% of each run, Pallas kernels for 24% -> 27%
where the time goes in v6:
time: 74.9 us; the launch traced here: 74.5 us
  starting transfers between devices  30.7 us (41%)
  Pallas kernels  24.7 us (33%)
  waiting for transfers between devices  15.6 us (21%)
  local copies, waits for them, and re-layouts  1.54 us (2%)
  matrix products  1.05 us (1%)
  between operations  0.81 us (1%)
    ppermute x25, starting transfers between devices, exchange(): return lax.ppermute(value, axis, [(i, i ^ mask) for i in range(size)])  30.7 us
    ppermute x25, waiting for transfers between devices, exchange(): return lax.ppermute(value, axis, [(i, i ^ mask) for i in range(size)])  15.6 us
    pallas_call x4, Pallas kernels, match_chunk(): pl.pallas_call(functools.partial(match_kernel, start=start, count=count,...  12.7 us
    pallas_call x1, Pallas kernels, per_device(): pl.pallas_call(functools.partial(target_kernel, tiles=tiles), in_specs=[p...  4.88 us
    pallas_call x3, Pallas kernels, pack(): pl.pallas_call(functools.partial(pack_kernel, chunks=chunks, edges=siblin...  3.9 us
    pallas_call x1, Pallas kernels, per_device(): pl.pallas_call(functools.partial(difference_kernel, group=group, masks=ma...  1.73 us
  transfers between devices with their start and end apart: 25, of which 9 were waited for; matrix products, arithmetic and copies ran while one was open for 4% of the time, Pallas kernels for 27%

profile of v6, /device:TPU:0, one launch (start us, length us, event | category | flops | bytes accessed | tf_op | source)
XLA Modules:
  0.0 74.5 jit_solution(14914673665569636251)
XLA Ops:
  1.2 1.8 %shard_map.115 = (bf16[4,96,384]{2,1,0:T(8,128)(2,1)}, bf16[4,96,384]{2,1,0:T(8,128)(2,1)S(1)}) custom-call(s32[1]{0:T(128)} %bitcast.1.row_ref, bf16[18,96,384]{2,1,0:T(8,128)(2,1)} %bitcast.22, bf16[18,96,384]{2,1,0:T(8,128)(2,1)} %bitcast.17), custom_call_target="tpu_custom_call" | custom-call | tf_op jit(solution)/shard_map/pallas_call | solution.py:64
  3.0 3.0 %collective-permute-start.5 = (bf16[4,96,384]{2,1,0:T(8,128)(2,1)}, bf16[4,96,384]{2,1,0:T(8,128)(2,1)S(1)}, u32[]{:S(2)}, u32[]{:S(2)}) collective-permute-start(bf16[4,96,384]{2,1,0:T(8,128)(2,1)} %get-tuple-element.50), channel_id=1, source_target_pairs={{0,2},{1,3},{2,0},{3,1},{4,6},{5,7},{6,4},{7,5},{8,10},{9,11},{10,... | collective-permute-start | bytes 884744 | tf_op jit(solution)/shard_map/ppermute | solution.py:351
  11.3 2.8 %collective-permute-done.5.refs_2_.refs_6_ = bf16[4,96,384]{2,1,0:T(8,128)(2,1)S(1)} collective-permute-done((bf16[4,96,384]{2,1,0:T(8,128)(2,1)}, bf16[4,96,384]{2,1,0:T(8,128)(2,1)S(1)}, u32[]{:S(2)}, u32[]{:S(2)}) %collective-permute-start.5) | collective-permute-done | bytes 294944 | tf_op jit(solution)/shard_map/ppermute | solution.py:351
  15.1 2.1 %collective-permute-start.6 = (bf16[3,96,384]{2,1,0:T(8,128)(2,1)S(1)}, bf16[3,96,384]{2,1,0:T(8,128)(2,1)S(1)}, u32[]{:S(2)}, u32[]{:S(2)}) collective-permute-start(bf16[3,96,384]{2,1,0:T(8,128)(2,1)S(1)} %get-tuple-element.51), channel_id=1, source_target_pairs={{0,2},{1,3},{2,0},{3,1},{4,6},{5,7},{6,4},{7,5},{8,10},{9,11},{10,... | collective-permute-start | bytes 663560 | tf_op jit(solution)/shard_map/ppermute | solution.py:351
  17.3 4.9 %shard_map.114 = (s32[54]{0:T(128)S(1)}, s32[27]{0:T(128)S(1)}, f32[9]{0:T(128)S(1)}, f32[3]{0:T(128)S(1)}, bf16[9,96,384]{2,1,0:T(8,128)(2,1)S(1)}, /*index=5*/...) custom-call(s32[2]{0:T(128)S(1)} %pad_add_fusion.place_ref, s32[432]{0:T(512)S(1)} %bitcast.14, ...), custom_call_target="tpu_custom_call" | custom-call | tf_op jit(solution)/shard_map/pallas_call | solution.py:420
  22.4 1.7 %collective-permute-start.3 = (bf16[2,96,384]{2,1,0:T(8,128)(2,1)S(1)}, bf16[2,96,384]{2,1,0:T(8,128)(2,1)S(1)}, u32[]{:S(2)}, u32[]{:S(2)}) collective-permute-start(bf16[2,96,384]{2,1,0:T(8,128)(2,1)S(1)} %get-tuple-element.49), channel_id=1, source_target_pairs={{0,3},{1,2},{2,1},{3,0},{4,7},{5,6},{6,5},{7,4},{8,11},{9,10},{10,... | collective-permute-start | bytes 442376 | tf_op jit(solution)/shard_map/ppermute | solution.py:351
  24.1 5.0 %shard_map.117 = (f32[9,96,384]{2,1,0:T(8,128)S(1)}, f32[9,96,384]{2,1,0:T(8,128)S(1)}, f32[24,96,128]{2,1,0:T(8,128)S(1)}, f32[24,96,128]{2,1,0:T(8,128)S(1)}) custom-call(s32[27]{0:T(128)S(1)} %get-tuple-element.42.slot_ref, f32[9]{0:T(128)S(1)} %get-tuple-element.43.weight_ref, s32[1]{0:T(128)} %bitcast.1.row_ref, ...), custom_call_target="tpu_custom_call" | custom-call | flops 8000000000 | bytes 4000000 | tf_op jit(solution)/shard_map/pallas_call | solution.py:268
  29.1 2.7 %collective-permute-done.7.refs_7_ = bf16[3,96,384]{2,1,0:T(8,128)(2,1)S(1)} collective-permute-done((bf16[3,96,384]{2,1,0:T(8,128)(2,1)S(1)}, bf16[3,96,384]{2,1,0:T(8,128)(2,1)S(1)}, u32[]{:S(2)}, u32[]{:S(2)}) %collective-permute-start.7) | collective-permute-done | bytes 221216 | tf_op jit(solution)/shard_map/ppermute | solution.py:351
  31.8 3.9 %shard_map.118 = (f32[9,96,384]{2,1,0:T(8,128)S(1)}, f32[9,96,384]{2,1,0:T(8,128)S(1)}, f32[24,96,128]{2,1,0:T(8,128)S(1)}, f32[24,96,128]{2,1,0:T(8,128)S(1)}) custom-call(s32[27]{0:T(128)S(1)} %get-tuple-element.42.slot_ref, f32[9]{0:T(128)S(1)} %get-tuple-element.43.weight_ref, ...), custom_call_target="tpu_custom_call", output_to_operand_aliasing={{0}: (12, {}), {1}: (13, {}), {2}: (14, {}), {3}: (15, {})} | custom-call | flops 6000000000 | bytes 3000000 | tf_op jit(solution)/shard_map/pallas_call | solution.py:268
  35.7 1.7 %collective-permute-done.3.refs_7_ = bf16[2,96,384]{2,1,0:T(8,128)(2,1)S(1)} collective-permute-done((bf16[2,96,384]{2,1,0:T(8,128)(2,1)S(1)}, bf16[2,96,384]{2,1,0:T(8,128)(2,1)S(1)}, u32[]{:S(2)}, u32[]{:S(2)}) %collective-permute-start.3) | collective-permute-done | bytes 147488 | tf_op jit(solution)/shard_map/ppermute | solution.py:351
  37.4 2.2 %shard_map.119 = (f32[9,96,384]{2,1,0:T(8,128)S(1)}, f32[24,96,128]{2,1,0:T(8,128)S(1)}, bf16[24,96,128]{2,1,0:T(8,128)(2,1)S(1)}, bf16[2,224,384]{2,1,0:T(8,128)(2,1)S(1)}) custom-call(s32[27]{0:T(128)S(1)} %get-tuple-element.42.slot_ref, f32[9]{0:T(128)S(1)} %get-tuple-element.43.weight_ref, ...), custom_call_target="tpu_custom_call", output_to_operand_aliasing={{0}: (12, {}), {1}: (13, {})} | custom-call | flops 2000000000 | bytes 2000000 | tf_op jit(solution)/shard_map/pallas_call | solution.py:268
  40.1 1.7 %shard_map.120 = (f32[9,96,384]{2,1,0:T(8,128)S(1)}, f32[24,96,128]{2,1,0:T(8,128)S(1)}) custom-call(s32[27]{0:T(128)S(1)} %get-tuple-element.42.slot_ref, f32[9]{0:T(128)S(1)} %get-tuple-element.43.weight_ref, s32[1]{0:T(128)} %bitcast.1.row_ref, f32[9,24,128]{2,1,0:T(8,128)S(1)} %get-tuple-element.44.refs_0_, ...), custom_call_target="tpu_custom_call", output_to_operand_aliasing={{0}: (5, {}), {1}: (6, {})} | custom-call | flops 2000000000 | bytes 2000000 | tf_op jit(solution)/shard_map/pallas_call | solution.py:268
  41.9 1.8 %collective-permute-start.11 = (bf16[3,96,128]{2,1,0:T(8,128)(2,1)S(1)}, bf16[3,96,128]{2,1,0:T(8,128)(2,1)S(1)}, u32[]{:S(2)}, u32[]{:S(2)}) collective-permute-start(bf16[3,96,128]{2,1,0:T(8,128)(2,1)S(1)} %get-tuple-element.71), channel_id=1, source_target_pairs={{0,4},{4,0},{8,12},{12,8},{16,20},{20,16},{24,28},{28,24},{1,5},{5... | collective-permute-start | bytes 221192 | tf_op jit(solution)/shard_map/ppermute | solution.py:351
  44.0 1.7 %collective-permute-start.15 = (bf16[3,96,128]{2,1,0:T(8,128)(2,1)S(1)}, bf16[3,96,128]{2,1,0:T(8,128)(2,1)S(1)}, u32[]{:S(2)}, u32[]{:S(2)}) collective-permute-start(bf16[3,96,128]{2,1,0:T(8,128)(2,1)S(1)} %get-tuple-element.75), channel_id=1, source_target_pairs={{0,4},{4,0},{8,12},{12,8},{16,20},{20,16},{24,28},{28,24},{1,5},{5... | collective-permute-start | bytes 221192 | tf_op jit(solution)/shard_map/ppermute | solution.py:351
  46.7 2.1 %collective-permute-start.12 = (bf16[3,96,128]{2,1,0:T(8,128)(2,1)S(1)}, bf16[3,96,128]{2,1,0:T(8,128)(2,1)S(1)}, u32[]{:S(2)}, u32[]{:S(2)}) collective-permute-start(bf16[3,96,128]{2,1,0:T(8,128)(2,1)S(1)} %shard_map.122), channel_id=1, source_target_pairs={{0,8},{4,12},{8,0},{12,4},{16,24},{20,28},{24,16},{28,20},{1,9},{5... | collective-permute-start | bytes 221192 | tf_op jit(solution)/shard_map/ppermute | solution.py:351
  48.8 2.7 %collective-permute-start.14 = (bf16[3,96,128]{2,1,0:T(8,128)(2,1)S(1)}, bf16[3,96,128]{2,1,0:T(8,128)(2,1)S(1)}, u32[]{:S(2)}, u32[]{:S(2)}) collective-permute-start(bf16[3,96,128]{2,1,0:T(8,128)(2,1)S(1)} %shard_map.123), channel_id=1, source_target_pairs={{0,16},{4,20},{8,24},{12,28},{16,0},{20,4},{24,8},{28,12},{1,17},{... | collective-permute-start | bytes 221192 | tf_op jit(solution)/shard_map/ppermute | solution.py:351
  51.5 2.6 %collective-permute-start.16 = (bf16[3,96,128]{2,1,0:T(8,128)(2,1)S(1)}, bf16[3,96,128]{2,1,0:T(8,128)(2,1)S(1)}, u32[]{:S(2)}, u32[]{:S(2)}) collective-permute-start(bf16[3,96,128]{2,1,0:T(8,128)(2,1)S(1)} %shard_map.124), channel_id=1, source_target_pairs={{0,24},{4,28},{8,16},{12,20},{16,8},{20,12},{24,0},{28,4},{1,25},{... | collective-permute-start | bytes 221192 | tf_op jit(solution)/shard_map/ppermute | solution.py:351
  54.1 2.3 %collective-permute-done.14.refs_3_ = bf16[3,96,128]{2,1,0:T(8,128)(2,1)S(1)} collective-permute-done((bf16[3,96,128]{2,1,0:T(8,128)(2,1)S(1)}, bf16[3,96,128]{2,1,0:T(8,128)(2,1)S(1)}, u32[]{:S(2)}, u32[]{:S(2)}) %collective-permute-start.14) | collective-permute-done | bytes 73760 | tf_op jit(solution)/shard_map/ppermute | solution.py:351
  59.6 2.2 %collective-permute-start.20 = (bf16[3,96,128]{2,1,0:T(8,128)(2,1)S(1)}, bf16[3,96,128]{2,1,0:T(8,128)(2,1)S(1)}, u32[]{:S(2)}, u32[]{:S(2)}) collective-permute-start(bf16[3,96,128]{2,1,0:T(8,128)(2,1)S(1)} %get-tuple-element.77.refs_7_.template_ref), channel_id=1, source_target_pairs={{0,16},{4,20},{8,24},{12,28},{16,0},{20,4},{24,8},{28,12},{1,17},{... | collective-permute-start | bytes 221192 | tf_op jit(solution)/shard_map/ppermute | solution.py:351
  63.0 1.6 %collective-permute-start.24 = (bf16[3,96,128]{2,1,0:T(8,128)(2,1)S(1)}, bf16[3,96,128]{2,1,0:T(8,128)(2,1)S(1)}, u32[]{:S(2)}, u32[]{:S(2)}) collective-permute-start(bf16[3,96,128]{2,1,0:T(8,128)(2,1)S(1)} %get-tuple-element.77.refs_7_.template_ref), channel_id=1, source_target_pairs={{0,4},{4,0},{8,12},{12,8},{16,20},{20,16},{24,28},{28,24},{1,5},{5... | collective-permute-start | bytes 221192 | tf_op jit(solution)/shard_map/ppermute | solution.py:351
  64.6 1.7 %collective-permute-start.23 = (bf16[3,96,128]{2,1,0:T(8,128)(2,1)S(1)}, bf16[3,96,128]{2,1,0:T(8,128)(2,1)S(1)}, u32[]{:S(2)}, u32[]{:S(2)}) collective-permute-start(bf16[3,96,128]{2,1,0:T(8,128)(2,1)S(1)} %collective-permute-done.22.refs_5_), channel_id=1, source_target_pairs={{0,4},{4,0},{8,12},{12,8},{16,20},{20,16},{24,28},{28,24},{1,5},{5... | collective-permute-start | bytes 221192 | tf_op jit(solution)/shard_map/ppermute | solution.py:351
  66.6 1.8 %collective-permute-done.18.refs_1_ = bf16[3,96,128]{2,1,0:T(8,128)(2,1)S(1)} collective-permute-done((bf16[3,96,128]{2,1,0:T(8,128)(2,1)S(1)}, bf16[3,96,128]{2,1,0:T(8,128)(2,1)S(1)}, u32[]{:S(2)}, u32[]{:S(2)}) %collective-permute-start.18) | collective-permute-done | bytes 73760 | tf_op jit(solution)/shard_map/ppermute | solution.py:351
  70.8 2.0 %collective-permute-done.19.refs_0_ = bf16[3,96,128]{2,1,0:T(8,128)(2,1)S(1)} collective-permute-done((bf16[3,96,128]{2,1,0:T(8,128)(2,1)S(1)}, bf16[3,96,128]{2,1,0:T(8,128)(2,1)S(1)}, u32[]{:S(2)}, u32[]{:S(2)}) %collective-permute-start.19) | collective-permute-done | bytes 73760 | tf_op jit(solution)/shard_map/ppermute | solution.py:351
  72.8 1.7 %shard_map.126 = bf16[18,96,384]{2,1,0:T(8,128)(2,1)} custom-call(s32[54]{0:T(128)S(1)} %get-tuple-element.41.slot_ref, s32[1]{0:T(128)} %bitcast.1.row_ref, f32[9,96,384]{2,1,0:T(8,128)S(1)} %get-tuple-element.63.own_ref, f32[9,96,384]{2,1,0:T(8,128)S(1)} %collective-permute-done.17.other_ref, bf16[3,96,128]{2,1,0:T(8,128)(2,1)S(1)} %collective-permute-done.19.refs_0_, ...), custom_call_target="tpu_custom_call" | custom-call | tf_op jit(solution)/shard_map/pallas_call | solution.py:510
  (55 shorter events, 16.1 us)
Async XLA Ops:
  0.6 8.0 %collective-permute-start = (bf16[18,96,384]{2,1,0:T(8,128)(2,1)}, bf16[18,96,384]{2,1,0:T(8,128)(2,1)S(1)}, u32[]{:S(2)}, u32[]{:S(2)}) collective-permute-start(bf16[18,96,384]{2,1,0:T(8,128)(2,1)} %bitcast.16), channel_id=1, source_target_pairs={{0,1},{1,0},{2,3},{3,2},{4,5},{5,4},{6,7},{7,6},{8,9},{9,8},{10,11... | collective-permute-start | bytes 3981320 | tf_op jit(solution)/shard_map/ppermute | solution.py:351
  1.1 21.2 %collective-permute-start.1 = (bf16[18,96,384]{2,1,0:T(8,128)(2,1)}, bf16[18,96,384]{2,1,0:T(8,128)(2,1)S(1)}, u32[]{:S(2)}, u32[]{:S(2)}) collective-permute-start(bf16[18,96,384]{2,1,0:T(8,128)(2,1)} %bitcast.21), channel_id=1, source_target_pairs={{0,1},{1,0},{2,3},{3,2},{4,5},{5,4},{6,7},{7,6},{8,9},{9,8},{10,11... | collective-permute-start | bytes 3981320 | tf_op jit(solution)/shard_map/ppermute | solution.py:351
  3.0 11.0 %collective-permute-start.5 = (bf16[4,96,384]{2,1,0:T(8,128)(2,1)}, bf16[4,96,384]{2,1,0:T(8,128)(2,1)S(1)}, u32[]{:S(2)}, u32[]{:S(2)}) collective-permute-start(bf16[4,96,384]{2,1,0:T(8,128)(2,1)} %get-tuple-element.50), channel_id=1, source_target_pairs={{0,2},{1,3},{2,0},{3,1},{4,6},{5,7},{6,4},{7,5},{8,10},{9,11},{10,... | collective-permute-start | bytes 884744 | tf_op jit(solution)/shard_map/ppermute | solution.py:351
  6.0 16.2 %collective-permute-start.8 = (bf16[4,96,384]{2,1,0:T(8,128)(2,1)S(1)}, bf16[4,96,384]{2,1,0:T(8,128)(2,1)S(1)}, u32[]{:S(2)}, u32[]{:S(2)}) collective-permute-start(bf16[4,96,384]{2,1,0:T(8,128)(2,1)S(1)} %get-tuple-element.53), channel_id=1, source_target_pairs={{0,3},{1,2},{2,1},{3,0},{4,7},{5,6},{6,5},{7,4},{8,11},{9,10},{10,... | collective-permute-start | bytes 884744 | tf_op jit(solution)/shard_map/ppermute | solution.py:351
  9.7 14.4 %collective-permute-start.4 = (bf16[9,16,384]{2,1,0:T(8,128)(2,1)S(1)}, bf16[9,16,384]{2,1,0:T(8,128)(2,1)S(1)}, u32[]{:S(2)}, u32[]{:S(2)}) collective-permute-start(bf16[9,16,384]{2,1,0:T(8,128)(2,1)S(1)} %get-tuple-element.40.refs_4_), channel_id=1, source_target_pairs={{0,2},{1,3},{2,0},{3,1},{4,6},{5,7},{6,4},{7,5},{8,10},{9,11},{10,... | collective-permute-start | bytes 331784 | tf_op jit(solution)/shard_map/ppermute | solution.py:351
  15.1 14.0 %collective-permute-start.6 = (bf16[3,96,384]{2,1,0:T(8,128)(2,1)S(1)}, bf16[3,96,384]{2,1,0:T(8,128)(2,1)S(1)}, u32[]{:S(2)}, u32[]{:S(2)}) collective-permute-start(bf16[3,96,384]{2,1,0:T(8,128)(2,1)S(1)} %get-tuple-element.51), channel_id=1, source_target_pairs={{0,2},{1,3},{2,0},{3,1},{4,6},{5,7},{6,4},{7,5},{8,10},{9,11},{10,... | collective-permute-start | bytes 663560 | tf_op jit(solution)/shard_map/ppermute | solution.py:351
  17.3 14.5 %collective-permute-start.7 = (bf16[3,96,384]{2,1,0:T(8,128)(2,1)S(1)}, bf16[3,96,384]{2,1,0:T(8,128)(2,1)S(1)}, u32[]{:S(2)}, u32[]{:S(2)}) collective-permute-start(bf16[3,96,384]{2,1,0:T(8,128)(2,1)S(1)} %get-tuple-element.52), channel_id=1, source_target_pairs={{0,3},{1,2},{2,1},{3,0},{4,7},{5,6},{6,5},{7,4},{8,11},{9,10},{10,... | collective-permute-start | bytes 663560 | tf_op jit(solution)/shard_map/ppermute | solution.py:351
  22.2 13.5 %collective-permute-start.2 = (bf16[2,96,384]{2,1,0:T(8,128)(2,1)S(1)}, bf16[2,96,384]{2,1,0:T(8,128)(2,1)S(1)}, u32[]{:S(2)}, u32[]{:S(2)}) collective-permute-start(bf16[2,96,384]{2,1,0:T(8,128)(2,1)S(1)} %get-tuple-element.48), channel_id=1, source_target_pairs={{0,2},{1,3},{2,0},{3,1},{4,6},{5,7},{6,4},{7,5},{8,10},{9,11},{10,... | collective-permute-start | bytes 442376 | tf_op jit(solution)/shard_map/ppermute | solution.py:351
  22.4 15.1 %collective-permute-start.3 = (bf16[2,96,384]{2,1,0:T(8,128)(2,1)S(1)}, bf16[2,96,384]{2,1,0:T(8,128)(2,1)S(1)}, u32[]{:S(2)}, u32[]{:S(2)}) collective-permute-start(bf16[2,96,384]{2,1,0:T(8,128)(2,1)S(1)} %get-tuple-element.49), channel_id=1, source_target_pairs={{0,3},{1,2},{2,1},{3,0},{4,7},{5,6},{6,5},{7,4},{8,11},{9,10},{10,... | collective-permute-start | bytes 442376 | tf_op jit(solution)/shard_map/ppermute | solution.py:351
  41.9 4.7 %collective-permute-start.11 = (bf16[3,96,128]{2,1,0:T(8,128)(2,1)S(1)}, bf16[3,96,128]{2,1,0:T(8,128)(2,1)S(1)}, u32[]{:S(2)}, u32[]{:S(2)}) collective-permute-start(bf16[3,96,128]{2,1,0:T(8,128)(2,1)S(1)} %get-tuple-element.71), channel_id=1, source_target_pairs={{0,4},{4,0},{8,12},{12,8},{16,20},{20,16},{24,28},{28,24},{1,5},{5... | collective-permute-start | bytes 221192 | tf_op jit(solution)/shard_map/ppermute | solution.py:351
  43.7 5.1 %collective-permute-start.13 = (bf16[3,96,128]{2,1,0:T(8,128)(2,1)S(1)}, bf16[3,96,128]{2,1,0:T(8,128)(2,1)S(1)}, u32[]{:S(2)}, u32[]{:S(2)}) collective-permute-start(bf16[3,96,128]{2,1,0:T(8,128)(2,1)S(1)} %get-tuple-element.73), channel_id=1, source_target_pairs={{0,4},{4,0},{8,12},{12,8},{16,20},{20,16},{24,28},{28,24},{1,5},{5... | collective-permute-start | bytes 221192 | tf_op jit(solution)/shard_map/ppermute | solution.py:351
  44.0 7.5 %collective-permute-start.15 = (bf16[3,96,128]{2,1,0:T(8,128)(2,1)S(1)}, bf16[3,96,128]{2,1,0:T(8,128)(2,1)S(1)}, u32[]{:S(2)}, u32[]{:S(2)}) collective-permute-start(bf16[3,96,128]{2,1,0:T(8,128)(2,1)S(1)} %get-tuple-element.75), channel_id=1, source_target_pairs={{0,4},{4,0},{8,12},{12,8},{16,20},{20,16},{24,28},{28,24},{1,5},{5... | collective-permute-start | bytes 221192 | tf_op jit(solution)/shard_map/ppermute | solution.py:351
  45.7 8.4 %collective-permute-start.10 = (bf16[3,96,128]{2,1,0:T(8,128)(2,1)S(1)}, bf16[3,96,128]{2,1,0:T(8,128)(2,1)S(1)}, u32[]{:S(2)}, u32[]{:S(2)}) collective-permute-start(bf16[3,96,128]{2,1,0:T(8,128)(2,1)S(1)} %get-tuple-element.69), channel_id=1, source_target_pairs={{0,4},{4,0},{8,12},{12,8},{16,20},{20,16},{24,28},{28,24},{1,5},{5... | collective-permute-start | bytes 221192 | tf_op jit(solution)/shard_map/ppermute | solution.py:351
  46.7 7.4 %collective-permute-start.12 = (bf16[3,96,128]{2,1,0:T(8,128)(2,1)S(1)}, bf16[3,96,128]{2,1,0:T(8,128)(2,1)S(1)}, u32[]{:S(2)}, u32[]{:S(2)}) collective-permute-start(bf16[3,96,128]{2,1,0:T(8,128)(2,1)S(1)} %shard_map.122), channel_id=1, source_target_pairs={{0,8},{4,12},{8,0},{12,4},{16,24},{20,28},{24,16},{28,20},{1,9},{5... | collective-permute-start | bytes 221192 | tf_op jit(solution)/shard_map/ppermute | solution.py:351
  48.8 7.6 %collective-permute-start.14 = (bf16[3,96,128]{2,1,0:T(8,128)(2,1)S(1)}, bf16[3,96,128]{2,1,0:T(8,128)(2,1)S(1)}, u32[]{:S(2)}, u32[]{:S(2)}) collective-permute-start(bf16[3,96,128]{2,1,0:T(8,128)(2,1)S(1)} %shard_map.123), channel_id=1, source_target_pairs={{0,16},{4,20},{8,24},{12,28},{16,0},{20,4},{24,8},{28,12},{1,17},{... | collective-permute-start | bytes 221192 | tf_op jit(solution)/shard_map/ppermute | solution.py:351
  51.5 6.3 %collective-permute-start.16 = (bf16[3,96,128]{2,1,0:T(8,128)(2,1)S(1)}, bf16[3,96,128]{2,1,0:T(8,128)(2,1)S(1)}, u32[]{:S(2)}, u32[]{:S(2)}) collective-permute-start(bf16[3,96,128]{2,1,0:T(8,128)(2,1)S(1)} %shard_map.124), channel_id=1, source_target_pairs={{0,24},{4,28},{8,16},{12,20},{16,8},{20,12},{24,0},{28,4},{1,25},{... | collective-permute-start | bytes 221192 | tf_op jit(solution)/shard_map/ppermute | solution.py:351
  58.4 14.3 %collective-permute-start.17 = (f32[9,96,384]{2,1,0:T(8,128)S(1)}, f32[9,96,384]{2,1,0:T(8,128)S(1)}, u32[]{:S(2)}, u32[]{:S(2)}) collective-permute-start(f32[9,96,384]{2,1,0:T(8,128)S(1)} %get-tuple-element.76), channel_id=1, source_target_pairs={{0,1},{1,0},{2,3},{3,2},{4,5},{5,4},{6,7},{7,6},{8,9},{9,8},{10,11... | collective-permute-start | bytes 3981320 | tf_op jit(solution)/shard_map/ppermute | solution.py:351
  58.5 6.1 %collective-permute-start.22 = (bf16[3,96,128]{2,1,0:T(8,128)(2,1)S(1)}, bf16[3,96,128]{2,1,0:T(8,128)(2,1)S(1)}, u32[]{:S(2)}, u32[]{:S(2)}) collective-permute-start(bf16[3,96,128]{2,1,0:T(8,128)(2,1)S(1)} %get-tuple-element.77.refs_7_.template_ref), channel_id=1, source_target_pairs={{0,8},{4,12},{8,0},{12,4},{16,24},{20,28},{24,16},{28,20},{1,9},{5... | collective-permute-start | bytes 221192 | tf_op jit(solution)/shard_map/ppermute | solution.py:351
  59.6 6.7 %collective-permute-start.20 = (bf16[3,96,128]{2,1,0:T(8,128)(2,1)S(1)}, bf16[3,96,128]{2,1,0:T(8,128)(2,1)S(1)}, u32[]{:S(2)}, u32[]{:S(2)}) collective-permute-start(bf16[3,96,128]{2,1,0:T(8,128)(2,1)S(1)} %get-tuple-element.77.refs_7_.template_ref), channel_id=1, source_target_pairs={{0,16},{4,20},{8,24},{12,28},{16,0},{20,4},{24,8},{28,12},{1,17},{... | collective-permute-start | bytes 221192 | tf_op jit(solution)/shard_map/ppermute | solution.py:351
  61.8 6.6 %collective-permute-start.18 = (bf16[3,96,128]{2,1,0:T(8,128)(2,1)S(1)}, bf16[3,96,128]{2,1,0:T(8,128)(2,1)S(1)}, u32[]{:S(2)}, u32[]{:S(2)}) collective-permute-start(bf16[3,96,128]{2,1,0:T(8,128)(2,1)S(1)} %get-tuple-element.77.refs_7_.template_ref), channel_id=1, source_target_pairs={{0,24},{4,28},{8,16},{12,20},{16,8},{20,12},{24,0},{28,4},{1,25},{... | collective-permute-start | bytes 221192 | tf_op jit(solution)/shard_map/ppermute | solution.py:351
  63.0 7.5 %collective-permute-start.24 = (bf16[3,96,128]{2,1,0:T(8,128)(2,1)S(1)}, bf16[3,96,128]{2,1,0:T(8,128)(2,1)S(1)}, u32[]{:S(2)}, u32[]{:S(2)}) collective-permute-start(bf16[3,96,128]{2,1,0:T(8,128)(2,1)S(1)} %get-tuple-element.77.refs_7_.template_ref), channel_id=1, source_target_pairs={{0,4},{4,0},{8,12},{12,8},{16,20},{20,16},{24,28},{28,24},{1,5},{5... | collective-permute-start | bytes 221192 | tf_op jit(solution)/shard_map/ppermute | solution.py:351
  64.6 5.9 %collective-permute-start.23 = (bf16[3,96,128]{2,1,0:T(8,128)(2,1)S(1)}, bf16[3,96,128]{2,1,0:T(8,128)(2,1)S(1)}, u32[]{:S(2)}, u32[]{:S(2)}) collective-permute-start(bf16[3,96,128]{2,1,0:T(8,128)(2,1)S(1)} %collective-permute-done.22.refs_5_), channel_id=1, source_target_pairs={{0,4},{4,0},{8,12},{12,8},{16,20},{20,16},{24,28},{28,24},{1,5},{5... | collective-permute-start | bytes 221192 | tf_op jit(solution)/shard_map/ppermute | solution.py:351
  66.3 4.5 %collective-permute-start.21 = (bf16[3,96,128]{2,1,0:T(8,128)(2,1)S(1)}, bf16[3,96,128]{2,1,0:T(8,128)(2,1)S(1)}, u32[]{:S(2)}, u32[]{:S(2)}) collective-permute-start(bf16[3,96,128]{2,1,0:T(8,128)(2,1)S(1)} %collective-permute-done.20.refs_3_), channel_id=1, source_target_pairs={{0,4},{4,0},{8,12},{12,8},{16,20},{20,16},{24,28},{28,24},{1,5},{5... | collective-permute-start | bytes 221192 | tf_op jit(solution)/shard_map/ppermute | solution.py:351
  68.4 4.4 %collective-permute-start.19 = (bf16[3,96,128]{2,1,0:T(8,128)(2,1)S(1)}, bf16[3,96,128]{2,1,0:T(8,128)(2,1)S(1)}, u32[]{:S(2)}, u32[]{:S(2)}) collective-permute-start(bf16[3,96,128]{2,1,0:T(8,128)(2,1)S(1)} %collective-permute-done.18.refs_1_), channel_id=1, source_target_pairs={{0,4},{4,0},{8,12},{12,8},{16,20},{20,16},{24,28},{28,24},{1,5},{5... | collective-permute-start | bytes 221192 | tf_op jit(solution)/shard_map/ppermute | solution.py:351
  (6 other events, 32.1 us)

commit v7 on v6

--- a/solution.py
+++ b/solution.py
@@ -9,8 +9,8 @@
 
 TILE = 128
 ALIGN = 16
-CHUNKS = (4, 3, 2)
-BLOCK = 48
+CHUNKS = (3, 4, 2)
+BLOCK = 32
 DEPTH = 256
 MIB = 1024 * 1024
 VMEM = 20 * MIB
@@ -200,7 +200,9 @@
             ring = warped_ref[g, pl.ds(at, band + 2 * pad), :]
             ring = jnp.concatenate([ring, jnp.zeros((band + 2 * pad, TILE), BF16)], axis=1)
             stack = stacks[m][g]
-            stack[:, span * inner :, :] = jnp.zeros((blocks, DEPTH - span * inner, width), BF16)
+            if span * inner < DEPTH:
+                rest = (blocks, DEPTH - span * inner, width)
+                stack[:, span * inner :, :] = jnp.zeros(rest, BF16)
             for b in range(inner):
                 turn = (inner // 2 - b) % width
                 shifted = pltpu.roll(ring, turn, 1) if turn else ring

time: 74.9 us -> 73.9 us (0.987)
  Pallas kernels: 24.7 us -> 23 us
  local copies, waits for them, and re-layouts: 1.54 us -> 2.48 us
    pallas_call x4, Pallas kernels: 12.7 us -> 11.8 us  [match_chunk(): pl.pallas_call(functools.partial(match_kernel, start=start, count=count,...]
    pad x1, local copies, waits for them, and re-layouts: 0.81 us -> 1.74 us  [per_device(): jnp.pad(profiles, ((0, 0), (0, rows_kept - tap_count + -rows_kept % 8), (...]
  transfers between devices with their start and end apart: 25 -> 25, of which waited for: 9 -> 8; matrix products, arithmetic and copies ran while one was open for 4% -> 6% of each run, Pallas kernels for 27% -> 25%
where the time goes in v7:
time: 73.9 us; the launch traced here: 73.5 us
  starting transfers between devices  30.3 us (41%)
  Pallas kernels  23 us (31%)
  waiting for transfers between devices  15.1 us (20%)
  local copies, waits for them, and re-layouts  2.48 us (3%)
  matrix products  1.74 us (2%)
  between operations  0.79 us (1%)
    ppermute x25, starting transfers between devices, exchange(): return lax.ppermute(value, axis, [(i, i ^ mask) for i in range(size)])  30.3 us
    ppermute x25, waiting for transfers between devices, exchange(): return lax.ppermute(value, axis, [(i, i ^ mask) for i in range(size)])  15.1 us
    pallas_call x4, Pallas kernels, match_chunk(): pl.pallas_call(functools.partial(match_kernel, start=start, count=count,...  11.8 us
    pallas_call x1, Pallas kernels, per_device(): pl.pallas_call(functools.partial(target_kernel, tiles=tiles), in_specs=[p...  4.88 us
    pallas_call x3, Pallas kernels, pack(): pl.pallas_call(functools.partial(pack_kernel, chunks=chunks, edges=siblin...  3.23 us
    pad x1, local copies, waits for them, and re-layouts, per_device(): jnp.pad(profiles, ((0, 0), (0, rows_kept - tap_count + -rows_kept % 8), (...  1.74 us
    dot_general x1, matrix products, per_device(): jnp.einsum('nkt,ku->nut', scaled, taps.astype(BF16), preferred_element_ty...  1.74 us
    pallas_call x1, Pallas kernels, per_device(): pl.pallas_call(functools.partial(difference_kernel, group=group, masks=ma...  1.73 us
  transfers between devices with their start and end apart: 25, of which 8 were waited for; matrix products, arithmetic and copies ran while one was open for 6% of the time, Pallas kernels for 25%

profile of v7, /device:TPU:0, one launch (start us, length us, event | category | flops | bytes accessed | tf_op | source)
XLA Modules:
  0.0 73.5 jit_solution(18052658164492155047)
XLA Ops:
  2.3 3.0 %collective-permute-start.5 = (bf16[3,96,384]{2,1,0:T(8,128)(2,1)S(1)}, bf16[3,96,384]{2,1,0:T(8,128)(2,1)S(1)}, u32[]{:S(2)}, u32[]{:S(2)}) collective-permute-start(bf16[3,96,384]{2,1,0:T(8,128)(2,1)S(1)} %get-tuple-element.50), channel_id=1, source_target_pairs={{0,2},{1,3},{2,0},{3,1},{4,6},{5,7},{6,4},{7,5},{8,10},{9,11},{10,... | collective-permute-start | bytes 663560 | tf_op jit(solution)/shard_map/ppermute | solution.py:353
  6.0 1.7 %convolution_bitcast_fusion = f32[18,21,21]{2,1,0:T(8,128)} fusion(f32[21,21]{1,0:T(8,128)} %param.14, f32[18,21]{1,0:T(8,128)S(1)} %mul.15), kind=kOutput, calls=%fused_computation | convolution fusion | flops 349713 | bytes 35028 | tf_op jit(solution)/shard_map/profiles/nkt,ku->nut/dot_general | solution.py:406
  7.8 1.7 %pad.4.refs_3_ = f32[18,24,128]{2,1,0:T(8,128)} pad(f32[18,21,21]{2,1,0:T(8,128)} %convolution_bitcast_fusion, f32[]{:T(128)} %constant.11.clone.1), padding=0_0x0_3x6_101 | pad | bytes 252940 | tf_op jit(solution)/shard_map/profiles/jit(_pad)/pad | solution.py:411
  10.6 1.6 %collective-permute-start.4 = (bf16[9,16,384]{2,1,0:T(8,128)(2,1)S(1)}, bf16[9,16,384]{2,1,0:T(8,128)(2,1)S(1)}, u32[]{:S(2)}, u32[]{:S(2)}) collective-permute-start(bf16[9,16,384]{2,1,0:T(8,128)(2,1)S(1)} %get-tuple-element.40.refs_4_), channel_id=1, source_target_pairs={{0,2},{1,3},{2,0},{3,1},{4,6},{5,7},{6,4},{7,5},{8,10},{9,11},{10,... | collective-permute-start | bytes 331784 | tf_op jit(solution)/shard_map/ppermute | solution.py:353
  15.2 4.9 %shard_map.114 = (s32[54]{0:T(128)S(1)}, s32[27]{0:T(128)S(1)}, f32[9]{0:T(128)S(1)}, f32[3]{0:T(128)S(1)}, bf16[9,96,384]{2,1,0:T(8,128)(2,1)S(1)}, /*index=5*/...) custom-call(s32[2]{0:T(128)S(1)} %pad_add_fusion.place_ref, s32[432]{0:T(512)S(1)} %bitcast.14, ...), custom_call_target="tpu_custom_call" | custom-call | tf_op jit(solution)/shard_map/pallas_call | solution.py:422
  21.9 3.6 %shard_map.117 = (f32[9,96,384]{2,1,0:T(8,128)S(1)}, f32[9,96,384]{2,1,0:T(8,128)S(1)}, f32[24,96,128]{2,1,0:T(8,128)S(1)}, f32[24,96,128]{2,1,0:T(8,128)S(1)}) custom-call(s32[27]{0:T(128)S(1)} %get-tuple-element.42.slot_ref, f32[9]{0:T(128)S(1)} %get-tuple-element.43.weight_ref, s32[1]{0:T(128)} %bitcast.1.row_ref, ...), custom_call_target="tpu_custom_call" | custom-call | flops 6000000000 | bytes 3000000 | tf_op jit(solution)/shard_map/pallas_call | solution.py:270
  25.6 5.3 %collective-permute-done.7.refs_7_ = bf16[4,96,384]{2,1,0:T(8,128)(2,1)S(1)} collective-permute-done((bf16[4,96,384]{2,1,0:T(8,128)(2,1)S(1)}, bf16[4,96,384]{2,1,0:T(8,128)(2,1)S(1)}, u32[]{:S(2)}, u32[]{:S(2)}) %collective-permute-start.7) | collective-permute-done | bytes 294944 | tf_op jit(solution)/shard_map/ppermute | solution.py:353
  30.9 4.5 %shard_map.118 = (f32[9,96,384]{2,1,0:T(8,128)S(1)}, f32[9,96,384]{2,1,0:T(8,128)S(1)}, f32[24,96,128]{2,1,0:T(8,128)S(1)}, f32[24,96,128]{2,1,0:T(8,128)S(1)}) custom-call(s32[27]{0:T(128)S(1)} %get-tuple-element.42.slot_ref, f32[9]{0:T(128)S(1)} %get-tuple-element.43.weight_ref, ...), custom_call_target="tpu_custom_call", output_to_operand_aliasing={{0}: (12, {}), {1}: (13, {}), {2}: (14, {}), {3}: (15, {})} | custom-call | flops 8000000000 | bytes 4000000 | tf_op jit(solution)/shard_map/pallas_call | solution.py:270
  36.5 2.1 %shard_map.119 = (f32[9,96,384]{2,1,0:T(8,128)S(1)}, f32[24,96,128]{2,1,0:T(8,128)S(1)}, bf16[24,96,128]{2,1,0:T(8,128)(2,1)S(1)}, bf16[2,224,384]{2,1,0:T(8,128)(2,1)S(1)}) custom-call(s32[27]{0:T(128)S(1)} %get-tuple-element.42.slot_ref, f32[9]{0:T(128)S(1)} %get-tuple-element.43.weight_ref, ...), custom_call_target="tpu_custom_call", output_to_operand_aliasing={{0}: (12, {}), {1}: (13, {})} | custom-call | flops 2000000000 | bytes 2000000 | tf_op jit(solution)/shard_map/pallas_call | solution.py:270
  39.1 1.5 %shard_map.120 = (f32[9,96,384]{2,1,0:T(8,128)S(1)}, f32[24,96,128]{2,1,0:T(8,128)S(1)}) custom-call(s32[27]{0:T(128)S(1)} %get-tuple-element.42.slot_ref, f32[9]{0:T(128)S(1)} %get-tuple-element.43.weight_ref, s32[1]{0:T(128)} %bitcast.1.row_ref, f32[9,24,128]{2,1,0:T(8,128)S(1)} %get-tuple-element.44.refs_0_, ...), custom_call_target="tpu_custom_call", output_to_operand_aliasing={{0}: (5, {}), {1}: (6, {})} | custom-call | flops 2000000000 | bytes 2000000 | tf_op jit(solution)/shard_map/pallas_call | solution.py:270
  40.9 1.8 %collective-permute-start.11 = (bf16[3,96,128]{2,1,0:T(8,128)(2,1)S(1)}, bf16[3,96,128]{2,1,0:T(8,128)(2,1)S(1)}, u32[]{:S(2)}, u32[]{:S(2)}) collective-permute-start(bf16[3,96,128]{2,1,0:T(8,128)(2,1)S(1)} %get-tuple-element.71), channel_id=1, source_target_pairs={{0,4},{4,0},{8,12},{12,8},{16,20},{20,16},{24,28},{28,24},{1,5},{5... | collective-permute-start | bytes 221192 | tf_op jit(solution)/shard_map/ppermute | solution.py:353
  43.0 1.7 %collective-permute-start.15 = (bf16[3,96,128]{2,1,0:T(8,128)(2,1)S(1)}, bf16[3,96,128]{2,1,0:T(8,128)(2,1)S(1)}, u32[]{:S(2)}, u32[]{:S(2)}) collective-permute-start(bf16[3,96,128]{2,1,0:T(8,128)(2,1)S(1)} %get-tuple-element.75), channel_id=1, source_target_pairs={{0,4},{4,0},{8,12},{12,8},{16,20},{20,16},{24,28},{28,24},{1,5},{5... | collective-permute-start | bytes 221192 | tf_op jit(solution)/shard_map/ppermute | solution.py:353
  45.7 2.1 %collective-permute-start.12 = (bf16[3,96,128]{2,1,0:T(8,128)(2,1)S(1)}, bf16[3,96,128]{2,1,0:T(8,128)(2,1)S(1)}, u32[]{:S(2)}, u32[]{:S(2)}) collective-permute-start(bf16[3,96,128]{2,1,0:T(8,128)(2,1)S(1)} %shard_map.122), channel_id=1, source_target_pairs={{0,8},{4,12},{8,0},{12,4},{16,24},{20,28},{24,16},{28,20},{1,9},{5... | collective-permute-start | bytes 221192 | tf_op jit(solution)/shard_map/ppermute | solution.py:353
  47.8 2.6 %collective-permute-start.14 = (bf16[3,96,128]{2,1,0:T(8,128)(2,1)S(1)}, bf16[3,96,128]{2,1,0:T(8,128)(2,1)S(1)}, u32[]{:S(2)}, u32[]{:S(2)}) collective-permute-start(bf16[3,96,128]{2,1,0:T(8,128)(2,1)S(1)} %shard_map.123), channel_id=1, source_target_pairs={{0,16},{4,20},{8,24},{12,28},{16,0},{20,4},{24,8},{28,12},{1,17},{... | collective-permute-start | bytes 221192 | tf_op jit(solution)/shard_map/ppermute | solution.py:353
  50.5 2.6 %collective-permute-start.16 = (bf16[3,96,128]{2,1,0:T(8,128)(2,1)S(1)}, bf16[3,96,128]{2,1,0:T(8,128)(2,1)S(1)}, u32[]{:S(2)}, u32[]{:S(2)}) collective-permute-start(bf16[3,96,128]{2,1,0:T(8,128)(2,1)S(1)} %shard_map.124), channel_id=1, source_target_pairs={{0,24},{4,28},{8,16},{12,20},{16,8},{20,12},{24,0},{28,4},{1,25},{... | collective-permute-start | bytes 221192 | tf_op jit(solution)/shard_map/ppermute | solution.py:353
  53.0 2.2 %collective-permute-done.14.refs_3_ = bf16[3,96,128]{2,1,0:T(8,128)(2,1)S(1)} collective-permute-done((bf16[3,96,128]{2,1,0:T(8,128)(2,1)S(1)}, bf16[3,96,128]{2,1,0:T(8,128)(2,1)S(1)}, u32[]{:S(2)}, u32[]{:S(2)}) %collective-permute-start.14) | collective-permute-done | bytes 73760 | tf_op jit(solution)/shard_map/ppermute | solution.py:353
  55.3 1.5 %collective-permute-done.16.refs_4_ = bf16[3,96,128]{2,1,0:T(8,128)(2,1)S(1)} collective-permute-done((bf16[3,96,128]{2,1,0:T(8,128)(2,1)S(1)}, bf16[3,96,128]{2,1,0:T(8,128)(2,1)S(1)}, u32[]{:S(2)}, u32[]{:S(2)}) %collective-permute-start.16) | collective-permute-done | bytes 73760 | tf_op jit(solution)/shard_map/ppermute | solution.py:353
  58.6 2.2 %collective-permute-start.20 = (bf16[3,96,128]{2,1,0:T(8,128)(2,1)S(1)}, bf16[3,96,128]{2,1,0:T(8,128)(2,1)S(1)}, u32[]{:S(2)}, u32[]{:S(2)}) collective-permute-start(bf16[3,96,128]{2,1,0:T(8,128)(2,1)S(1)} %get-tuple-element.77.refs_7_.template_ref), channel_id=1, source_target_pairs={{0,16},{4,20},{8,24},{12,28},{16,0},{20,4},{24,8},{28,12},{1,17},{... | collective-permute-start | bytes 221192 | tf_op jit(solution)/shard_map/ppermute | solution.py:353
  61.9 1.6 %collective-permute-start.24 = (bf16[3,96,128]{2,1,0:T(8,128)(2,1)S(1)}, bf16[3,96,128]{2,1,0:T(8,128)(2,1)S(1)}, u32[]{:S(2)}, u32[]{:S(2)}) collective-permute-start(bf16[3,96,128]{2,1,0:T(8,128)(2,1)S(1)} %get-tuple-element.77.refs_7_.template_ref), channel_id=1, source_target_pairs={{0,4},{4,0},{8,12},{12,8},{16,20},{20,16},{24,28},{28,24},{1,5},{5... | collective-permute-start | bytes 221192 | tf_op jit(solution)/shard_map/ppermute | solution.py:353
  64.0 1.6 %collective-permute-start.21 = (bf16[3,96,128]{2,1,0:T(8,128)(2,1)S(1)}, bf16[3,96,128]{2,1,0:T(8,128)(2,1)S(1)}, u32[]{:S(2)}, u32[]{:S(2)}) collective-permute-start(bf16[3,96,128]{2,1,0:T(8,128)(2,1)S(1)} %collective-permute-done.20.refs_3_), channel_id=1, source_target_pairs={{0,4},{4,0},{8,12},{12,8},{16,20},{20,16},{24,28},{28,24},{1,5},{5... | collective-permute-start | bytes 221192 | tf_op jit(solution)/shard_map/ppermute | solution.py:353
  65.6 1.9 %collective-permute-done.18.refs_1_ = bf16[3,96,128]{2,1,0:T(8,128)(2,1)S(1)} collective-permute-done((bf16[3,96,128]{2,1,0:T(8,128)(2,1)S(1)}, bf16[3,96,128]{2,1,0:T(8,128)(2,1)S(1)}, u32[]{:S(2)}, u32[]{:S(2)}) %collective-permute-start.18) | collective-permute-done | bytes 73760 | tf_op jit(solution)/shard_map/ppermute | solution.py:353
  67.4 1.4 %collective-permute-start.19 = (bf16[3,96,128]{2,1,0:T(8,128)(2,1)S(1)}, bf16[3,96,128]{2,1,0:T(8,128)(2,1)S(1)}, u32[]{:S(2)}, u32[]{:S(2)}) collective-permute-start(bf16[3,96,128]{2,1,0:T(8,128)(2,1)S(1)} %collective-permute-done.18.refs_1_), channel_id=1, source_target_pairs={{0,4},{4,0},{8,12},{12,8},{16,20},{20,16},{24,28},{28,24},{1,5},{5... | collective-permute-start | bytes 221192 | tf_op jit(solution)/shard_map/ppermute | solution.py:353
  69.5 2.2 %collective-permute-done.19.refs_0_ = bf16[3,96,128]{2,1,0:T(8,128)(2,1)S(1)} collective-permute-done((bf16[3,96,128]{2,1,0:T(8,128)(2,1)S(1)}, bf16[3,96,128]{2,1,0:T(8,128)(2,1)S(1)}, u32[]{:S(2)}, u32[]{:S(2)}) %collective-permute-start.19) | collective-permute-done | bytes 73760 | tf_op jit(solution)/shard_map/ppermute | solution.py:353
  71.8 1.7 %shard_map.126 = bf16[18,96,384]{2,1,0:T(8,128)(2,1)} custom-call(s32[54]{0:T(128)S(1)} %get-tuple-element.41.slot_ref, s32[1]{0:T(128)} %bitcast.1.row_ref, f32[9,96,384]{2,1,0:T(8,128)S(1)} %get-tuple-element.63.own_ref, f32[9,96,384]{2,1,0:T(8,128)S(1)} %collective-permute-done.17.other_ref, bf16[3,96,128]{2,1,0:T(8,128)(2,1)S(1)} %collective-permute-done.19.refs_0_, ...), custom_call_target="tpu_custom_call" | custom-call | tf_op jit(solution)/shard_map/pallas_call | solution.py:512
  (55 shorter events, 15.5 us)
Async XLA Ops:
  0.6 8.9 %collective-permute-start = (bf16[18,96,384]{2,1,0:T(8,128)(2,1)}, bf16[18,96,384]{2,1,0:T(8,128)(2,1)S(1)}, u32[]{:S(2)}, u32[]{:S(2)}) collective-permute-start(bf16[18,96,384]{2,1,0:T(8,128)(2,1)} %bitcast.16), channel_id=1, source_target_pairs={{0,1},{1,0},{2,3},{3,2},{4,5},{5,4},{6,7},{7,6},{8,9},{9,8},{10,11... | collective-permute-start | bytes 3981320 | tf_op jit(solution)/shard_map/ppermute | solution.py:353
  1.1 19.3 %collective-permute-start.1 = (bf16[18,96,384]{2,1,0:T(8,128)(2,1)}, bf16[18,96,384]{2,1,0:T(8,128)(2,1)S(1)}, u32[]{:S(2)}, u32[]{:S(2)}) collective-permute-start(bf16[18,96,384]{2,1,0:T(8,128)(2,1)} %bitcast.21), channel_id=1, source_target_pairs={{0,1},{1,0},{2,3},{3,2},{4,5},{5,4},{6,7},{7,6},{8,9},{9,8},{10,11... | collective-permute-start | bytes 3981320 | tf_op jit(solution)/shard_map/ppermute | solution.py:353
  2.3 9.9 %collective-permute-start.5 = (bf16[3,96,384]{2,1,0:T(8,128)(2,1)S(1)}, bf16[3,96,384]{2,1,0:T(8,128)(2,1)S(1)}, u32[]{:S(2)}, u32[]{:S(2)}) collective-permute-start(bf16[3,96,384]{2,1,0:T(8,128)(2,1)S(1)} %get-tuple-element.50), channel_id=1, source_target_pairs={{0,2},{1,3},{2,0},{3,1},{4,6},{5,7},{6,4},{7,5},{8,10},{9,11},{10,... | collective-permute-start | bytes 663560 | tf_op jit(solution)/shard_map/ppermute | solution.py:353
  5.3 14.7 %collective-permute-start.8 = (bf16[3,96,384]{2,1,0:T(8,128)(2,1)S(1)}, bf16[3,96,384]{2,1,0:T(8,128)(2,1)S(1)}, u32[]{:S(2)}, u32[]{:S(2)}) collective-permute-start(bf16[3,96,384]{2,1,0:T(8,128)(2,1)S(1)} %get-tuple-element.53), channel_id=1, source_target_pairs={{0,3},{1,2},{2,1},{3,0},{4,7},{5,6},{6,5},{7,4},{8,11},{9,10},{10,... | collective-permute-start | bytes 663560 | tf_op jit(solution)/shard_map/ppermute | solution.py:353
  10.6 11.4 %collective-permute-start.4 = (bf16[9,16,384]{2,1,0:T(8,128)(2,1)S(1)}, bf16[9,16,384]{2,1,0:T(8,128)(2,1)S(1)}, u32[]{:S(2)}, u32[]{:S(2)}) collective-permute-start(bf16[9,16,384]{2,1,0:T(8,128)(2,1)S(1)} %get-tuple-element.40.refs_4_), channel_id=1, source_target_pairs={{0,2},{1,3},{2,0},{3,1},{4,6},{5,7},{6,4},{7,5},{8,10},{9,11},{10,... | collective-permute-start | bytes 331784 | tf_op jit(solution)/shard_map/ppermute | solution.py:353
  13.4 12.2 %collective-permute-start.6 = (bf16[4,96,384]{2,1,0:T(8,128)(2,1)S(1)}, bf16[4,96,384]{2,1,0:T(8,128)(2,1)S(1)}, u32[]{:S(2)}, u32[]{:S(2)}) collective-permute-start(bf16[4,96,384]{2,1,0:T(8,128)(2,1)S(1)} %get-tuple-element.51), channel_id=1, source_target_pairs={{0,2},{1,3},{2,0},{3,1},{4,6},{5,7},{6,4},{7,5},{8,10},{9,11},{10,... | collective-permute-start | bytes 884744 | tf_op jit(solution)/shard_map/ppermute | solution.py:353
  14.8 16.1 %collective-permute-start.7 = (bf16[4,96,384]{2,1,0:T(8,128)(2,1)S(1)}, bf16[4,96,384]{2,1,0:T(8,128)(2,1)S(1)}, u32[]{:S(2)}, u32[]{:S(2)}) collective-permute-start(bf16[4,96,384]{2,1,0:T(8,128)(2,1)S(1)} %get-tuple-element.52), channel_id=1, source_target_pairs={{0,3},{1,2},{2,1},{3,0},{4,7},{5,6},{6,5},{7,4},{8,11},{9,10},{10,... | collective-permute-start | bytes 884744 | tf_op jit(solution)/shard_map/ppermute | solution.py:353
  20.1 15.3 %collective-permute-start.2 = (bf16[2,96,384]{2,1,0:T(8,128)(2,1)S(1)}, bf16[2,96,384]{2,1,0:T(8,128)(2,1)S(1)}, u32[]{:S(2)}, u32[]{:S(2)}) collective-permute-start(bf16[2,96,384]{2,1,0:T(8,128)(2,1)S(1)} %get-tuple-element.48), channel_id=1, source_target_pairs={{0,2},{1,3},{2,0},{3,1},{4,6},{5,7},{6,4},{7,5},{8,10},{9,11},{10,... | collective-permute-start | bytes 442376 | tf_op jit(solution)/shard_map/ppermute | solution.py:353
  20.5 16.0 %collective-permute-start.3 = (bf16[2,96,384]{2,1,0:T(8,128)(2,1)S(1)}, bf16[2,96,384]{2,1,0:T(8,128)(2,1)S(1)}, u32[]{:S(2)}, u32[]{:S(2)}) collective-permute-start(bf16[2,96,384]{2,1,0:T(8,128)(2,1)S(1)} %get-tuple-element.49), channel_id=1, source_target_pairs={{0,3},{1,2},{2,1},{3,0},{4,7},{5,6},{6,5},{7,4},{8,11},{9,10},{10,... | collective-permute-start | bytes 442376 | tf_op jit(solution)/shard_map/ppermute | solution.py:353
  40.9 4.8 %collective-permute-start.11 = (bf16[3,96,128]{2,1,0:T(8,128)(2,1)S(1)}, bf16[3,96,128]{2,1,0:T(8,128)(2,1)S(1)}, u32[]{:S(2)}, u32[]{:S(2)}) collective-permute-start(bf16[3,96,128]{2,1,0:T(8,128)(2,1)S(1)} %get-tuple-element.71), channel_id=1, source_target_pairs={{0,4},{4,0},{8,12},{12,8},{16,20},{20,16},{24,28},{28,24},{1,5},{5... | collective-permute-start | bytes 221192 | tf_op jit(solution)/shard_map/ppermute | solution.py:353
  42.6 5.1 %collective-permute-start.13 = (bf16[3,96,128]{2,1,0:T(8,128)(2,1)S(1)}, bf16[3,96,128]{2,1,0:T(8,128)(2,1)S(1)}, u32[]{:S(2)}, u32[]{:S(2)}) collective-permute-start(bf16[3,96,128]{2,1,0:T(8,128)(2,1)S(1)} %get-tuple-element.73), channel_id=1, source_target_pairs={{0,4},{4,0},{8,12},{12,8},{16,20},{20,16},{24,28},{28,24},{1,5},{5... | collective-permute-start | bytes 221192 | tf_op jit(solution)/shard_map/ppermute | solution.py:353
  43.0 7.5 %collective-permute-start.15 = (bf16[3,96,128]{2,1,0:T(8,128)(2,1)S(1)}, bf16[3,96,128]{2,1,0:T(8,128)(2,1)S(1)}, u32[]{:S(2)}, u32[]{:S(2)}) collective-permute-start(bf16[3,96,128]{2,1,0:T(8,128)(2,1)S(1)} %get-tuple-element.75), channel_id=1, source_target_pairs={{0,4},{4,0},{8,12},{12,8},{16,20},{20,16},{24,28},{28,24},{1,5},{5... | collective-permute-start | bytes 221192 | tf_op jit(solution)/shard_map/ppermute | solution.py:353
  44.7 8.4 %collective-permute-start.10 = (bf16[3,96,128]{2,1,0:T(8,128)(2,1)S(1)}, bf16[3,96,128]{2,1,0:T(8,128)(2,1)S(1)}, u32[]{:S(2)}, u32[]{:S(2)}) collective-permute-start(bf16[3,96,128]{2,1,0:T(8,128)(2,1)S(1)} %get-tuple-element.69), channel_id=1, source_target_pairs={{0,4},{4,0},{8,12},{12,8},{16,20},{20,16},{24,28},{28,24},{1,5},{5... | collective-permute-start | bytes 221192 | tf_op jit(solution)/shard_map/ppermute | solution.py:353
  45.7 7.4 %collective-permute-start.12 = (bf16[3,96,128]{2,1,0:T(8,128)(2,1)S(1)}, bf16[3,96,128]{2,1,0:T(8,128)(2,1)S(1)}, u32[]{:S(2)}, u32[]{:S(2)}) collective-permute-start(bf16[3,96,128]{2,1,0:T(8,128)(2,1)S(1)} %shard_map.122), channel_id=1, source_target_pairs={{0,8},{4,12},{8,0},{12,4},{16,24},{20,28},{24,16},{28,20},{1,9},{5... | collective-permute-start | bytes 221192 | tf_op jit(solution)/shard_map/ppermute | solution.py:353
  47.8 7.5 %collective-permute-start.14 = (bf16[3,96,128]{2,1,0:T(8,128)(2,1)S(1)}, bf16[3,96,128]{2,1,0:T(8,128)(2,1)S(1)}, u32[]{:S(2)}, u32[]{:S(2)}) collective-permute-start(bf16[3,96,128]{2,1,0:T(8,128)(2,1)S(1)} %shard_map.123), channel_id=1, source_target_pairs={{0,16},{4,20},{8,24},{12,28},{16,0},{20,4},{24,8},{28,12},{1,17},{... | collective-permute-start | bytes 221192 | tf_op jit(solution)/shard_map/ppermute | solution.py:353
  50.5 6.3 %collective-permute-start.16 = (bf16[3,96,128]{2,1,0:T(8,128)(2,1)S(1)}, bf16[3,96,128]{2,1,0:T(8,128)(2,1)S(1)}, u32[]{:S(2)}, u32[]{:S(2)}) collective-permute-start(bf16[3,96,128]{2,1,0:T(8,128)(2,1)S(1)} %shard_map.124), channel_id=1, source_target_pairs={{0,24},{4,28},{8,16},{12,20},{16,8},{20,12},{24,0},{28,4},{1,25},{... | collective-permute-start | bytes 221192 | tf_op jit(solution)/shard_map/ppermute | solution.py:353
  57.4 14.4 %collective-permute-start.17 = (f32[9,96,384]{2,1,0:T(8,128)S(1)}, f32[9,96,384]{2,1,0:T(8,128)S(1)}, u32[]{:S(2)}, u32[]{:S(2)}) collective-permute-start(f32[9,96,384]{2,1,0:T(8,128)S(1)} %get-tuple-element.76), channel_id=1, source_target_pairs={{0,1},{1,0},{2,3},{3,2},{4,5},{5,4},{6,7},{7,6},{8,9},{9,8},{10,11... | collective-permute-start | bytes 3981320 | tf_op jit(solution)/shard_map/ppermute | solution.py:353
  57.5 6.1 %collective-permute-start.22 = (bf16[3,96,128]{2,1,0:T(8,128)(2,1)S(1)}, bf16[3,96,128]{2,1,0:T(8,128)(2,1)S(1)}, u32[]{:S(2)}, u32[]{:S(2)}) collective-permute-start(bf16[3,96,128]{2,1,0:T(8,128)(2,1)S(1)} %get-tuple-element.77.refs_7_.template_ref), channel_id=1, source_target_pairs={{0,8},{4,12},{8,0},{12,4},{16,24},{20,28},{24,16},{28,20},{1,9},{5... | collective-permute-start | bytes 221192 | tf_op jit(solution)/shard_map/ppermute | solution.py:353
  58.6 5.4 %collective-permute-start.20 = (bf16[3,96,128]{2,1,0:T(8,128)(2,1)S(1)}, bf16[3,96,128]{2,1,0:T(8,128)(2,1)S(1)}, u32[]{:S(2)}, u32[]{:S(2)}) collective-permute-start(bf16[3,96,128]{2,1,0:T(8,128)(2,1)S(1)} %get-tuple-element.77.refs_7_.template_ref), channel_id=1, source_target_pairs={{0,16},{4,20},{8,24},{12,28},{16,0},{20,4},{24,8},{28,12},{1,17},{... | collective-permute-start | bytes 221192 | tf_op jit(solution)/shard_map/ppermute | solution.py:353
  60.8 6.6 %collective-permute-start.18 = (bf16[3,96,128]{2,1,0:T(8,128)(2,1)S(1)}, bf16[3,96,128]{2,1,0:T(8,128)(2,1)S(1)}, u32[]{:S(2)}, u32[]{:S(2)}) collective-permute-start(bf16[3,96,128]{2,1,0:T(8,128)(2,1)S(1)} %get-tuple-element.77.refs_7_.template_ref), channel_id=1, source_target_pairs={{0,24},{4,28},{8,16},{12,20},{16,8},{20,12},{24,0},{28,4},{1,25},{... | collective-permute-start | bytes 221192 | tf_op jit(solution)/shard_map/ppermute | solution.py:353
  61.9 7.6 %collective-permute-start.24 = (bf16[3,96,128]{2,1,0:T(8,128)(2,1)S(1)}, bf16[3,96,128]{2,1,0:T(8,128)(2,1)S(1)}, u32[]{:S(2)}, u32[]{:S(2)}) collective-permute-start(bf16[3,96,128]{2,1,0:T(8,128)(2,1)S(1)} %get-tuple-element.77.refs_7_.template_ref), channel_id=1, source_target_pairs={{0,4},{4,0},{8,12},{12,8},{16,20},{20,16},{24,28},{28,24},{1,5},{5... | collective-permute-start | bytes 221192 | tf_op jit(solution)/shard_map/ppermute | solution.py:353
  63.6 6.0 %collective-permute-start.23 = (bf16[3,96,128]{2,1,0:T(8,128)(2,1)S(1)}, bf16[3,96,128]{2,1,0:T(8,128)(2,1)S(1)}, u32[]{:S(2)}, u32[]{:S(2)}) collective-permute-start(bf16[3,96,128]{2,1,0:T(8,128)(2,1)S(1)} %collective-permute-done.22.refs_5_), channel_id=1, source_target_pairs={{0,4},{4,0},{8,12},{12,8},{16,20},{20,16},{24,28},{28,24},{1,5},{5... | collective-permute-start | bytes 221192 | tf_op jit(solution)/shard_map/ppermute | solution.py:353
  64.0 5.6 %collective-permute-start.21 = (bf16[3,96,128]{2,1,0:T(8,128)(2,1)S(1)}, bf16[3,96,128]{2,1,0:T(8,128)(2,1)S(1)}, u32[]{:S(2)}, u32[]{:S(2)}) collective-permute-start(bf16[3,96,128]{2,1,0:T(8,128)(2,1)S(1)} %collective-permute-done.20.refs_3_), channel_id=1, source_target_pairs={{0,4},{4,0},{8,12},{12,8},{16,20},{20,16},{24,28},{28,24},{1,5},{5... | collective-permute-start | bytes 221192 | tf_op jit(solution)/shard_map/ppermute | solution.py:353
  67.4 4.4 %collective-permute-start.19 = (bf16[3,96,128]{2,1,0:T(8,128)(2,1)S(1)}, bf16[3,96,128]{2,1,0:T(8,128)(2,1)S(1)}, u32[]{:S(2)}, u32[]{:S(2)}) collective-permute-start(bf16[3,96,128]{2,1,0:T(8,128)(2,1)S(1)} %collective-permute-done.18.refs_1_), channel_id=1, source_target_pairs={{0,4},{4,0},{8,12},{12,8},{16,20},{20,16},{24,28},{28,24},{1,5},{5... | collective-permute-start | bytes 221192 | tf_op jit(solution)/shard_map/ppermute | solution.py:353
  (6 other events, 16.9 us)

commit v8 on v7

--- a/solution.py
+++ b/solution.py
@@ -9,7 +9,7 @@
 
 TILE = 128
 ALIGN = 16
-CHUNKS = (3, 4, 2)
+CHUNKS = (2, 5, 2)
 BLOCK = 32
 DEPTH = 256
 MIB = 1024 * 1024

time: 73.9 us -> 73.6 us (level)
  waiting for transfers between devices: 15.1 us -> 17.7 us
  local copies, waits for them, and re-layouts: 2.48 us -> 0.85 us
  matrix products: 1.74 us -> 0.27 us
    ppermute x25, waiting for transfers between devices: 15.1 us -> 17.7 us  [exchange(): return lax.ppermute(value, axis, [(i, i ^ mask) for i in range(size)])]
    dot_general x1, matrix products: 1.74 us -> 0.27 us  [per_device(): jnp.einsum('nkt,ku->nut', scaled, taps.astype(BF16), preferred_element_ty...]
    pad x1, local copies, waits for them, and re-layouts: 1.74 us -> 0.81 us  [per_device(): jnp.pad(profiles, ((0, 0), (0, rows_kept - tap_count + -rows_kept % 8), (...]
  transfers between devices with their start and end apart: 25 -> 25, of which waited for: 8 -> 10; matrix products, arithmetic and copies ran while one was open for 6% -> 2% of each run, Pallas kernels for 25% -> 25%
where the time goes in v8:
time: 73.6 us; the launch traced here: 73.4 us
  starting transfers between devices  30.7 us (42%)
  Pallas kernels  23.1 us (31%)
  waiting for transfers between devices  17.7 us (24%)
  local copies, waits for them, and re-layouts  0.85 us (1%)
  between operations  0.81 us (1%)
    ppermute x25, starting transfers between devices, exchange(): return lax.ppermute(value, axis, [(i, i ^ mask) for i in range(size)])  30.7 us
    ppermute x25, waiting for transfers between devices, exchange(): return lax.ppermute(value, axis, [(i, i ^ mask) for i in range(size)])  17.7 us
    pallas_call x4, Pallas kernels, match_chunk(): pl.pallas_call(functools.partial(match_kernel, start=start, count=count,...  11.9 us
    pallas_call x1, Pallas kernels, per_device(): pl.pallas_call(functools.partial(target_kernel, tiles=tiles), in_specs=[p...  4.88 us
    pallas_call x3, Pallas kernels, pack(): pl.pallas_call(functools.partial(pack_kernel, chunks=chunks, edges=siblin...  3.19 us
    pallas_call x1, Pallas kernels, per_device(): pl.pallas_call(functools.partial(difference_kernel, group=group, masks=ma...  1.73 us
  transfers between devices with their start and end apart: 25, of which 10 were waited for; matrix products, arithmetic and copies ran while one was open for 2% of the time, Pallas kernels for 25%

profile of v8, /device:TPU:0, one launch (start us, length us, event | category | flops | bytes accessed | tf_op | source)
XLA Modules:
  0.0 73.4 jit_solution(17134918095614240703)
XLA Ops:
  2.3 3.0 %collective-permute-start.5 = (bf16[2,96,384]{2,1,0:T(8,128)(2,1)S(1)}, bf16[2,96,384]{2,1,0:T(8,128)(2,1)S(1)}, u32[]{:S(2)}, u32[]{:S(2)}) collective-permute-start(bf16[2,96,384]{2,1,0:T(8,128)(2,1)S(1)} %get-tuple-element.50), channel_id=1, source_target_pairs={{0,2},{1,3},{2,0},{3,1},{4,6},{5,7},{6,4},{7,5},{8,10},{9,11},{10,... | collective-permute-start | bytes 442376 | tf_op jit(solution)/shard_map/ppermute | solution.py:353
  7.4 1.6 %collective-permute-start.4 = (bf16[9,16,384]{2,1,0:T(8,128)(2,1)S(1)}, bf16[9,16,384]{2,1,0:T(8,128)(2,1)S(1)}, u32[]{:S(2)}, u32[]{:S(2)}) collective-permute-start(bf16[9,16,384]{2,1,0:T(8,128)(2,1)S(1)} %get-tuple-element.40.refs_4_), channel_id=1, source_target_pairs={{0,2},{1,3},{2,0},{3,1},{4,6},{5,7},{6,4},{7,5},{8,10},{9,11},{10,... | collective-permute-start | bytes 331784 | tf_op jit(solution)/shard_map/ppermute | solution.py:353
  11.1 2.1 %collective-permute-start.6 = (bf16[5,96,384]{2,1,0:T(8,128)(2,1)S(1)}, bf16[5,96,384]{2,1,0:T(8,128)(2,1)S(1)}, u32[]{:S(2)}, u32[]{:S(2)}) collective-permute-start(bf16[5,96,384]{2,1,0:T(8,128)(2,1)S(1)} %get-tuple-element.51), channel_id=1, source_target_pairs={{0,2},{1,3},{2,0},{3,1},{4,6},{5,7},{6,4},{7,5},{8,10},{9,11},{10,... | collective-permute-start | bytes 1105928 | tf_op jit(solution)/shard_map/ppermute | solution.py:353
  13.2 4.9 %shard_map.114 = (s32[54]{0:T(128)S(1)}, s32[27]{0:T(128)S(1)}, f32[9]{0:T(128)S(1)}, f32[3]{0:T(128)S(1)}, bf16[9,96,384]{2,1,0:T(8,128)(2,1)S(1)}, /*index=5*/...) custom-call(s32[2]{0:T(128)S(1)} %pad_add_fusion.place_ref, s32[432]{0:T(512)S(1)} %bitcast.14, ...), custom_call_target="tpu_custom_call" | custom-call | tf_op jit(solution)/shard_map/pallas_call | solution.py:422
  18.3 1.7 %collective-permute-start.3 = (bf16[2,96,384]{2,1,0:T(8,128)(2,1)S(1)}, bf16[2,96,384]{2,1,0:T(8,128)(2,1)S(1)}, u32[]{:S(2)}, u32[]{:S(2)}) collective-permute-start(bf16[2,96,384]{2,1,0:T(8,128)(2,1)S(1)} %get-tuple-element.49), channel_id=1, source_target_pairs={{0,3},{1,2},{2,1},{3,0},{4,7},{5,6},{6,5},{7,4},{8,11},{9,10},{10,... | collective-permute-start | bytes 442376 | tf_op jit(solution)/shard_map/ppermute | solution.py:353
  20.0 2.9 %shard_map.117 = (f32[9,96,384]{2,1,0:T(8,128)S(1)}, f32[9,96,384]{2,1,0:T(8,128)S(1)}, f32[24,96,128]{2,1,0:T(8,128)S(1)}, f32[24,96,128]{2,1,0:T(8,128)S(1)}) custom-call(s32[27]{0:T(128)S(1)} %get-tuple-element.42.slot_ref, f32[9]{0:T(128)S(1)} %get-tuple-element.43.weight_ref, s32[1]{0:T(128)} %bitcast.1.row_ref, ...), custom_call_target="tpu_custom_call" | custom-call | flops 4000000000 | bytes 2000000 | tf_op jit(solution)/shard_map/pallas_call | solution.py:270
  23.4 7.5 %collective-permute-done.7.refs_7_ = bf16[5,96,384]{2,1,0:T(8,128)(2,1)S(1)} collective-permute-done((bf16[5,96,384]{2,1,0:T(8,128)(2,1)S(1)}, bf16[5,96,384]{2,1,0:T(8,128)(2,1)S(1)}, u32[]{:S(2)}, u32[]{:S(2)}) %collective-permute-start.7) | collective-permute-done | bytes 368672 | tf_op jit(solution)/shard_map/ppermute | solution.py:353
  30.8 5.3 %shard_map.118 = (f32[9,96,384]{2,1,0:T(8,128)S(1)}, f32[9,96,384]{2,1,0:T(8,128)S(1)}, f32[24,96,128]{2,1,0:T(8,128)S(1)}, f32[24,96,128]{2,1,0:T(8,128)S(1)}) custom-call(s32[27]{0:T(128)S(1)} %get-tuple-element.42.slot_ref, f32[9]{0:T(128)S(1)} %get-tuple-element.43.weight_ref, ...), custom_call_target="tpu_custom_call", output_to_operand_aliasing={{0}: (12, {}), {1}: (13, {}), {2}: (14, {}), {3}: (15, {})} | custom-call | flops 10000000000 | bytes 5000000 | tf_op jit(solution)/shard_map/pallas_call | solution.py:270
  36.5 2.1 %shard_map.119 = (f32[9,96,384]{2,1,0:T(8,128)S(1)}, f32[24,96,128]{2,1,0:T(8,128)S(1)}, bf16[24,96,128]{2,1,0:T(8,128)(2,1)S(1)}, bf16[2,224,384]{2,1,0:T(8,128)(2,1)S(1)}) custom-call(s32[27]{0:T(128)S(1)} %get-tuple-element.42.slot_ref, f32[9]{0:T(128)S(1)} %get-tuple-element.43.weight_ref, ...), custom_call_target="tpu_custom_call", output_to_operand_aliasing={{0}: (12, {}), {1}: (13, {})} | custom-call | flops 2000000000 | bytes 2000000 | tf_op jit(solution)/shard_map/pallas_call | solution.py:270
  39.1 1.5 %shard_map.120 = (f32[9,96,384]{2,1,0:T(8,128)S(1)}, f32[24,96,128]{2,1,0:T(8,128)S(1)}) custom-call(s32[27]{0:T(128)S(1)} %get-tuple-element.42.slot_ref, f32[9]{0:T(128)S(1)} %get-tuple-element.43.weight_ref, s32[1]{0:T(128)} %bitcast.1.row_ref, f32[9,24,128]{2,1,0:T(8,128)S(1)} %get-tuple-element.44.refs_0_, ...), custom_call_target="tpu_custom_call", output_to_operand_aliasing={{0}: (5, {}), {1}: (6, {})} | custom-call | flops 2000000000 | bytes 2000000 | tf_op jit(solution)/shard_map/pallas_call | solution.py:270
  40.8 1.8 %collective-permute-start.11 = (bf16[3,96,128]{2,1,0:T(8,128)(2,1)S(1)}, bf16[3,96,128]{2,1,0:T(8,128)(2,1)S(1)}, u32[]{:S(2)}, u32[]{:S(2)}) collective-permute-start(bf16[3,96,128]{2,1,0:T(8,128)(2,1)S(1)} %get-tuple-element.71), channel_id=1, source_target_pairs={{0,4},{4,0},{8,12},{12,8},{16,20},{20,16},{24,28},{28,24},{1,5},{5... | collective-permute-start | bytes 221192 | tf_op jit(solution)/shard_map/ppermute | solution.py:353
  42.9 1.7 %collective-permute-start.15 = (bf16[3,96,128]{2,1,0:T(8,128)(2,1)S(1)}, bf16[3,96,128]{2,1,0:T(8,128)(2,1)S(1)}, u32[]{:S(2)}, u32[]{:S(2)}) collective-permute-start(bf16[3,96,128]{2,1,0:T(8,128)(2,1)S(1)} %get-tuple-element.75), channel_id=1, source_target_pairs={{0,4},{4,0},{8,12},{12,8},{16,20},{20,16},{24,28},{28,24},{1,5},{5... | collective-permute-start | bytes 221192 | tf_op jit(solution)/shard_map/ppermute | solution.py:353
  45.6 2.1 %collective-permute-start.12 = (bf16[3,96,128]{2,1,0:T(8,128)(2,1)S(1)}, bf16[3,96,128]{2,1,0:T(8,128)(2,1)S(1)}, u32[]{:S(2)}, u32[]{:S(2)}) collective-permute-start(bf16[3,96,128]{2,1,0:T(8,128)(2,1)S(1)} %shard_map.122), channel_id=1, source_target_pairs={{0,8},{4,12},{8,0},{12,4},{16,24},{20,28},{24,16},{28,20},{1,9},{5... | collective-permute-start | bytes 221192 | tf_op jit(solution)/shard_map/ppermute | solution.py:353
  47.7 2.7 %collective-permute-start.14 = (bf16[3,96,128]{2,1,0:T(8,128)(2,1)S(1)}, bf16[3,96,128]{2,1,0:T(8,128)(2,1)S(1)}, u32[]{:S(2)}, u32[]{:S(2)}) collective-permute-start(bf16[3,96,128]{2,1,0:T(8,128)(2,1)S(1)} %shard_map.123), channel_id=1, source_target_pairs={{0,16},{4,20},{8,24},{12,28},{16,0},{20,4},{24,8},{28,12},{1,17},{... | collective-permute-start | bytes 221192 | tf_op jit(solution)/shard_map/ppermute | solution.py:353
  50.4 2.6 %collective-permute-start.16 = (bf16[3,96,128]{2,1,0:T(8,128)(2,1)S(1)}, bf16[3,96,128]{2,1,0:T(8,128)(2,1)S(1)}, u32[]{:S(2)}, u32[]{:S(2)}) collective-permute-start(bf16[3,96,128]{2,1,0:T(8,128)(2,1)S(1)} %shard_map.124), channel_id=1, source_target_pairs={{0,24},{4,28},{8,16},{12,20},{16,8},{20,12},{24,0},{28,4},{1,25},{... | collective-permute-start | bytes 221192 | tf_op jit(solution)/shard_map/ppermute | solution.py:353
  53.0 2.2 %collective-permute-done.14.refs_3_ = bf16[3,96,128]{2,1,0:T(8,128)(2,1)S(1)} collective-permute-done((bf16[3,96,128]{2,1,0:T(8,128)(2,1)S(1)}, bf16[3,96,128]{2,1,0:T(8,128)(2,1)S(1)}, u32[]{:S(2)}, u32[]{:S(2)}) %collective-permute-start.14) | collective-permute-done | bytes 73760 | tf_op jit(solution)/shard_map/ppermute | solution.py:353
  55.2 1.5 %collective-permute-done.16.refs_4_ = bf16[3,96,128]{2,1,0:T(8,128)(2,1)S(1)} collective-permute-done((bf16[3,96,128]{2,1,0:T(8,128)(2,1)S(1)}, bf16[3,96,128]{2,1,0:T(8,128)(2,1)S(1)}, u32[]{:S(2)}, u32[]{:S(2)}) %collective-permute-start.16) | collective-permute-done | bytes 73760 | tf_op jit(solution)/shard_map/ppermute | solution.py:353
  58.5 2.2 %collective-permute-start.20 = (bf16[3,96,128]{2,1,0:T(8,128)(2,1)S(1)}, bf16[3,96,128]{2,1,0:T(8,128)(2,1)S(1)}, u32[]{:S(2)}, u32[]{:S(2)}) collective-permute-start(bf16[3,96,128]{2,1,0:T(8,128)(2,1)S(1)} %get-tuple-element.77.refs_7_.template_ref), channel_id=1, source_target_pairs={{0,16},{4,20},{8,24},{12,28},{16,0},{20,4},{24,8},{28,12},{1,17},{... | collective-permute-start | bytes 221192 | tf_op jit(solution)/shard_map/ppermute | solution.py:353
  61.8 1.6 %collective-permute-start.24 = (bf16[3,96,128]{2,1,0:T(8,128)(2,1)S(1)}, bf16[3,96,128]{2,1,0:T(8,128)(2,1)S(1)}, u32[]{:S(2)}, u32[]{:S(2)}) collective-permute-start(bf16[3,96,128]{2,1,0:T(8,128)(2,1)S(1)} %get-tuple-element.77.refs_7_.template_ref), channel_id=1, source_target_pairs={{0,4},{4,0},{8,12},{12,8},{16,20},{20,16},{24,28},{28,24},{1,5},{5... | collective-permute-start | bytes 221192 | tf_op jit(solution)/shard_map/ppermute | solution.py:353
  63.9 1.6 %collective-permute-start.21 = (bf16[3,96,128]{2,1,0:T(8,128)(2,1)S(1)}, bf16[3,96,128]{2,1,0:T(8,128)(2,1)S(1)}, u32[]{:S(2)}, u32[]{:S(2)}) collective-permute-start(bf16[3,96,128]{2,1,0:T(8,128)(2,1)S(1)} %collective-permute-done.20.refs_3_), channel_id=1, source_target_pairs={{0,4},{4,0},{8,12},{12,8},{16,20},{20,16},{24,28},{28,24},{1,5},{5... | collective-permute-start | bytes 221192 | tf_op jit(solution)/shard_map/ppermute | solution.py:353
  65.5 1.8 %collective-permute-done.18.refs_1_ = bf16[3,96,128]{2,1,0:T(8,128)(2,1)S(1)} collective-permute-done((bf16[3,96,128]{2,1,0:T(8,128)(2,1)S(1)}, bf16[3,96,128]{2,1,0:T(8,128)(2,1)S(1)}, u32[]{:S(2)}, u32[]{:S(2)}) %collective-permute-start.18) | collective-permute-done | bytes 73760 | tf_op jit(solution)/shard_map/ppermute | solution.py:353
  67.3 1.5 %collective-permute-start.19 = (bf16[3,96,128]{2,1,0:T(8,128)(2,1)S(1)}, bf16[3,96,128]{2,1,0:T(8,128)(2,1)S(1)}, u32[]{:S(2)}, u32[]{:S(2)}) collective-permute-start(bf16[3,96,128]{2,1,0:T(8,128)(2,1)S(1)} %collective-permute-done.18.refs_1_), channel_id=1, source_target_pairs={{0,4},{4,0},{8,12},{12,8},{16,20},{20,16},{24,28},{28,24},{1,5},{5... | collective-permute-start | bytes 221192 | tf_op jit(solution)/shard_map/ppermute | solution.py:353
  69.5 2.2 %collective-permute-done.19.refs_0_ = bf16[3,96,128]{2,1,0:T(8,128)(2,1)S(1)} collective-permute-done((bf16[3,96,128]{2,1,0:T(8,128)(2,1)S(1)}, bf16[3,96,128]{2,1,0:T(8,128)(2,1)S(1)}, u32[]{:S(2)}, u32[]{:S(2)}) %collective-permute-start.19) | collective-permute-done | bytes 73760 | tf_op jit(solution)/shard_map/ppermute | solution.py:353
  71.7 1.7 %shard_map.126 = bf16[18,96,384]{2,1,0:T(8,128)(2,1)} custom-call(s32[54]{0:T(128)S(1)} %get-tuple-element.41.slot_ref, s32[1]{0:T(128)} %bitcast.1.row_ref, f32[9,96,384]{2,1,0:T(8,128)S(1)} %get-tuple-element.63.own_ref, f32[9,96,384]{2,1,0:T(8,128)S(1)} %collective-permute-done.17.other_ref, bf16[3,96,128]{2,1,0:T(8,128)(2,1)S(1)} %collective-permute-done.19.refs_0_, ...), custom_call_target="tpu_custom_call" | custom-call | tf_op jit(solution)/shard_map/pallas_call | solution.py:512
  (59 shorter events, 12.7 us)
Async XLA Ops:
  0.6 5.8 %collective-permute-start = (bf16[18,96,384]{2,1,0:T(8,128)(2,1)}, bf16[18,96,384]{2,1,0:T(8,128)(2,1)S(1)}, u32[]{:S(2)}, u32[]{:S(2)}) collective-permute-start(bf16[18,96,384]{2,1,0:T(8,128)(2,1)} %bitcast.16), channel_id=1, source_target_pairs={{0,1},{1,0},{2,3},{3,2},{4,5},{5,4},{6,7},{7,6},{8,9},{9,8},{10,11... | collective-permute-start | bytes 3981320 | tf_op jit(solution)/shard_map/ppermute | solution.py:353
  1.1 17.2 %collective-permute-start.1 = (bf16[18,96,384]{2,1,0:T(8,128)(2,1)}, bf16[18,96,384]{2,1,0:T(8,128)(2,1)S(1)}, u32[]{:S(2)}, u32[]{:S(2)}) collective-permute-start(bf16[18,96,384]{2,1,0:T(8,128)(2,1)} %bitcast.21), channel_id=1, source_target_pairs={{0,1},{1,0},{2,3},{3,2},{4,5},{5,4},{6,7},{7,6},{8,9},{9,8},{10,11... | collective-permute-start | bytes 3981320 | tf_op jit(solution)/shard_map/ppermute | solution.py:353
  2.3 7.7 %collective-permute-start.5 = (bf16[2,96,384]{2,1,0:T(8,128)(2,1)S(1)}, bf16[2,96,384]{2,1,0:T(8,128)(2,1)S(1)}, u32[]{:S(2)}, u32[]{:S(2)}) collective-permute-start(bf16[2,96,384]{2,1,0:T(8,128)(2,1)S(1)} %get-tuple-element.50), channel_id=1, source_target_pairs={{0,2},{1,3},{2,0},{3,1},{4,6},{5,7},{6,4},{7,5},{8,10},{9,11},{10,... | collective-permute-start | bytes 442376 | tf_op jit(solution)/shard_map/ppermute | solution.py:353
  5.3 12.8 %collective-permute-start.8 = (bf16[2,96,384]{2,1,0:T(8,128)(2,1)S(1)}, bf16[2,96,384]{2,1,0:T(8,128)(2,1)S(1)}, u32[]{:S(2)}, u32[]{:S(2)}) collective-permute-start(bf16[2,96,384]{2,1,0:T(8,128)(2,1)S(1)} %get-tuple-element.53), channel_id=1, source_target_pairs={{0,3},{1,2},{2,1},{3,0},{4,7},{5,6},{6,5},{7,4},{8,11},{9,10},{10,... | collective-permute-start | bytes 442376 | tf_op jit(solution)/shard_map/ppermute | solution.py:353
  7.4 12.6 %collective-permute-start.4 = (bf16[9,16,384]{2,1,0:T(8,128)(2,1)S(1)}, bf16[9,16,384]{2,1,0:T(8,128)(2,1)S(1)}, u32[]{:S(2)}, u32[]{:S(2)}) collective-permute-start(bf16[9,16,384]{2,1,0:T(8,128)(2,1)S(1)} %get-tuple-element.40.refs_4_), channel_id=1, source_target_pairs={{0,2},{1,3},{2,0},{3,1},{4,6},{5,7},{6,4},{7,5},{8,10},{9,11},{10,... | collective-permute-start | bytes 331784 | tf_op jit(solution)/shard_map/ppermute | solution.py:353
  11.1 12.3 %collective-permute-start.6 = (bf16[5,96,384]{2,1,0:T(8,128)(2,1)S(1)}, bf16[5,96,384]{2,1,0:T(8,128)(2,1)S(1)}, u32[]{:S(2)}, u32[]{:S(2)}) collective-permute-start(bf16[5,96,384]{2,1,0:T(8,128)(2,1)S(1)} %get-tuple-element.51), channel_id=1, source_target_pairs={{0,2},{1,3},{2,0},{3,1},{4,6},{5,7},{6,4},{7,5},{8,10},{9,11},{10,... | collective-permute-start | bytes 1105928 | tf_op jit(solution)/shard_map/ppermute | solution.py:353
  13.2 17.6 %collective-permute-start.7 = (bf16[5,96,384]{2,1,0:T(8,128)(2,1)S(1)}, bf16[5,96,384]{2,1,0:T(8,128)(2,1)S(1)}, u32[]{:S(2)}, u32[]{:S(2)}) collective-permute-start(bf16[5,96,384]{2,1,0:T(8,128)(2,1)S(1)} %get-tuple-element.52), channel_id=1, source_target_pairs={{0,3},{1,2},{2,1},{3,0},{4,7},{5,6},{6,5},{7,4},{8,11},{9,10},{10,... | collective-permute-start | bytes 1105928 | tf_op jit(solution)/shard_map/ppermute | solution.py:353
  18.1 18.0 %collective-permute-start.2 = (bf16[2,96,384]{2,1,0:T(8,128)(2,1)S(1)}, bf16[2,96,384]{2,1,0:T(8,128)(2,1)S(1)}, u32[]{:S(2)}, u32[]{:S(2)}) collective-permute-start(bf16[2,96,384]{2,1,0:T(8,128)(2,1)S(1)} %get-tuple-element.48), channel_id=1, source_target_pairs={{0,2},{1,3},{2,0},{3,1},{4,6},{5,7},{6,4},{7,5},{8,10},{9,11},{10,... | collective-permute-start | bytes 442376 | tf_op jit(solution)/shard_map/ppermute | solution.py:353
  18.3 18.2 %collective-permute-start.3 = (bf16[2,96,384]{2,1,0:T(8,128)(2,1)S(1)}, bf16[2,96,384]{2,1,0:T(8,128)(2,1)S(1)}, u32[]{:S(2)}, u32[]{:S(2)}) collective-permute-start(bf16[2,96,384]{2,1,0:T(8,128)(2,1)S(1)} %get-tuple-element.49), channel_id=1, source_target_pairs={{0,3},{1,2},{2,1},{3,0},{4,7},{5,6},{6,5},{7,4},{8,11},{9,10},{10,... | collective-permute-start | bytes 442376 | tf_op jit(solution)/shard_map/ppermute | solution.py:353
  40.8 4.8 %collective-permute-start.11 = (bf16[3,96,128]{2,1,0:T(8,128)(2,1)S(1)}, bf16[3,96,128]{2,1,0:T(8,128)(2,1)S(1)}, u32[]{:S(2)}, u32[]{:S(2)}) collective-permute-start(bf16[3,96,128]{2,1,0:T(8,128)(2,1)S(1)} %get-tuple-element.71), channel_id=1, source_target_pairs={{0,4},{4,0},{8,12},{12,8},{16,20},{20,16},{24,28},{28,24},{1,5},{5... | collective-permute-start | bytes 221192 | tf_op jit(solution)/shard_map/ppermute | solution.py:353
  42.6 5.1 %collective-permute-start.13 = (bf16[3,96,128]{2,1,0:T(8,128)(2,1)S(1)}, bf16[3,96,128]{2,1,0:T(8,128)(2,1)S(1)}, u32[]{:S(2)}, u32[]{:S(2)}) collective-permute-start(bf16[3,96,128]{2,1,0:T(8,128)(2,1)S(1)} %get-tuple-element.73), channel_id=1, source_target_pairs={{0,4},{4,0},{8,12},{12,8},{16,20},{20,16},{24,28},{28,24},{1,5},{5... | collective-permute-start | bytes 221192 | tf_op jit(solution)/shard_map/ppermute | solution.py:353
  42.9 7.5 %collective-permute-start.15 = (bf16[3,96,128]{2,1,0:T(8,128)(2,1)S(1)}, bf16[3,96,128]{2,1,0:T(8,128)(2,1)S(1)}, u32[]{:S(2)}, u32[]{:S(2)}) collective-permute-start(bf16[3,96,128]{2,1,0:T(8,128)(2,1)S(1)} %get-tuple-element.75), channel_id=1, source_target_pairs={{0,4},{4,0},{8,12},{12,8},{16,20},{20,16},{24,28},{28,24},{1,5},{5... | collective-permute-start | bytes 221192 | tf_op jit(solution)/shard_map/ppermute | solution.py:353
  44.6 8.4 %collective-permute-start.10 = (bf16[3,96,128]{2,1,0:T(8,128)(2,1)S(1)}, bf16[3,96,128]{2,1,0:T(8,128)(2,1)S(1)}, u32[]{:S(2)}, u32[]{:S(2)}) collective-permute-start(bf16[3,96,128]{2,1,0:T(8,128)(2,1)S(1)} %get-tuple-element.69), channel_id=1, source_target_pairs={{0,4},{4,0},{8,12},{12,8},{16,20},{20,16},{24,28},{28,24},{1,5},{5... | collective-permute-start | bytes 221192 | tf_op jit(solution)/shard_map/ppermute | solution.py:353
  45.6 7.4 %collective-permute-start.12 = (bf16[3,96,128]{2,1,0:T(8,128)(2,1)S(1)}, bf16[3,96,128]{2,1,0:T(8,128)(2,1)S(1)}, u32[]{:S(2)}, u32[]{:S(2)}) collective-permute-start(bf16[3,96,128]{2,1,0:T(8,128)(2,1)S(1)} %shard_map.122), channel_id=1, source_target_pairs={{0,8},{4,12},{8,0},{12,4},{16,24},{20,28},{24,16},{28,20},{1,9},{5... | collective-permute-start | bytes 221192 | tf_op jit(solution)/shard_map/ppermute | solution.py:353
  47.7 7.5 %collective-permute-start.14 = (bf16[3,96,128]{2,1,0:T(8,128)(2,1)S(1)}, bf16[3,96,128]{2,1,0:T(8,128)(2,1)S(1)}, u32[]{:S(2)}, u32[]{:S(2)}) collective-permute-start(bf16[3,96,128]{2,1,0:T(8,128)(2,1)S(1)} %shard_map.123), channel_id=1, source_target_pairs={{0,16},{4,20},{8,24},{12,28},{16,0},{20,4},{24,8},{28,12},{1,17},{... | collective-permute-start | bytes 221192 | tf_op jit(solution)/shard_map/ppermute | solution.py:353
  50.4 6.3 %collective-permute-start.16 = (bf16[3,96,128]{2,1,0:T(8,128)(2,1)S(1)}, bf16[3,96,128]{2,1,0:T(8,128)(2,1)S(1)}, u32[]{:S(2)}, u32[]{:S(2)}) collective-permute-start(bf16[3,96,128]{2,1,0:T(8,128)(2,1)S(1)} %shard_map.124), channel_id=1, source_target_pairs={{0,24},{4,28},{8,16},{12,20},{16,8},{20,12},{24,0},{28,4},{1,25},{... | collective-permute-start | bytes 221192 | tf_op jit(solution)/shard_map/ppermute | solution.py:353
  57.3 14.4 %collective-permute-start.17 = (f32[9,96,384]{2,1,0:T(8,128)S(1)}, f32[9,96,384]{2,1,0:T(8,128)S(1)}, u32[]{:S(2)}, u32[]{:S(2)}) collective-permute-start(f32[9,96,384]{2,1,0:T(8,128)S(1)} %get-tuple-element.76), channel_id=1, source_target_pairs={{0,1},{1,0},{2,3},{3,2},{4,5},{5,4},{6,7},{7,6},{8,9},{9,8},{10,11... | collective-permute-start | bytes 3981320 | tf_op jit(solution)/shard_map/ppermute | solution.py:353
  57.4 6.1 %collective-permute-start.22 = (bf16[3,96,128]{2,1,0:T(8,128)(2,1)S(1)}, bf16[3,96,128]{2,1,0:T(8,128)(2,1)S(1)}, u32[]{:S(2)}, u32[]{:S(2)}) collective-permute-start(bf16[3,96,128]{2,1,0:T(8,128)(2,1)S(1)} %get-tuple-element.77.refs_7_.template_ref), channel_id=1, source_target_pairs={{0,8},{4,12},{8,0},{12,4},{16,24},{20,28},{24,16},{28,20},{1,9},{5... | collective-permute-start | bytes 221192 | tf_op jit(solution)/shard_map/ppermute | solution.py:353
  58.5 5.4 %collective-permute-start.20 = (bf16[3,96,128]{2,1,0:T(8,128)(2,1)S(1)}, bf16[3,96,128]{2,1,0:T(8,128)(2,1)S(1)}, u32[]{:S(2)}, u32[]{:S(2)}) collective-permute-start(bf16[3,96,128]{2,1,0:T(8,128)(2,1)S(1)} %get-tuple-element.77.refs_7_.template_ref), channel_id=1, source_target_pairs={{0,16},{4,20},{8,24},{12,28},{16,0},{20,4},{24,8},{28,12},{1,17},{... | collective-permute-start | bytes 221192 | tf_op jit(solution)/shard_map/ppermute | solution.py:353
  60.7 6.6 %collective-permute-start.18 = (bf16[3,96,128]{2,1,0:T(8,128)(2,1)S(1)}, bf16[3,96,128]{2,1,0:T(8,128)(2,1)S(1)}, u32[]{:S(2)}, u32[]{:S(2)}) collective-permute-start(bf16[3,96,128]{2,1,0:T(8,128)(2,1)S(1)} %get-tuple-element.77.refs_7_.template_ref), channel_id=1, source_target_pairs={{0,24},{4,28},{8,16},{12,20},{16,8},{20,12},{24,0},{28,4},{1,25},{... | collective-permute-start | bytes 221192 | tf_op jit(solution)/shard_map/ppermute | solution.py:353
  61.8 7.6 %collective-permute-start.24 = (bf16[3,96,128]{2,1,0:T(8,128)(2,1)S(1)}, bf16[3,96,128]{2,1,0:T(8,128)(2,1)S(1)}, u32[]{:S(2)}, u32[]{:S(2)}) collective-permute-start(bf16[3,96,128]{2,1,0:T(8,128)(2,1)S(1)} %get-tuple-element.77.refs_7_.template_ref), channel_id=1, source_target_pairs={{0,4},{4,0},{8,12},{12,8},{16,20},{20,16},{24,28},{28,24},{1,5},{5... | collective-permute-start | bytes 221192 | tf_op jit(solution)/shard_map/ppermute | solution.py:353
  63.5 6.0 %collective-permute-start.23 = (bf16[3,96,128]{2,1,0:T(8,128)(2,1)S(1)}, bf16[3,96,128]{2,1,0:T(8,128)(2,1)S(1)}, u32[]{:S(2)}, u32[]{:S(2)}) collective-permute-start(bf16[3,96,128]{2,1,0:T(8,128)(2,1)S(1)} %collective-permute-done.22.refs_5_), channel_id=1, source_target_pairs={{0,4},{4,0},{8,12},{12,8},{16,20},{20,16},{24,28},{28,24},{1,5},{5... | collective-permute-start | bytes 221192 | tf_op jit(solution)/shard_map/ppermute | solution.py:353
  63.9 5.6 %collective-permute-start.21 = (bf16[3,96,128]{2,1,0:T(8,128)(2,1)S(1)}, bf16[3,96,128]{2,1,0:T(8,128)(2,1)S(1)}, u32[]{:S(2)}, u32[]{:S(2)}) collective-permute-start(bf16[3,96,128]{2,1,0:T(8,128)(2,1)S(1)} %collective-permute-done.20.refs_3_), channel_id=1, source_target_pairs={{0,4},{4,0},{8,12},{12,8},{16,20},{20,16},{24,28},{28,24},{1,5},{5... | collective-permute-start | bytes 221192 | tf_op jit(solution)/shard_map/ppermute | solution.py:353
  67.3 4.4 %collective-permute-start.19 = (bf16[3,96,128]{2,1,0:T(8,128)(2,1)S(1)}, bf16[3,96,128]{2,1,0:T(8,128)(2,1)S(1)}, u32[]{:S(2)}, u32[]{:S(2)}) collective-permute-start(bf16[3,96,128]{2,1,0:T(8,128)(2,1)S(1)} %collective-permute-done.18.refs_1_), channel_id=1, source_target_pairs={{0,4},{4,0},{8,12},{12,8},{16,20},{20,16},{24,28},{28,24},{1,5},{5... | collective-permute-start | bytes 221192 | tf_op jit(solution)/shard_map/ppermute | solution.py:353
  (8 other events, 30.9 us)
